TPU v7x, 32 devices: a whole 2x2x4 slice. The times are simulated.
32 devices in a mesh: group: 2 (over x), expert: 8 (over z, core), tensor: 2 (over y).
Axes of the slice: x: 2, y: 2, z: 4, core: 2. Of those that a mesh axis runs over, the one named last changes fastest.
Arguments:
- heads_out: bfloat16 [1024, 4096], P(('group', 'expert'), 'tensor'), parts along dimension 0, may hold values from -6 to 6
- out_proj: bfloat16 [4096, 2880], P('tensor'), may hold values from -0.09375 to 0.09375
- norm_gain: float32 [2880], replicated, may hold values from 0.25 to 1.75
- gate_up: bfloat16 [8, 2880, 2, 2880], P('expert', None, None, 'tensor'), may hold values from -0.109375 to 0.109375
- down_proj: bfloat16 [8, 2880, 2880], P('expert', 'tensor'), may hold values from -0.109375 to 0.109375
- routes: int32 [1024, 4], P(('group', 'expert', 'tensor')), parts along dimension 0, may hold values from 0 to 7, all different within a row; in each aligned block of 32 rows (0 to 31, 32 to 63, ...) at most 24 rows name the same one
- gate_weights: float32 [1024, 4], P(('group', 'expert', 'tensor')), parts along dimension 0, may hold values from 0.05 to 0.5
Outputs:
- combined: bfloat16 [1024, 2880], P(('group', 'expert', 'tensor')), parts along dimension 0
There are 2 independent parts, one for each index of `group`. A program takes and returns all parts, laid end to end along the dimension named above; an argument that names none is the same for every part. Nothing has to cross between parts.
Inputs may be any that keep to these rules, and one draw needn't show every extreme that they name: `routes`: each row names 4 different experts. Within the rows of one device (aligned blocks of 32 rows) no expert is named by more than 24 rows, and in every draw some expert is named by exactly 24 rows of some block.
All inputs are finite; a program needn't handle non-finite values.
Results may differ from a plain program's by a relative error of at most 0.02.
Values may be sent and summed in bfloat16 or wider, within the bound.
No kernel may reach another device: no remote copies, remote signals or barrier semaphores. Data moves between devices by JAX's collectives and lax.ppermute only.
A program may use at most 128 MiB of HBM per device.

v0:
```python
import math

import jax
import jax.numpy as jnp
from jax import lax
from jax.sharding import PartitionSpec as P

HB = 64


def hadamard(order):
    positions = jnp.arange(order, dtype=jnp.int32)
    common = jnp.bitwise_and(positions[:, None], positions[None, :])
    ones_count = jnp.zeros((order, order), jnp.int32)
    for bit_pos in range(order.bit_length()):
        ones_count = ones_count + jnp.bitwise_and(jnp.right_shift(common, bit_pos), 1)
    parity = 1 - 2 * jnp.bitwise_and(ones_count, 1)
    return parity.astype(jnp.float32) / math.sqrt(order)


def rotate(values, rotation):
    blocks = values.reshape(-1, HB)
    turned = jnp.dot(
        blocks, rotation, precision=lax.Precision.HIGHEST, preferred_element_type=jnp.float32
    )
    return turned.reshape(values.shape)


def slot_places(route_rows, experts, capacity):
    flat_routes = route_rows.reshape(-1)
    onehot = (flat_routes[:, None] == jnp.arange(experts, dtype=jnp.int32)[None, :]).astype(
        jnp.int32
    )
    before = jnp.cumsum(onehot, axis=0) - onehot
    places = flat_routes * capacity + jnp.sum(before * onehot, axis=1)
    return places.reshape(route_rows.shape)


def slot_rows(places, normed, experts, capacity):
    slots = jnp.arange(experts * capacity, dtype=jnp.int32)
    select = jnp.sum((places[None, :, :] == slots[:, None, None]).astype(jnp.float32), axis=2)
    filled = jnp.dot(select.astype(jnp.bfloat16), normed, preferred_element_type=jnp.float32)
    return filled.astype(jnp.bfloat16).reshape(experts, capacity, normed.shape[1])


def expert_hidden(row_block, weights_in):
    both = jnp.einsum("rd,dcf->rcf", row_block, weights_in, preferred_element_type=jnp.float32)
    gate_part = both[:, 0, :]
    up_part = both[:, 1, :]
    return (gate_part * jax.nn.sigmoid(1.702 * gate_part) * (up_part + 1.0)).astype(jnp.bfloat16)


def per_device(heads_out, out_proj, norm_gain, gate_up, down_proj, routes, gate_weights):
    token_count, topk = routes.shape
    width = out_proj.shape[1]
    experts = lax.axis_size("expert")
    capacity = min(token_count, token_count * topk // experts + token_count * topk // (2 * experts))
    rotation = hadamard(HB)
    weights_in = gate_up[0]
    weights_out = down_proj[0]
    row_block = heads_out
    hidden = lax.psum_scatter(
        jnp.dot(row_block, out_proj, preferred_element_type=jnp.float32).astype(jnp.bfloat16),
        "tensor",
        scatter_dimension=0,
        tiled=True,
    ).astype(jnp.float32)
    scale = lax.rsqrt(jnp.mean(hidden * hidden, axis=1, keepdims=True) + 1e-05)
    normed = (hidden * scale * norm_gain).astype(jnp.bfloat16)
    places = slot_places(routes, experts, capacity)
    own_rows = slot_rows(places, normed, experts, capacity)
    arrived = lax.all_to_all(own_rows, "expert", split_axis=0, concat_axis=0, tiled=True)
    activation = expert_hidden(
        lax.all_gather(arrived.reshape(-1, width), "tensor", axis=0, tiled=True), weights_in
    )
    row_block = activation
    expert_out = lax.psum_scatter(
        jnp.dot(row_block, weights_out, preferred_element_type=jnp.float32).astype(jnp.bfloat16),
        "tensor",
        scatter_dimension=0,
        tiled=True,
    ).astype(jnp.float32)
    rotated = rotate(expert_out, rotation).astype(jnp.bfloat16).reshape(experts, capacity, width)
    returned = lax.all_to_all(rotated, "expert", split_axis=0, concat_axis=0, tiled=True)
    slots = jnp.arange(experts * capacity, dtype=jnp.int32)
    weight_map = jnp.sum(
        (places[:, :, None] == slots[None, None, :]).astype(jnp.float32) * gate_weights[:, :, None],
        axis=1,
    )
    mixed = jnp.dot(
        weight_map,
        returned.reshape(-1, width),
        precision=lax.Precision.HIGHEST,
        preferred_element_type=jnp.float32,
    )
    return rotate(mixed, rotation).astype(jnp.bfloat16)


def solution(mesh):
    return jax.shard_map(
        per_device,
        mesh=mesh,
        in_specs=(
            P(("group", "expert"), "tensor"),
            P("tensor", None),
            P(),
            P("expert", None, None, "tensor"),
            P("expert", "tensor", None),
            P(("group", "expert", "tensor"), None),
            P(("group", "expert", "tensor"), None),
        ),
        out_specs=P(("group", "expert", "tensor"), None),
        check_vma=False,
    )
```

profile of v0, /device:TPU:0, one launch (start us, length us, event | category | flops | bytes accessed | tf_op | source)
XLA Modules:
  0.0 210.9 jit_solution(10715439081195108464)
XLA Ops:
  6.5 0.0 copy-start
  6.5 0.0 copy-start.2
  6.5 0.0 copy-start.1
  6.5 0.0 reduce-scatter.3.cloned.1.call-start
  6.5 0.9 copy-done
  7.5 8.7 %convolution_convert_fusion.2 = bf16[64,2880]{1,0:T(8,128)(2,1)} fusion(bf16[64,2048]{1,0:T(8,128)(2,1)S(1)} %copy-done, bf16[2048,2880]{0,1:T(8,128)(2,1)} %param.8), kind=kOutput, calls=%fused_computation.7 | convolution fusion | flops 755159040 | bytes 12427264 | tf_op jit(solution)/shard_map/dot_general | solution.py:63
  16.2 0.0 reduce-scatter.3.cloned.1.call-update
  16.2 0.0 all-gather.2.cloned.1.call-start
  16.3 0.0 copy-done.2
  16.3 0.1 copy.25
  16.4 0.1 eq.20
  16.5 0.1 fusion.19
  16.6 0.2 reduce_window_sum.11
  16.8 0.2 select_reduce_fusion.1
  16.9 0.1 reduce_sum.39
  17.0 0.1 copy.26
  17.1 0.1 convert_reduce_fusion
  17.2 14.8 %reduce-scatter.3.cloned.1.call-done = bf16[32,2880]{1,0:T(8,128)(2,1)} async-done(((bf16[64,2880]{1,0:T(8,128)(2,1)}), bf16[32,2880]{1,0:T(8,128)(2,1)}) %reduce-scatter.3.cloned.1.call-update) | async-done | bytes 184336 | tf_op jit(solution)/shard_map/reduce_scatter | solution.py:62
  32.0 1.1 fusion.13
  33.1 0.0 copy-done.1
  33.1 1.4 convolution_convert_fusion.1
  34.6 32.9 %all_to_all.10 = bf16[8,24,2880]{2,1,0:T(8,128)(2,1)} all-to-all(bf16[8,24,2880]{2,1,0:T(8,128)(2,1)S(1)} %bitcast.26), channel_id=1, replica_groups=mesh['group'=2,'expert'=8,'tensor'=2] {'expert'}, dimensions={0} | all-to-all | bytes 2211840 | tf_op jit(solution)/shard_map/all_to_all | solution.py:72
  67.4 0.0 all-gather.2.cloned.1.call-update
  67.5 0.0 reduce-scatter.5.cloned.1.call-start
  67.5 33.0 %all-gather.2.cloned.1.call-done = bf16[384,2880]{1,0:T(8,128)(2,1)} async-done(((bf16[192,2880]{1,0:T(8,128)(2,1)}), bf16[384,2880]{1,0:T(8,128)(2,1)}) %all-gather.2.cloned.1.call-update) | async-done | bytes 2211856 | tf_op jit(solution)/shard_map/all_gather | solution.py:74
  100.5 12.8 %fusion = f32[384,2,1440]{0,2,1:T(8,128)S(1)} fusion(bf16[1,2880,2,1440]{1,3,2,0:T(8,128)(2,1)} %param.10, bf16[384,2880]{1,0:T(8,128)(2,1)} %all-gather.2.cloned.1.call-done), kind=kOutput, calls=%fused_computation | convolution fusion | flops 6370099200 | bytes 23224320 | tf_op jit(solution)/shard_map/rd,dcf->rcf/dot_general | solution.py:47
  113.3 9.3 %fusion.4 = bf16[384,2880]{1,0:T(8,128)(2,1)} fusion(bf16[1,1440,2880]{2,1,0:T(8,128)(2,1)} %param.11, f32[384,2,1440]{0,2,1:T(8,128)S(1)} %fusion), kind=kOutput, calls=%fused_computation.5 | convolution fusion | flops 3190579200 | bytes 14929920 | tf_op jit(solution)/shard_map/dot_general | solution.py:78
  122.6 0.0 reduce-scatter.5.cloned.1.call-update
  122.7 33.8 %reduce-scatter.5.cloned.1.call-done = bf16[192,2880]{1,0:T(8,128)(2,1)} async-done(((bf16[384,2880]{1,0:T(8,128)(2,1)}), bf16[192,2880]{1,0:T(8,128)(2,1)}) %reduce-scatter.5.cloned.1.call-update) | async-done | bytes 1105936 | tf_op jit(solution)/shard_map/reduce_scatter | solution.py:77
  156.5 3.0 %reshape.48 = bf16[8640,64]{1,0:T(8,128)(2,1)S(1)} reshape(bf16[192,2880]{1,0:T(8,128)(2,1)} %reduce-scatter.5.cloned.1.call-done) | data formatting | bytes 2211840 | tf_op jit(solution)/shard_map/reshape | solution.py:22
  159.5 3.3 %convolution_convert_fusion = bf16[8640,64]{0,1:T(8,128)(2,1)} fusion(bf16[8640,64]{1,0:T(8,128)(2,1)S(1)} %reshape.48), kind=kOutput, calls=%fused_computation.2 | convolution fusion | flops 425332736 | bytes 2211840 | tf_op jit(solution)/shard_map/dot_general | solution.py:23
  162.8 3.2 %copy.27 = bf16[8640,64]{1,0:T(8,128)(2,1)S(1)} copy(bf16[8640,64]{0,1:T(8,128)(2,1)} %convolution_convert_fusion) | data formatting | bytes 2211840 | tf_op jit(solution)/shard_map/convert_element_type | solution.py:83
  166.0 0.0 copy-start.3
  166.0 2.4 %convert_element_type.62 = bf16[8,24,2880]{2,1,0:T(8,128)(2,1)} reshape(bf16[8640,64]{1,0:T(8,128)(2,1)S(1)} %copy.27) | data formatting | bytes 2211840 | tf_op jit(solution)/shard_map/convert_element_type | solution.py:83
  168.4 4.6 %all-to-all-start.1 = ((bf16[8,24,2880]{2,1,0:T(8,128)(2,1)}), bf16[8,24,2880]{2,1,0:T(8,128)(2,1)S(1)}, u32[]{:S(2)}, u32[]{:S(2)}) async-start(bf16[8,24,2880]{2,1,0:T(8,128)(2,1)} %convert_element_type.62), calls=%async_computation.3 | async-start | bytes 2260992 | tf_op jit(solution)/shard_map/all_to_all | solution.py:84
  173.0 0.0 copy-done.3
  173.0 0.1 select_reduce_fusion
  173.1 28.2 %all-to-all-done.1 = bf16[8,24,2880]{2,1,0:T(8,128)(2,1)S(1)} async-done(((bf16[8,24,2880]{2,1,0:T(8,128)(2,1)}), bf16[8,24,2880]{2,1,0:T(8,128)(2,1)S(1)}, u32[]{:S(2)}, u32[]{:S(2)}) %all-to-all-start.1) | async-done | bytes 1105952 | tf_op jit(solution)/shard_map/all_to_all | solution.py:84
  201.3 0.7 fusion.39
  202.0 0.2 reshape.50
  202.2 1.0 convolution_convert_fusion.3
  203.2 0.2 copy.28
  203.4 0.9 convert_element_type.64
  (2 shorter events, 0.0 us)
Async XLA Ops:
  6.5 1.0 copy-start
  6.5 9.7 %copy-start.2 = (s32[32,4]{0,1:T(4,128)S(1)}, s32[32,4]{0,1:T(4,128)}, u32[]{:S(2)}) copy-start(s32[32,4]{0,1:T(4,128)} %param.12) | copy-start | bytes 1540
  6.5 26.6 %copy-start.1 = (f32[2880]{0:T(1024)S(1)}, f32[2880]{0:T(1024)}, u32[]{:S(2)}) copy-start(f32[2880]{0:T(1024)} %param.9) | copy-start | bytes 34564
  6.5 25.5 %reduce-scatter.3.cloned.1.call-start = ((), (), s32[]{:S(2)}) async-start(), calls=%async_computation.4 | async-start | bytes 565248 | tf_op jit(solution)/shard_map/reduce_scatter | solution.py:62
  16.2 84.3 %all-gather.2.cloned.1.call-start = ((), (), s32[]{:S(2)}) async-start(), calls=%async_computation.5 | async-start | bytes 3391488 | tf_op jit(solution)/shard_map/all_gather | solution.py:74
  67.5 89.0 %reduce-scatter.5.cloned.1.call-start = ((), (), s32[]{:S(2)}) async-start(), calls=%async_computation.6 | async-start | bytes 3391488 | tf_op jit(solution)/shard_map/reduce_scatter | solution.py:77
  166.0 7.0 %copy-start.3 = (f32[32,4]{0,1:T(4,128)S(1)}, f32[32,4]{0,1:T(4,128)}, u32[]{:S(2)}) copy-start(f32[32,4]{0,1:T(4,128)} %param.13) | copy-start | bytes 1540
  168.4 32.9 %all-to-all-start.1 = ((bf16[8,24,2880]{2,1,0:T(8,128)(2,1)}), bf16[8,24,2880]{2,1,0:T(8,128)(2,1)S(1)}, u32[]{:S(2)}, u32[]{:S(2)}) async-start(bf16[8,24,2880]{2,1,0:T(8,128)(2,1)} %convert_element_type.62), calls=%async_computation.3 | async-start | bytes 2260992 | tf_op jit(solution)/shard_map/all_to_all | solution.py:84
Sparse Core Ops, SparseCore 0:
  16.4 15.6 reduce-scatter.2
  67.6 32.8 all-gather.1
  122.8 33.6 reduce-scatter.4
where the time goes:
time: 211 us
  waiting for transfers between devices  110 us (52%)
  matrix products  37.2 us (18%)
  blocking collectives  32.9 us (16%)
  between operations  13.2 us (6%)
  local copies, waits for them, and re-layouts  11.3 us (5%)
  starting transfers between devices  4.68 us (2%)
    reduce_scatter x1, waiting for transfers between devices, per_device(): lax.psum_scatter(jnp.dot(row_block, weights_out, preferred_element_type=j...  33.8 us
    all_gather x1, waiting for transfers between devices, per_device(): lax.all_gather(arrived.reshape(-1, width), 'tensor', axis=0, tiled=True)  33 us
    all_to_all x1, blocking collectives, per_device(): lax.all_to_all(own_rows, 'expert', split_axis=0, concat_axis=0, tiled=True)  32.9 us
    all_to_all x1, waiting for transfers between devices, per_device(): lax.all_to_all(rotated, 'expert', split_axis=0, concat_axis=0, tiled=True)  28.2 us
    reduce_scatter x1, waiting for transfers between devices, per_device(): lax.psum_scatter(jnp.dot(row_block, out_proj, preferred_element_type=jnp....  14.8 us
    dot_general x1, matrix products, expert_hidden(): jnp.einsum('rd,dcf->rcf', row_block, weights_in, preferred_element_type=j...  12.8 us
    dot_general x1, matrix products, per_device(): jnp.dot(row_block, weights_out, preferred_element_type=jnp.float32)  9.3 us
    dot_general x1, matrix products, per_device(): jnp.dot(row_block, out_proj, preferred_element_type=jnp.float32)  8.72 us
  transfers between devices with their start and end apart: 4, of which 4 were waited for; matrix products, arithmetic and copies ran while one was open for 0% of the time, Pallas kernels for 0%

commit v1 on v0

v1 whole, which is shorter than its diff:
```python
import functools

import jax
import jax.numpy as jnp
from jax import lax
from jax.experimental import pallas as pl
from jax.experimental.pallas import tpu as pltpu
from jax.sharding import PartitionSpec as P

F32 = jnp.float32
BF16 = jnp.bfloat16
NT = (((1,), (1,)), ((), ()))


def out_proj_kernel(heads_ref, w_ref, out_ref):
    out_ref[...] = lax.dot_general(
        heads_ref[...], w_ref[...], NT, preferred_element_type=F32
    ).astype(BF16)


def project(heads_out, out_proj_t):
    rows, depth = heads_out.shape
    width = out_proj_t.shape[0]
    return pl.pallas_call(
        out_proj_kernel,
        grid=(pl.cdiv(width, 384),),
        in_specs=[
            pl.BlockSpec((rows, depth), lambda i: (0, 0)),
            pl.BlockSpec((384, depth), lambda i: (i, 0)),
        ],
        out_specs=pl.BlockSpec((rows, 384), lambda i: (0, i)),
        out_shape=jax.ShapeDtypeStruct((rows, width), BF16),
        compiler_params=pltpu.CompilerParams(vmem_limit_bytes=10 * 2**20),
        name="project",
    )(heads_out, out_proj_t)


def norm_kernel(experts, *refs):
    *parts, gain_ref, routes_ref, weights_ref, out_ref = refs
    hidden = parts[0][...].astype(F32)
    for part in parts[1:]:
        hidden = hidden + part[...].astype(F32)
    rows, width = hidden.shape
    scale = lax.rsqrt(jnp.mean(hidden * hidden, axis=1, keepdims=True) + 1e-05)
    out_ref[:, :width] = (hidden * scale * gain_ref[...]).astype(BF16)
    extra = out_ref.shape[1] - width
    column = lax.broadcasted_iota(jnp.int32, (rows, extra), 1)
    expert, term = lax.rem(column, experts), lax.div(column, experts)
    weight = jnp.zeros((rows, extra), F32)
    for k in range(routes_ref.shape[1]):
        weight = weight + jnp.where(routes_ref[:, k : k + 1] == expert, weights_ref[:, k : k + 1], 0.0)
    high = weight.astype(BF16).astype(F32)
    middle = (weight - high).astype(BF16).astype(F32)
    low = weight - high - middle
    out_ref[:, width:] = jnp.where(
        term == 0, high, jnp.where(term == 1, middle, jnp.where(term == 2, low, 0.0))
    ).astype(BF16)


def expert_kernel(experts, pieces, expert_ref, *refs):
    tokens, (w_in_ref, w_out_ref, near_ref, far_ref, act_ref) = refs[:pieces], refs[pieces:]
    hidden, width = w_out_ref.shape
    block = jnp.concatenate([piece[...] for piece in tokens], axis=0)
    x, extra = block[:, :width], block[:, width:].astype(F32)
    column = lax.broadcasted_iota(jnp.int32, extra.shape, 1)
    mine = (lax.rem(column, experts) == expert_ref[0]) & (column < 3 * experts)
    weight = jnp.sum(jnp.where(mine, extra, 0.0), axis=1, keepdims=True)
    step = 480 if hidden % 480 == 0 else hidden
    for start in range(0, hidden, step):
        gate = lax.dot_general(x, w_in_ref[0, start : start + step], NT, preferred_element_type=F32)
        up = lax.dot_general(x, w_in_ref[1, start : start + step], NT, preferred_element_type=F32)
        act = gate * jax.nn.sigmoid(1.702 * gate) * (up + 1.0)
        act_ref[:, start : start + step] = act.astype(BF16)
    out = jnp.dot(act_ref[...], w_out_ref[...], preferred_element_type=F32) * weight
    half = out.shape[0] // 2
    near_ref[...] = out[:half].astype(BF16)
    far_ref[...] = out[half:].astype(BF16)


def expert_chunk(expert, tokens, w_in, w_out, experts):
    rows = sum(piece.shape[0] for piece in tokens)
    hidden, width = w_out.shape
    vmem = pl.BlockSpec(memory_space=pltpu.VMEM)
    half = jax.ShapeDtypeStruct((rows // 2, width), BF16)
    return pl.pallas_call(
        functools.partial(expert_kernel, experts, len(tokens)),
        in_specs=[pl.BlockSpec(memory_space=pltpu.SMEM)] + [vmem] * (len(tokens) + 2),
        out_specs=[vmem, vmem],
        out_shape=[half, half],
        scratch_shapes=[pltpu.VMEM((rows, hidden), BF16)],
        compiler_params=pltpu.CompilerParams(vmem_limit_bytes=24 * 2**20),
        cost_estimate=pl.CostEstimate(
            flops=6 * rows * hidden * width, bytes_accessed=6 * hidden * width, transcendentals=rows * hidden
        ),
        name="expert",
    )(expert, *tokens, w_in, w_out)


def per_device(sizes, heads_out, out_proj, norm_gain, gate_up, down_proj, routes, gate_weights):
    experts, tensors = sizes
    tokens = routes.shape[0]
    width = out_proj.shape[1]
    padded = -(-(width + 3 * experts) // 128) * 128
    expert = lax.axis_index("expert")
    tensor = lax.axis_index("tensor")

    def swap(values, axis, distance):
        pairs = [(i, i ^ distance) for i in range(lax.axis_size(axis))]
        return lax.ppermute(values, axis, pairs)

    partial = project(heads_out, out_proj.T)

    def rows_of(owner):
        return lax.dynamic_slice_in_dim(partial, owner * tokens, tokens, 0)

    parts = [rows_of(tensor)]
    parts += [swap(rows_of(tensor ^ j), "tensor", j) for j in range(1, tensors)]
    own = pl.pallas_call(
        functools.partial(norm_kernel, experts),
        out_shape=jax.ShapeDtypeStruct((tokens, padded), BF16),
        compiler_params=pltpu.CompilerParams(vmem_limit_bytes=8 * 2**20),
        name="norm",
    )(*parts, norm_gain.reshape(1, width), routes, gate_weights)

    w_in = gate_up[0].transpose(1, 2, 0)
    w_out = down_proj[0]
    me = expert.reshape(1)
    arrived = [own] + [swap(own, "expert", 2 * k) for k in range(1, experts // 2)]
    results = []
    for k, block in enumerate(arrived):
        here = [block] + [swap(block, "tensor", j) for j in range(1, tensors)]
        there = [swap(piece, "expert", 1) for piece in here]
        near, far = expert_chunk(me, here + there, w_in, w_out, experts)
        total = near.astype(F32) + swap(far, "expert", 1).astype(F32)
        mine = total[:tokens]
        for j in range(1, tensors):
            mine = mine + swap(
                total[j * tokens : (j + 1) * tokens].astype(BF16), "tensor", j
            ).astype(F32)
        results.append(mine if k == 0 else swap(mine.astype(BF16), "expert", 2 * k).astype(F32))
    return sum(results[1:], results[0]).astype(BF16)


def solution(mesh):
    return jax.shard_map(
        functools.partial(per_device, (mesh.shape["expert"], mesh.shape["tensor"])),
        mesh=mesh,
        in_specs=(
            P(("group", "expert"), "tensor"),
            P("tensor", None),
            P(),
            P("expert", None, None, "tensor"),
            P("expert", "tensor", None),
            P(("group", "expert", "tensor"), None),
            P(("group", "expert", "tensor"), None),
        ),
        out_specs=P(("group", "expert", "tensor"), None),
        check_vma=False,
    )
```

time: 211 us -> 117 us (0.55)
  waiting for transfers between devices: 110 us -> 34.4 us
  matrix products: 37.2 us -> 0 us
  blocking collectives: 32.9 us -> 0 us
  Pallas kernels: 0 us -> 31.2 us
  starting transfers between devices: 4.68 us -> 29.2 us
  between operations: 13.2 us -> 0.17 us
  local copies, waits for them, and re-layouts: 11.3 us -> 20.7 us
    reduce_scatter x2 -> x0, waiting for transfers between devices: 48.6 us -> none  [the longest x1 33.8 us: per_device(): lax.psum_scatter(jnp.dot(row_block, weights_out, preferred_element_type=j...]
    dot_general x7 -> x0, matrix products: 37.2 us -> none  [the longest x1 12.8 us: expert_hidden(): jnp.einsum('rd,dcf->rcf', row_block, weights_in, preferred_element_type=j...]
    ppermute x0 -> x27, waiting for transfers between devices: none -> 34.4 us  [swap(): return lax.ppermute(values, axis, pairs)]
    all_gather x1 -> x0, waiting for transfers between devices: 33 us -> none  [per_device(): lax.all_gather(arrived.reshape(-1, width), 'tensor', axis=0, tiled=True)]
    all_to_all x1 -> x0, blocking collectives: 32.9 us -> none  [per_device(): lax.all_to_all(own_rows, 'expert', split_axis=0, concat_axis=0, tiled=True)]
    pallas_call x0 -> x6, Pallas kernels: none -> 31.2 us  [the longest x4 25.8 us: expert_chunk(): pl.pallas_call(functools.partial(expert_kernel, experts, len(tokens)), in...]
    ppermute x0 -> x27, starting transfers between devices: none -> 29.2 us  [swap(): return lax.ppermute(values, axis, pairs)]
    all_to_all x1 -> x0, waiting for transfers between devices: 28.2 us -> none  [per_device(): lax.all_to_all(rotated, 'expert', split_axis=0, concat_axis=0, tiled=True)]
  transfers between devices with their start and end apart: 4 -> 27, of which waited for: 4 -> 6; matrix products, arithmetic and copies ran while one was open for 0% -> 1% of each run, Pallas kernels for 0% -> 22%
where the time goes in v1:
time: 117 us
  waiting for transfers between devices  34.4 us (29%)
  Pallas kernels  31.2 us (27%)
  starting transfers between devices  29.2 us (25%)
  local copies, waits for them, and re-layouts  20.7 us (18%)
  other arithmetic  1.21 us (1%)
    ppermute x27, waiting for transfers between devices, swap(): return lax.ppermute(values, axis, pairs)  34.4 us
    ppermute x27, starting transfers between devices, swap(): return lax.ppermute(values, axis, pairs)  29.2 us
    pallas_call x4, Pallas kernels, expert_chunk(): pl.pallas_call(functools.partial(expert_kernel, experts, len(tokens)), in...  25.8 us
    unnamed x24, local copies, waits for them, and re-layouts  20.6 us
    pallas_call x1, Pallas kernels, project(): pl.pallas_call(out_proj_kernel, grid=(pl.cdiv(width, 384),), in_specs=[pl...  5.11 us
  transfers between devices with their start and end apart: 27, of which 6 were waited for; matrix products, arithmetic and copies ran while one was open for 1% of the time, Pallas kernels for 22%

profile of v1, /device:TPU:0, one launch (start us, length us, event | category | flops | bytes accessed | tf_op | source)
XLA Modules:
  0.0 116.8 jit_solution(8893077685363233366)
XLA Ops:
  0.0 4.4 %copy-done.3 = bf16[2048,2880]{0,1:T(8,128)(2,1)S(1)} copy-done((bf16[2048,2880]{0,1:T(8,128)(2,1)S(1)}, bf16[2048,2880]{0,1:T(8,128)(2,1)}, u32[]{:S(2)}) %copy-start.3) | copy-done | bytes 11796504
  4.4 0.9 copy-done.4
  5.3 5.1 %project.1 = bf16[64,2880]{1,0:T(8,128)(2,1)S(1)} custom-call(bf16[64,2048]{1,0:T(8,128)(2,1)S(1)} %copy-done.4, bf16[2880,2048]{1,0:T(8,128)(2,1)S(1)} %bitcast.16), custom_call_target="tpu_custom_call" | custom-call | tf_op jit(solution)/shard_map/project/pallas_call | solution.py:24
  10.5 3.0 %collective-permute-start = (bf16[32,2880]{1,0:T(8,128)(2,1)S(1)}, bf16[32,2880]{1,0:T(8,128)(2,1)S(1)}, u32[]{:S(2)}, u32[]{:S(2)}) collective-permute-start(bf16[32,2880]{1,0:T(8,128)(2,1)S(1)} %get-tuple-element.21), channel_id=1, source_target_pairs={{0,1},{1,0},{2,3},{3,2},{4,5},{5,4},{6,7},{7,6},{8,9},{9,8},{10,11... | collective-permute-start | bytes 552968 | tf_op jit(solution)/shard_map/ppermute | solution.py:109
  13.5 0.1 copy.8.refs_3_
  13.6 0.1 copy.9.refs_4_
  13.7 4.5 %collective-permute-done.refs_1_ = bf16[32,2880]{1,0:T(8,128)(2,1)S(1)} collective-permute-done((bf16[32,2880]{1,0:T(8,128)(2,1)S(1)}, bf16[32,2880]{1,0:T(8,128)(2,1)S(1)}, u32[]{:S(2)}, u32[]{:S(2)}) %collective-permute-start) | collective-permute-done | bytes 184352 | tf_op jit(solution)/shard_map/ppermute | solution.py:109
  18.3 0.3 norm.1.refs_0_
  18.5 1.8 %collective-permute-start.6 = (bf16[32,2944]{1,0:T(8,128)(2,1)S(1)}, bf16[32,2944]{1,0:T(8,128)(2,1)S(1)}, u32[]{:S(2)}, u32[]{:S(2)}) collective-permute-start(bf16[32,2944]{1,0:T(8,128)(2,1)S(1)} %norm.1.refs_0_), channel_id=1, source_target_pairs={{0,4},{2,6},{4,0},{6,2},{8,12},{10,14},{12,8},{14,10},{1,5},{3,7},... | collective-permute-start | bytes 565256 | tf_op jit(solution)/shard_map/ppermute | solution.py:109
  20.3 1.5 %collective-permute-start.1 = (bf16[32,2944]{1,0:T(8,128)(2,1)S(1)}, bf16[32,2944]{1,0:T(8,128)(2,1)S(1)}, u32[]{:S(2)}, u32[]{:S(2)}) collective-permute-start(bf16[32,2944]{1,0:T(8,128)(2,1)S(1)} %norm.1.refs_0_), channel_id=1, source_target_pairs={{0,1},{1,0},{2,3},{3,2},{4,5},{5,4},{6,7},{7,6},{8,9},{9,8},{10,11... | collective-permute-start | bytes 565256 | tf_op jit(solution)/shard_map/ppermute | solution.py:109
  21.9 2.6 %collective-permute-start.13 = (bf16[32,2944]{1,0:T(8,128)(2,1)S(1)}, bf16[32,2944]{1,0:T(8,128)(2,1)S(1)}, u32[]{:S(2)}, u32[]{:S(2)}) collective-permute-start(bf16[32,2944]{1,0:T(8,128)(2,1)S(1)} %norm.1.refs_0_), channel_id=1, source_target_pairs={{0,8},{2,10},{4,12},{6,14},{8,0},{10,2},{12,4},{14,6},{1,9},{3,11}... | collective-permute-start | bytes 565256 | tf_op jit(solution)/shard_map/ppermute | solution.py:109
  24.4 0.2 collective-permute-start.20
  24.7 1.0 collective-permute-done.6.refs_0_
  25.7 2.6 %collective-permute-start.7 = (bf16[32,2944]{1,0:T(8,128)(2,1)S(1)}, bf16[32,2944]{1,0:T(8,128)(2,1)S(1)}, u32[]{:S(2)}, u32[]{:S(2)}) collective-permute-start(bf16[32,2944]{1,0:T(8,128)(2,1)S(1)} %collective-permute-done.6.refs_0_), channel_id=1, source_target_pairs={{0,1},{1,0},{2,3},{3,2},{4,5},{5,4},{6,7},{7,6},{8,9},{9,8},{10,11... | collective-permute-start | bytes 565256 | tf_op jit(solution)/shard_map/ppermute | solution.py:109
  28.2 9.3 %collective-permute-done.13.refs_0_ = bf16[32,2944]{1,0:T(8,128)(2,1)S(1)} collective-permute-done((bf16[32,2944]{1,0:T(8,128)(2,1)S(1)}, bf16[32,2944]{1,0:T(8,128)(2,1)S(1)}, u32[]{:S(2)}, u32[]{:S(2)}) %collective-permute-start.13) | collective-permute-done | bytes 188448 | tf_op jit(solution)/shard_map/ppermute | solution.py:109
  37.5 0.9 collective-permute-start.14
  38.4 0.2 collective-permute-start.15
  38.7 1.1 collective-permute-start.21
  39.8 0.0 collective-permute-start.9
  39.8 5.8 %copy-done = bf16[1,2880,2,1440]{1,3,2,0:T(8,128)(2,1)S(1)} copy-done((bf16[1,2880,2,1440]{1,3,2,0:T(8,128)(2,1)S(1)}, bf16[1,2880,2,1440]{1,3,2,0:T(8,128)(2,1)}, u32[]{:S(2)}) %copy-start) | copy-done | bytes 16588824
  45.6 3.4 %copy-done.2 = bf16[1,1440,2880]{2,1,0:T(8,128)(2,1)S(1)} copy-done((bf16[1,1440,2880]{2,1,0:T(8,128)(2,1)S(1)}, bf16[1,1440,2880]{2,1,0:T(8,128)(2,1)}, u32[]{:S(2)}) %copy-start.2) | copy-done | bytes 8294424
  49.0 6.4 %expert.4 = (bf16[64,2880]{1,0:T(8,128)(2,1)S(1)}, bf16[64,2880]{1,0:T(8,128)(2,1)S(1)}) custom-call(s32[1]{0:T(128)} %bitcast.expert_ref, bf16[32,2944]{1,0:T(8,128)(2,1)S(1)} %norm.1.refs_0_, bf16[32,2944]{1,0:T(8,128)(2,1)S(1)} %collective-permute-done.1.refs_1_, bf16[32,2944]{1,0:T(8,128)(2,1)S(1)} %collective-permute-done.2.refs_2_, ...), custom_call_target="tpu_custom_call" | custom-call | flops 3185049600 | bytes 24883200 | tf_op jit(solution)/shard_map/expert/pallas_call | solution.py:85
  55.5 0.6 collective-permute-start.22
  56.0 0.1 collective-permute-start.4
  56.1 0.4 collective-permute-start.16
  56.6 0.1 collective-permute-start.23
  56.7 5.8 %copy-done.1 = bf16[1,2880,2,1440]{1,3,2,0:T(8,128)(2,1)S(1)} copy-done((bf16[1,2880,2,1440]{1,3,2,0:T(8,128)(2,1)S(1)}, bf16[1,2880,2,1440]{1,3,2,0:T(8,128)(2,1)}, u32[]{:S(2)}) %copy-start.1) | copy-done | bytes 16588824
  62.5 6.4 %expert.5 = (bf16[64,2880]{1,0:T(8,128)(2,1)S(1)}, bf16[64,2880]{1,0:T(8,128)(2,1)S(1)}) custom-call(s32[1]{0:T(128)} %bitcast.expert_ref, bf16[32,2944]{1,0:T(8,128)(2,1)S(1)} %collective-permute-done.6.refs_0_, bf16[32,2944]{1,0:T(8,128)(2,1)S(1)} %collective-permute-done.7.refs_1_, bf16[32,2944]{1,0:T(8,128)(2,1)S(1)} %collective-permute-done.8.refs_2_, ...), custom_call_target="tpu_custom_call" | custom-call | flops 3185049600 | bytes 24883200 | tf_op jit(solution)/shard_map/expert/pallas_call | solution.py:85
  68.9 0.5 collective-permute-start.10
  69.4 6.6 %expert.6 = (bf16[64,2880]{1,0:T(8,128)(2,1)S(1)}, bf16[64,2880]{1,0:T(8,128)(2,1)S(1)}) custom-call(s32[1]{0:T(128)} %bitcast.expert_ref, bf16[32,2944]{1,0:T(8,128)(2,1)S(1)} %collective-permute-done.13.refs_0_, bf16[32,2944]{1,0:T(8,128)(2,1)S(1)} %collective-permute-done.14.refs_1_, bf16[32,2944]{1,0:T(8,128)(2,1)S(1)} %collective-permute-done.15.refs_2_, ...), custom_call_target="tpu_custom_call" | custom-call | flops 3185049600 | bytes 24883200 | tf_op jit(solution)/shard_map/expert/pallas_call | solution.py:85
  76.0 0.2 collective-permute-start.17
  76.1 6.4 %expert.7 = (bf16[64,2880]{1,0:T(8,128)(2,1)S(1)}, bf16[64,2880]{1,0:T(8,128)(2,1)S(1)}) custom-call(s32[1]{0:T(128)} %bitcast.expert_ref, bf16[32,2944]{1,0:T(8,128)(2,1)S(1)} %collective-permute-done.20.refs_0_, bf16[32,2944]{1,0:T(8,128)(2,1)S(1)} %collective-permute-done.21.refs_1_, bf16[32,2944]{1,0:T(8,128)(2,1)S(1)} %collective-permute-done.22.refs_2_, ...), custom_call_target="tpu_custom_call" | custom-call | flops 3185049600 | bytes 24883200 | tf_op jit(solution)/shard_map/expert/pallas_call | solution.py:85
  82.5 0.5 collective-permute-start.24
  83.0 0.1 convert_add_fusion.3
  83.1 1.0 collective-permute-start.5
  84.1 0.1 convert_add_fusion.2
  84.2 1.2 collective-permute-start.11
  85.4 0.1 convert_add_fusion.1
  85.5 1.0 collective-permute-start.18
  86.5 0.1 convert_add_fusion
  86.6 1.2 %collective-permute-start.25 = (bf16[32,2880]{1,0:T(8,128)(2,1)S(1)}, bf16[32,2880]{1,0:T(8,128)(2,1)S(1)}, u32[]{:S(2)}, u32[]{:S(2)}) collective-permute-start(bf16[32,2880]{1,0:T(8,128)(2,1)S(1)} %slice.66), channel_id=1, source_target_pairs={{0,1},{1,0},{2,3},{3,2},{4,5},{5,4},{6,7},{7,6},{8,9},{9,8},{10,11... | collective-permute-start | bytes 552968 | tf_op jit(solution)/shard_map/ppermute | solution.py:109
  87.8 7.0 %collective-permute-done.11 = bf16[32,2880]{1,0:T(8,128)(2,1)S(1)} collective-permute-done((bf16[32,2880]{1,0:T(8,128)(2,1)S(1)}, bf16[32,2880]{1,0:T(8,128)(2,1)S(1)}, u32[]{:S(2)}, u32[]{:S(2)}) %collective-permute-start.11) | collective-permute-done | bytes 184352 | tf_op jit(solution)/shard_map/ppermute | solution.py:109
  94.8 2.9 %collective-permute-start.12 = (bf16[32,2880]{1,0:T(8,128)(2,1)S(1)}, bf16[32,2880]{1,0:T(8,128)(2,1)S(1)}, u32[]{:S(2)}, u32[]{:S(2)}) collective-permute-start(bf16[32,2880]{1,0:T(8,128)(2,1)S(1)} %fusion.2), channel_id=1, source_target_pairs={{0,4},{2,6},{4,0},{6,2},{8,12},{10,14},{12,8},{14,10},{1,5},{3,7},... | collective-permute-start | bytes 552968 | tf_op jit(solution)/shard_map/ppermute | solution.py:109
  97.7 1.1 collective-permute-done.18
  98.9 3.9 %collective-permute-start.19 = (bf16[32,2880]{1,0:T(8,128)(2,1)S(1)}, bf16[32,2880]{1,0:T(8,128)(2,1)S(1)}, u32[]{:S(2)}, u32[]{:S(2)}) collective-permute-start(bf16[32,2880]{1,0:T(8,128)(2,1)S(1)} %fusion.1), channel_id=1, source_target_pairs={{0,8},{2,10},{4,12},{6,14},{8,0},{10,2},{12,4},{14,6},{1,9},{3,11}... | collective-permute-start | bytes 552968 | tf_op jit(solution)/shard_map/ppermute | solution.py:109
  102.8 1.8 %collective-permute-start.26 = (bf16[32,2880]{1,0:T(8,128)(2,1)S(1)}, bf16[32,2880]{1,0:T(8,128)(2,1)S(1)}, u32[]{:S(2)}, u32[]{:S(2)}) collective-permute-start(bf16[32,2880]{1,0:T(8,128)(2,1)S(1)} %fusion), channel_id=1, source_target_pairs={{0,12},{2,14},{4,8},{6,10},{8,4},{10,6},{12,0},{14,2},{1,13},{3,15... | collective-permute-start | bytes 552968 | tf_op jit(solution)/shard_map/ppermute | solution.py:109
  104.7 11.4 %collective-permute-done.19 = bf16[32,2880]{1,0:T(8,128)(2,1)S(1)} collective-permute-done((bf16[32,2880]{1,0:T(8,128)(2,1)S(1)}, bf16[32,2880]{1,0:T(8,128)(2,1)S(1)}, u32[]{:S(2)}, u32[]{:S(2)}) %collective-permute-start.19) | collective-permute-done | bytes 184352 | tf_op jit(solution)/shard_map/ppermute | solution.py:109
  116.1 0.8 fusion.6
  (51 shorter events, 0.3 us)
Async XLA Ops:
  0.0 13.5 %copy-start.6 = (s32[32,4]{0,1:T(4,128)S(1)}, s32[32,4]{0,1:T(4,128)}, u32[]{:S(2)}) copy-start(s32[32,4]{0,1:T(4,128)} %param.12) | copy-start | bytes 1540
  0.0 13.6 %copy-start.7 = (f32[32,4]{0,1:T(4,128)S(1)}, f32[32,4]{0,1:T(4,128)}, u32[]{:S(2)}) copy-start(f32[32,4]{0,1:T(4,128)} %param.13) | copy-start | bytes 1540
  0.0 13.7 %copy-start.5 = (f32[2880]{0:T(1024)S(1)}, f32[2880]{0:T(1024)}, u32[]{:S(2)}) copy-start(f32[2880]{0:T(1024)} %param.9) | copy-start | bytes 34564
  0.0 4.4 %copy-start.3 = (bf16[2048,2880]{0,1:T(8,128)(2,1)S(1)}, bf16[2048,2880]{0,1:T(8,128)(2,1)}, u32[]{:S(2)}) copy-start(bf16[2048,2880]{0,1:T(8,128)(2,1)} %param.8) | copy-start | bytes 35389444
  4.4 0.9 copy-start.4
  10.5 7.8 %collective-permute-start = (bf16[32,2880]{1,0:T(8,128)(2,1)S(1)}, bf16[32,2880]{1,0:T(8,128)(2,1)S(1)}, u32[]{:S(2)}, u32[]{:S(2)}) collective-permute-start(bf16[32,2880]{1,0:T(8,128)(2,1)S(1)} %get-tuple-element.21), channel_id=1, source_target_pairs={{0,1},{1,0},{2,3},{3,2},{4,5},{5,4},{6,7},{7,6},{8,9},{9,8},{10,11... | collective-permute-start | bytes 552968 | tf_op jit(solution)/shard_map/ppermute | solution.py:109
  18.3 38.4 %slice-start = ((s8[8478720]{0:T(1024)(128)(4,1)}), s8[90112]{0:T(1024)(128)(4,1)S(1)}, s32[]{:S(2)}) async-start(s8[8478720]{0:T(1024)(128)(4,1)} %bitcast.11), calls=%async_computation | async-start | bytes 180224
  18.5 7.1 %collective-permute-start.6 = (bf16[32,2944]{1,0:T(8,128)(2,1)S(1)}, bf16[32,2944]{1,0:T(8,128)(2,1)S(1)}, u32[]{:S(2)}, u32[]{:S(2)}) collective-permute-start(bf16[32,2944]{1,0:T(8,128)(2,1)S(1)} %norm.1.refs_0_), channel_id=1, source_target_pairs={{0,4},{2,6},{4,0},{6,2},{8,12},{10,14},{12,8},{14,10},{1,5},{3,7},... | collective-permute-start | bytes 565256 | tf_op jit(solution)/shard_map/ppermute | solution.py:109
  20.3 7.9 %collective-permute-start.1 = (bf16[32,2944]{1,0:T(8,128)(2,1)S(1)}, bf16[32,2944]{1,0:T(8,128)(2,1)S(1)}, u32[]{:S(2)}, u32[]{:S(2)}) collective-permute-start(bf16[32,2944]{1,0:T(8,128)(2,1)S(1)} %norm.1.refs_0_), channel_id=1, source_target_pairs={{0,1},{1,0},{2,3},{3,2},{4,5},{5,4},{6,7},{7,6},{8,9},{9,8},{10,11... | collective-permute-start | bytes 565256 | tf_op jit(solution)/shard_map/ppermute | solution.py:109
  21.9 15.6 %collective-permute-start.13 = (bf16[32,2944]{1,0:T(8,128)(2,1)S(1)}, bf16[32,2944]{1,0:T(8,128)(2,1)S(1)}, u32[]{:S(2)}, u32[]{:S(2)}) collective-permute-start(bf16[32,2944]{1,0:T(8,128)(2,1)S(1)} %norm.1.refs_0_), channel_id=1, source_target_pairs={{0,8},{2,10},{4,12},{6,14},{8,0},{10,2},{12,4},{14,6},{1,9},{3,11}... | collective-permute-start | bytes 565256 | tf_op jit(solution)/shard_map/ppermute | solution.py:109
  24.4 13.1 %collective-permute-start.20 = (bf16[32,2944]{1,0:T(8,128)(2,1)S(1)}, bf16[32,2944]{1,0:T(8,128)(2,1)S(1)}, u32[]{:S(2)}, u32[]{:S(2)}) collective-permute-start(bf16[32,2944]{1,0:T(8,128)(2,1)S(1)} %norm.1.refs_0_), channel_id=1, source_target_pairs={{0,12},{2,14},{4,8},{6,10},{8,4},{10,6},{12,0},{14,2},{1,13},{3,15... | collective-permute-start | bytes 565256 | tf_op jit(solution)/shard_map/ppermute | solution.py:109
  24.7 13.8 %collective-permute-start.2 = (bf16[32,2944]{1,0:T(8,128)(2,1)S(1)}, bf16[32,2944]{1,0:T(8,128)(2,1)S(1)}, u32[]{:S(2)}, u32[]{:S(2)}) collective-permute-start(bf16[32,2944]{1,0:T(8,128)(2,1)S(1)} %norm.1.refs_0_), channel_id=1, source_target_pairs={{0,2},{2,0},{4,6},{6,4},{8,10},{10,8},{12,14},{14,12},{1,3},{3,1},... | collective-permute-start | bytes 565256 | tf_op jit(solution)/shard_map/ppermute | solution.py:109
  25.7 13.0 %collective-permute-start.7 = (bf16[32,2944]{1,0:T(8,128)(2,1)S(1)}, bf16[32,2944]{1,0:T(8,128)(2,1)S(1)}, u32[]{:S(2)}, u32[]{:S(2)}) collective-permute-start(bf16[32,2944]{1,0:T(8,128)(2,1)S(1)} %collective-permute-done.6.refs_0_), channel_id=1, source_target_pairs={{0,1},{1,0},{2,3},{3,2},{4,5},{5,4},{6,7},{7,6},{8,9},{9,8},{10,11... | collective-permute-start | bytes 565256 | tf_op jit(solution)/shard_map/ppermute | solution.py:109
  28.2 11.6 %collective-permute-start.3 = (bf16[32,2944]{1,0:T(8,128)(2,1)S(1)}, bf16[32,2944]{1,0:T(8,128)(2,1)S(1)}, u32[]{:S(2)}, u32[]{:S(2)}) collective-permute-start(bf16[32,2944]{1,0:T(8,128)(2,1)S(1)} %collective-permute-done.1.refs_1_), channel_id=1, source_target_pairs={{0,2},{2,0},{4,6},{6,4},{8,10},{10,8},{12,14},{14,12},{1,3},{3,1},... | collective-permute-start | bytes 565256 | tf_op jit(solution)/shard_map/ppermute | solution.py:109
  37.5 18.0 %collective-permute-start.8 = (bf16[32,2944]{1,0:T(8,128)(2,1)S(1)}, bf16[32,2944]{1,0:T(8,128)(2,1)S(1)}, u32[]{:S(2)}, u32[]{:S(2)}) collective-permute-start(bf16[32,2944]{1,0:T(8,128)(2,1)S(1)} %collective-permute-done.6.refs_0_), channel_id=1, source_target_pairs={{0,2},{2,0},{4,6},{6,4},{8,10},{10,8},{12,14},{14,12},{1,3},{3,1},... | collective-permute-start | bytes 565256 | tf_op jit(solution)/shard_map/ppermute | solution.py:109
  37.5 18.5 %collective-permute-start.14 = (bf16[32,2944]{1,0:T(8,128)(2,1)S(1)}, bf16[32,2944]{1,0:T(8,128)(2,1)S(1)}, u32[]{:S(2)}, u32[]{:S(2)}) collective-permute-start(bf16[32,2944]{1,0:T(8,128)(2,1)S(1)} %collective-permute-done.13.refs_0_), channel_id=1, source_target_pairs={{0,1},{1,0},{2,3},{3,2},{4,5},{5,4},{6,7},{7,6},{8,9},{9,8},{10,11... | collective-permute-start | bytes 565256 | tf_op jit(solution)/shard_map/ppermute | solution.py:109
  38.4 30.4 %collective-permute-start.15 = (bf16[32,2944]{1,0:T(8,128)(2,1)S(1)}, bf16[32,2944]{1,0:T(8,128)(2,1)S(1)}, u32[]{:S(2)}, u32[]{:S(2)}) collective-permute-start(bf16[32,2944]{1,0:T(8,128)(2,1)S(1)} %collective-permute-done.13.refs_0_), channel_id=1, source_target_pairs={{0,2},{2,0},{4,6},{6,4},{8,10},{10,8},{12,14},{14,12},{1,3},{3,1},... | collective-permute-start | bytes 565256 | tf_op jit(solution)/shard_map/ppermute | solution.py:109
  38.7 17.5 %collective-permute-start.21 = (bf16[32,2944]{1,0:T(8,128)(2,1)S(1)}, bf16[32,2944]{1,0:T(8,128)(2,1)S(1)}, u32[]{:S(2)}, u32[]{:S(2)}) collective-permute-start(bf16[32,2944]{1,0:T(8,128)(2,1)S(1)} %collective-permute-done.20.refs_0_), channel_id=1, source_target_pairs={{0,1},{1,0},{2,3},{3,2},{4,5},{5,4},{6,7},{7,6},{8,9},{9,8},{10,11... | collective-permute-start | bytes 565256 | tf_op jit(solution)/shard_map/ppermute | solution.py:109
  39.8 16.8 %collective-permute-start.9 = (bf16[32,2944]{1,0:T(8,128)(2,1)S(1)}, bf16[32,2944]{1,0:T(8,128)(2,1)S(1)}, u32[]{:S(2)}, u32[]{:S(2)}) collective-permute-start(bf16[32,2944]{1,0:T(8,128)(2,1)S(1)} %collective-permute-done.7.refs_1_), channel_id=1, source_target_pairs={{0,2},{2,0},{4,6},{6,4},{8,10},{10,8},{12,14},{14,12},{1,3},{3,1},... | collective-permute-start | bytes 565256 | tf_op jit(solution)/shard_map/ppermute | solution.py:109
  39.8 5.8 %copy-start = (bf16[1,2880,2,1440]{1,3,2,0:T(8,128)(2,1)S(1)}, bf16[1,2880,2,1440]{1,3,2,0:T(8,128)(2,1)}, u32[]{:S(2)}) copy-start(bf16[1,2880,2,1440]{1,3,2,0:T(8,128)(2,1)} %param.10) | copy-start | bytes 49766404
  45.6 3.4 %copy-start.2 = (bf16[1,1440,2880]{2,1,0:T(8,128)(2,1)S(1)}, bf16[1,1440,2880]{2,1,0:T(8,128)(2,1)}, u32[]{:S(2)}) copy-start(bf16[1,1440,2880]{2,1,0:T(8,128)(2,1)} %param.11) | copy-start | bytes 24883204
  49.0 7.6 %slice-start.1 = ((s8[8478720]{0:T(1024)(128)(4,1)}), s8[4194304]{0:T(1024)(128)(4,1)S(1)}, s32[]{:S(2)}) async-start(s8[8478720]{0:T(1024)(128)(4,1)} %bitcast.11), calls=%async_computation.1 | async-start | bytes 8388608
  49.0 7.6 %slice-start.2 = ((s8[8478720]{0:T(1024)(128)(4,1)}), s8[4194304]{0:T(1024)(128)(4,1)S(1)}, s32[]{:S(2)}) async-start(s8[8478720]{0:T(1024)(128)(4,1)} %bitcast.11), calls=%async_computation.2 | async-start | bytes 8388608
  55.5 20.7 %collective-permute-start.22 = (bf16[32,2944]{1,0:T(8,128)(2,1)S(1)}, bf16[32,2944]{1,0:T(8,128)(2,1)S(1)}, u32[]{:S(2)}, u32[]{:S(2)}) collective-permute-start(bf16[32,2944]{1,0:T(8,128)(2,1)S(1)} %collective-permute-done.20.refs_0_), channel_id=1, source_target_pairs={{0,2},{2,0},{4,6},{6,4},{8,10},{10,8},{12,14},{14,12},{1,3},{3,1},... | collective-permute-start | bytes 565256 | tf_op jit(solution)/shard_map/ppermute | solution.py:109
  56.0 27.0 %collective-permute-start.4 = (bf16[64,2880]{1,0:T(8,128)(2,1)S(1)}, bf16[64,2880]{1,0:T(8,128)(2,1)S(1)}, u32[]{:S(2)}, u32[]{:S(2)}) collective-permute-start(bf16[64,2880]{1,0:T(8,128)(2,1)S(1)} %get-tuple-element.14), channel_id=1, source_target_pairs={{0,2},{2,0},{4,6},{6,4},{8,10},{10,8},{12,14},{14,12},{1,3},{3,1},... | collective-permute-start | bytes 1105928 | tf_op jit(solution)/shard_map/ppermute | solution.py:109
  56.1 13.3 %collective-permute-start.16 = (bf16[32,2944]{1,0:T(8,128)(2,1)S(1)}, bf16[32,2944]{1,0:T(8,128)(2,1)S(1)}, u32[]{:S(2)}, u32[]{:S(2)}) collective-permute-start(bf16[32,2944]{1,0:T(8,128)(2,1)S(1)} %collective-permute-done.14.refs_1_), channel_id=1, source_target_pairs={{0,2},{2,0},{4,6},{6,4},{8,10},{10,8},{12,14},{14,12},{1,3},{3,1},... | collective-permute-start | bytes 565256 | tf_op jit(solution)/shard_map/ppermute | solution.py:109
  56.6 19.6 %collective-permute-start.23 = (bf16[32,2944]{1,0:T(8,128)(2,1)S(1)}, bf16[32,2944]{1,0:T(8,128)(2,1)S(1)}, u32[]{:S(2)}, u32[]{:S(2)}) collective-permute-start(bf16[32,2944]{1,0:T(8,128)(2,1)S(1)} %collective-permute-done.21.refs_1_), channel_id=1, source_target_pairs={{0,2},{2,0},{4,6},{6,4},{8,10},{10,8},{12,14},{14,12},{1,3},{3,1},... | collective-permute-start | bytes 565256 | tf_op jit(solution)/shard_map/ppermute | solution.py:109
  56.6 5.8 %copy-start.1 = (bf16[1,2880,2,1440]{1,3,2,0:T(8,128)(2,1)S(1)}, bf16[1,2880,2,1440]{1,3,2,0:T(8,128)(2,1)}, u32[]{:S(2)}) copy-start(bf16[1,2880,2,1440]{1,3,2,0:T(8,128)(2,1)} %param.10) | copy-start | bytes 49766404
  68.9 15.2 %collective-permute-start.10 = (bf16[64,2880]{1,0:T(8,128)(2,1)S(1)}, bf16[64,2880]{1,0:T(8,128)(2,1)S(1)}, u32[]{:S(2)}, u32[]{:S(2)}) collective-permute-start(bf16[64,2880]{1,0:T(8,128)(2,1)S(1)} %get-tuple-element.16), channel_id=1, source_target_pairs={{0,2},{2,0},{4,6},{6,4},{8,10},{10,8},{12,14},{14,12},{1,3},{3,1},... | collective-permute-start | bytes 1105928 | tf_op jit(solution)/shard_map/ppermute | solution.py:109
  76.0 9.4 %collective-permute-start.17 = (bf16[64,2880]{1,0:T(8,128)(2,1)S(1)}, bf16[64,2880]{1,0:T(8,128)(2,1)S(1)}, u32[]{:S(2)}, u32[]{:S(2)}) collective-permute-start(bf16[64,2880]{1,0:T(8,128)(2,1)S(1)} %get-tuple-element.18), channel_id=1, source_target_pairs={{0,2},{2,0},{4,6},{6,4},{8,10},{10,8},{12,14},{14,12},{1,3},{3,1},... | collective-permute-start | bytes 1105928 | tf_op jit(solution)/shard_map/ppermute | solution.py:109
  82.5 4.0 %collective-permute-start.24 = (bf16[64,2880]{1,0:T(8,128)(2,1)S(1)}, bf16[64,2880]{1,0:T(8,128)(2,1)S(1)}, u32[]{:S(2)}, u32[]{:S(2)}) collective-permute-start(bf16[64,2880]{1,0:T(8,128)(2,1)S(1)} %get-tuple-element.20), channel_id=1, source_target_pairs={{0,2},{2,0},{4,6},{6,4},{8,10},{10,8},{12,14},{14,12},{1,3},{3,1},... | collective-permute-start | bytes 1105928 | tf_op jit(solution)/shard_map/ppermute | solution.py:109
  83.1 21.5 %collective-permute-start.5 = (bf16[32,2880]{1,0:T(8,128)(2,1)S(1)}, bf16[32,2880]{1,0:T(8,128)(2,1)S(1)}, u32[]{:S(2)}, u32[]{:S(2)}) collective-permute-start(bf16[32,2880]{1,0:T(8,128)(2,1)S(1)} %slice.69), channel_id=1, source_target_pairs={{0,1},{1,0},{2,3},{3,2},{4,5},{5,4},{6,7},{7,6},{8,9},{9,8},{10,11... | collective-permute-start | bytes 552968 | tf_op jit(solution)/shard_map/ppermute | solution.py:109
  84.2 10.6 %collective-permute-start.11 = (bf16[32,2880]{1,0:T(8,128)(2,1)S(1)}, bf16[32,2880]{1,0:T(8,128)(2,1)S(1)}, u32[]{:S(2)}, u32[]{:S(2)}) collective-permute-start(bf16[32,2880]{1,0:T(8,128)(2,1)S(1)} %slice.68), channel_id=1, source_target_pairs={{0,1},{1,0},{2,3},{3,2},{4,5},{5,4},{6,7},{7,6},{8,9},{9,8},{10,11... | collective-permute-start | bytes 552968 | tf_op jit(solution)/shard_map/ppermute | solution.py:109
  85.5 13.3 %collective-permute-start.18 = (bf16[32,2880]{1,0:T(8,128)(2,1)S(1)}, bf16[32,2880]{1,0:T(8,128)(2,1)S(1)}, u32[]{:S(2)}, u32[]{:S(2)}) collective-permute-start(bf16[32,2880]{1,0:T(8,128)(2,1)S(1)} %slice.67), channel_id=1, source_target_pairs={{0,1},{1,0},{2,3},{3,2},{4,5},{5,4},{6,7},{7,6},{8,9},{9,8},{10,11... | collective-permute-start | bytes 552968 | tf_op jit(solution)/shard_map/ppermute | solution.py:109
  86.6 16.2 %collective-permute-start.25 = (bf16[32,2880]{1,0:T(8,128)(2,1)S(1)}, bf16[32,2880]{1,0:T(8,128)(2,1)S(1)}, u32[]{:S(2)}, u32[]{:S(2)}) collective-permute-start(bf16[32,2880]{1,0:T(8,128)(2,1)S(1)} %slice.66), channel_id=1, source_target_pairs={{0,1},{1,0},{2,3},{3,2},{4,5},{5,4},{6,7},{7,6},{8,9},{9,8},{10,11... | collective-permute-start | bytes 552968 | tf_op jit(solution)/shard_map/ppermute | solution.py:109
  94.8 9.8 %collective-permute-start.12 = (bf16[32,2880]{1,0:T(8,128)(2,1)S(1)}, bf16[32,2880]{1,0:T(8,128)(2,1)S(1)}, u32[]{:S(2)}, u32[]{:S(2)}) collective-permute-start(bf16[32,2880]{1,0:T(8,128)(2,1)S(1)} %fusion.2), channel_id=1, source_target_pairs={{0,4},{2,6},{4,0},{6,2},{8,12},{10,14},{12,8},{14,10},{1,5},{3,7},... | collective-permute-start | bytes 552968 | tf_op jit(solution)/shard_map/ppermute | solution.py:109
  98.9 17.2 %collective-permute-start.19 = (bf16[32,2880]{1,0:T(8,128)(2,1)S(1)}, bf16[32,2880]{1,0:T(8,128)(2,1)S(1)}, u32[]{:S(2)}, u32[]{:S(2)}) collective-permute-start(bf16[32,2880]{1,0:T(8,128)(2,1)S(1)} %fusion.1), channel_id=1, source_target_pairs={{0,8},{2,10},{4,12},{6,14},{8,0},{10,2},{12,4},{14,6},{1,9},{3,11}... | collective-permute-start | bytes 552968 | tf_op jit(solution)/shard_map/ppermute | solution.py:109
  102.8 13.2 %collective-permute-start.26 = (bf16[32,2880]{1,0:T(8,128)(2,1)S(1)}, bf16[32,2880]{1,0:T(8,128)(2,1)S(1)}, u32[]{:S(2)}, u32[]{:S(2)}) collective-permute-start(bf16[32,2880]{1,0:T(8,128)(2,1)S(1)} %fusion), channel_id=1, source_target_pairs={{0,12},{2,14},{4,8},{6,10},{8,4},{10,6},{12,0},{14,2},{1,13},{3,15... | collective-permute-start | bytes 552968 | tf_op jit(solution)/shard_map/ppermute | solution.py:109

commit v2 on v1

v2 whole, which is shorter than its diff:
```python
import functools

import jax
import jax.numpy as jnp
from jax import lax
from jax.experimental import pallas as pl
from jax.experimental.pallas import tpu as pltpu
from jax.sharding import PartitionSpec as P

F32 = jnp.float32
BF16 = jnp.bfloat16
NT = (((1,), (1,)), ((), ()))
TN = (((0,), (0,)), ((), ()))

AHEAD = 2
CHEAP = pl.CostEstimate(flops=0, bytes_accessed=0, transcendentals=0)


def project_kernel(tile, tensor_ref, heads_hbm, w_hbm, *refs):
    *part_refs, heads_ref, w_ref, out_ref, heads_sem, sems = refs
    width, depth = w_ref.shape
    first = pltpu.make_async_copy(heads_hbm, heads_ref, heads_sem)
    first.start()
    tiles = [(start, min(tile, width - start)) for start in range(0, width, tile)]
    copies = []
    for i, (start, size) in enumerate(tiles):
        rows = pl.ds(start, size)
        copies.append(pltpu.make_async_copy(w_hbm.at[rows], w_ref.at[rows], sems.at[i]))
    for copy in copies[:AHEAD]:
        copy.start()
    first.wait()
    heads = heads_ref[...]
    for i, (start, size) in enumerate(tiles):
        copies[i].wait()
        if i + AHEAD < len(tiles):
            copies[i + AHEAD].start()
        out = lax.dot_general(heads, w_ref[start : start + size], NT, preferred_element_type=F32)
        out_ref[:, start : start + size] = out.astype(BF16)
    tokens = part_refs[0].shape[0]
    for j, part_ref in enumerate(part_refs):
        start = pl.multiple_of((tensor_ref[0] ^ j) * tokens, tokens)
        part_ref[...] = out_ref[pl.ds(start, tokens)]


def project(tensor, heads_out, out_proj_t, tensors):
    rows, depth = heads_out.shape
    width = out_proj_t.shape[0]
    tile = 384
    hbm = pl.BlockSpec(memory_space=pltpu.HBM)
    part = jax.ShapeDtypeStruct((rows // tensors, width), BF16)
    return pl.pallas_call(
        functools.partial(project_kernel, tile),
        in_specs=[pl.BlockSpec(memory_space=pltpu.SMEM), hbm, hbm],
        out_specs=[pl.BlockSpec(memory_space=pltpu.VMEM)] * tensors,
        out_shape=[part] * tensors,
        scratch_shapes=[
            pltpu.VMEM((rows, depth), BF16),
            pltpu.VMEM((width, depth), BF16),
            pltpu.VMEM((rows, width), BF16),
            pltpu.SemaphoreType.DMA,
            pltpu.SemaphoreType.DMA((pl.cdiv(width, tile),)),
        ],
        compiler_params=pltpu.CompilerParams(vmem_limit_bytes=24 * 2**20),
        cost_estimate=CHEAP,
        name="project",
    )(
        tensor,
        pltpu.with_memory_space_constraint(heads_out, pltpu.HBM),
        pltpu.with_memory_space_constraint(out_proj_t, pltpu.HBM),
    )


def norm_kernel(experts, *refs):
    *parts, gain_ref, routes_ref, weights_ref, _, out_ref = refs
    hidden = parts[0][...].astype(F32)
    for part in parts[1:]:
        hidden = hidden + part[...].astype(F32)
    rows, width = hidden.shape
    scale = lax.rsqrt(jnp.mean(hidden * hidden, axis=1, keepdims=True) + 1e-05)
    out_ref[:, :width] = (hidden * scale * gain_ref[...]).astype(BF16)
    extra = out_ref.shape[1] - width
    column = lax.broadcasted_iota(jnp.int32, (rows, extra), 1)
    expert, term = lax.rem(column, experts), lax.div(column, experts)
    weight = jnp.zeros((rows, extra), F32)
    for k in range(routes_ref.shape[1]):
        weight = weight + jnp.where(routes_ref[:, k : k + 1] == expert, weights_ref[:, k : k + 1], 0.0)
    high = weight.astype(BF16).astype(F32)
    middle = (weight - high).astype(BF16).astype(F32)
    low = weight - high - middle
    out_ref[:, width:] = jnp.where(
        term == 0, high, jnp.where(term == 1, middle, jnp.where(term == 2, low, 0.0))
    ).astype(BF16)


def expert_kernel(experts, pieces, expert_ref, *refs):
    tokens = refs[:pieces]
    w_in_ref, w_out_ref = refs[pieces : pieces + 2]
    near_ref, far_ref, act_ref = refs[-3:]
    hidden, width = w_out_ref.shape
    block = jnp.concatenate([piece[...] for piece in tokens], axis=0)
    x, extra = block[:, :width], block[:, width:].astype(F32)
    column = lax.broadcasted_iota(jnp.int32, extra.shape, 1)
    mine = (lax.rem(column, experts) == expert_ref[0]) & (column < 3 * experts)
    weight = jnp.sum(jnp.where(mine, extra, 0.0), axis=1, keepdims=True)
    step = 480 if hidden % 480 == 0 else hidden
    for start in range(0, hidden, step):
        gate = lax.dot_general(w_in_ref[0, start : start + step], x, NT, preferred_element_type=F32)
        up = lax.dot_general(w_in_ref[1, start : start + step], x, NT, preferred_element_type=F32)
        act = gate * jax.nn.sigmoid(1.702 * gate) * (up + 1.0)
        act_ref[start : start + step, :] = act.astype(BF16)
    out = lax.dot_general(act_ref[...], w_out_ref[...], TN, preferred_element_type=F32) * weight
    half = out.shape[0] // 2
    near_ref[...] = out[:half].astype(BF16).reshape(near_ref.shape)
    far_ref[...] = out[half:].astype(BF16).reshape(far_ref.shape)


def expert_chunk(expert, tokens, w_in, w_out, experts, after):
    rows = sum(piece.shape[0] for piece in tokens)
    hidden, width = w_out.shape
    vmem = pl.BlockSpec(memory_space=pltpu.VMEM)
    unit = tokens[0].shape[0]
    half = jax.ShapeDtypeStruct((rows // 2 // unit, unit, width), BF16)
    return pl.pallas_call(
        functools.partial(expert_kernel, experts, len(tokens)),
        in_specs=[pl.BlockSpec(memory_space=pltpu.SMEM)]
        + [vmem] * (len(tokens) + 2)
        + [pl.BlockSpec(memory_space=pl.ANY)] * len(after),
        out_specs=[vmem, vmem],
        out_shape=[half, half],
        scratch_shapes=[pltpu.VMEM((hidden, rows), BF16)],
        compiler_params=pltpu.CompilerParams(vmem_limit_bytes=24 * 2**20),
        cost_estimate=pl.CostEstimate(
            flops=6 * rows * hidden * width, bytes_accessed=rows * width, transcendentals=rows * hidden
        ),
        name="expert",
    )(
        expert,
        *tokens,
        pltpu.with_memory_space_constraint(w_in, pltpu.VMEM),
        pltpu.with_memory_space_constraint(w_out, pltpu.VMEM),
        *after,
    )


def load_kernel(source_ref, *refs):
    target_ref, token_ref, sem = refs[-3:]
    copy = pltpu.make_async_copy(source_ref, target_ref, sem)
    copy.start()
    token_ref[...] = jnp.zeros_like(token_ref)
    copy.wait()


def load(weights, after):
    return pl.pallas_call(
        load_kernel,
        in_specs=[pl.BlockSpec(memory_space=pltpu.HBM)] + [pl.BlockSpec(memory_space=pl.ANY)] * len(after),
        out_specs=[pl.BlockSpec(memory_space=pltpu.VMEM)] * 2,
        out_shape=[pltpu.VMEM(weights.shape, weights.dtype), jax.ShapeDtypeStruct((8, 128), F32)],
        scratch_shapes=[pltpu.SemaphoreType.DMA],
        compiler_params=pltpu.CompilerParams(vmem_limit_bytes=2**20),
        cost_estimate=pl.CostEstimate(flops=0, bytes_accessed=2 * weights.size, transcendentals=0),
        name="load",
    )(pltpu.with_memory_space_constraint(weights, pltpu.HBM), *after)


def add_kernel(kept, near_ref, far_ref, *out_refs):
    for i, out_ref in enumerate(out_refs):
        total = near_ref[i].astype(F32) + far_ref[i].astype(F32)
        out_ref[...] = total.astype(out_ref.dtype)


def add_split(near, far, kept):
    blocks, *shape = near.shape
    return pl.pallas_call(
        functools.partial(add_kernel, kept),
        out_shape=[jax.ShapeDtypeStruct(shape, F32 if i < kept else BF16) for i in range(blocks)],
        compiler_params=pltpu.CompilerParams(vmem_limit_bytes=16 * 2**20),
        cost_estimate=CHEAP,
        name="add_split",
    )(near, far)


def gate_kernel(count, *refs):
    for source_ref, out_ref in zip(refs[:count], refs[len(refs) - count :]):
        out_ref[...] = source_ref[...]


def gate(values, after):
    vmem = pl.BlockSpec(memory_space=pltpu.VMEM)
    return pl.pallas_call(
        functools.partial(gate_kernel, len(values)),
        in_specs=[vmem] * len(values) + [pl.BlockSpec(memory_space=pl.ANY)] * len(after),
        out_specs=[vmem] * len(values),
        out_shape=[jax.ShapeDtypeStruct(value.shape, value.dtype) for value in values],
        compiler_params=pltpu.CompilerParams(vmem_limit_bytes=4 * 2**20),
        cost_estimate=CHEAP,
        name="gate",
    )(*values, *after)


def sum_kernel(count, *refs):
    total = refs[0][...].astype(F32)
    for term in refs[1:count]:
        total = total + term[...].astype(F32)
    refs[-1][...] = total.astype(refs[-1].dtype)


def add_up(terms, dtype, after=()):
    vmem = pl.BlockSpec(memory_space=pltpu.VMEM)
    return pl.pallas_call(
        functools.partial(sum_kernel, len(terms)),
        in_specs=[vmem] * len(terms) + [pl.BlockSpec(memory_space=pl.ANY)] * len(after),
        out_specs=vmem,
        out_shape=jax.ShapeDtypeStruct(terms[0].shape, dtype),
        compiler_params=pltpu.CompilerParams(vmem_limit_bytes=16 * 2**20),
        cost_estimate=CHEAP,
        name="add_up",
    )(*terms, *after)


def per_device(sizes, heads_out, out_proj, norm_gain, gate_up, down_proj, routes, gate_weights):
    experts, tensors = sizes
    tokens = routes.shape[0]
    width = out_proj.shape[1]
    padded = -(-(width + 3 * experts) // 128) * 128
    expert = lax.axis_index("expert")
    tensor = lax.axis_index("tensor")

    def swap(values, axis, distance):
        pairs = [(i, i ^ distance) for i in range(lax.axis_size(axis))]
        return lax.ppermute(values, axis, pairs)

    mine, *sent = project(tensor.reshape(1), heads_out, out_proj.T, tensors)
    gain = norm_gain.reshape(1, width)
    me = expert.reshape(1)
    w_in, w_in_there = load(gate_up[0].transpose(1, 2, 0), [*sent, gain, routes, gate_weights, me])
    parts = [mine] + [swap(sent[j - 1], "tensor", j) for j in range(1, tensors)]
    own = pl.pallas_call(
        functools.partial(norm_kernel, experts),
        in_specs=[pl.BlockSpec(memory_space=pltpu.VMEM)] * (tensors + 3) + [pl.BlockSpec(memory_space=pl.ANY)],
        out_shape=jax.ShapeDtypeStruct((tokens, padded), BF16),
        compiler_params=pltpu.CompilerParams(vmem_limit_bytes=8 * 2**20),
        name="norm",
    )(*parts, gain, routes, gate_weights, w_in_there)
    w_out, w_out_there = load(down_proj[0], [own])

    chips = experts // 2
    relayed = chips > 3
    order = [0, 1, 3, 2, *range(4, chips)][:chips] if relayed else list(range(chips))
    arrived = {0: own}
    for k in order[1:]:
        if relayed and k == 2:
            arrived[k] = swap(arrived[3], "expert", 2)
        else:
            arrived[k] = swap(own, "expert", 2 * k)
        if relayed and k == 3:
            (arrived[k],) = gate([arrived[k]], [w_out_there])
    chunks = [order[i : i + 2] for i in range(0, chips, 2)]

    def across(k):
        return [arrived[k]] + [swap(arrived[k], "tensor", j) for j in range(1, tensors)]

    here = {k: across(k) for k in order}
    sums, after = {}, ([arrived[2], *here[3][1:]] if relayed else [])
    for number, chunk in enumerate(chunks):
        there = {k: [swap(piece, "expert", 1) for piece in here[k]] for k in chunk}
        ordered = [side[k][j] for side in (here, there) for j in range(tensors) for k in chunk]
        near, far = expert_chunk(me, ordered, w_in, w_out, experts, after)
        after = []
        if number == 0 and len(chunks) > 1:
            last = here[chunks[1][-1]]
            far, *last[1:] = gate([far, *last[1:]], [])
        elif number == 1:
            (far,) = gate([far], sums[chunks[0][-1]][1:])
        count = len(chunk)
        added = add_split(near, swap(far, "expert", 1), count)
        for i, k in enumerate(chunk):
            sums[k] = [added[i], *(swap(added[j * count + i], "tensor", j) for j in range(1, tensors))]

    def back(k, after=()):
        distance = 1 if relayed and k == 3 else k
        return swap(add_up(sums[k], BF16, after), "expert", 2 * distance)

    terms = list(sums[0])
    for k in order[1:]:
        if relayed and k == 3:
            sums[2].append(back(k, terms[-1:]))
        else:
            terms.append(back(k))
    return add_up(terms, BF16)


def solution(mesh):
    return jax.shard_map(
        functools.partial(per_device, (mesh.shape["expert"], mesh.shape["tensor"])),
        mesh=mesh,
        in_specs=(
            P(("group", "expert"), "tensor"),
            P("tensor", None),
            P(),
            P("expert", None, None, "tensor"),
            P("expert", "tensor", None),
            P(("group", "expert", "tensor"), None),
            P(("group", "expert", "tensor"), None),
        ),
        out_specs=P(("group", "expert", "tensor"), None),
        check_vma=False,
    )
```

time: 117 us -> 84.4 us (0.72)
  local copies, waits for them, and re-layouts: 20.7 us -> 0.19 us
  waiting for transfers between devices: 34.4 us -> 24.7 us
  starting transfers between devices: 29.2 us -> 26.3 us
  Pallas kernels: 31.2 us -> 32.9 us
  other arithmetic: 1.21 us -> 0 us
    unnamed x24 -> x8, local copies, waits for them, and re-layouts: 20.6 us -> 0.19 us
    pallas_call x2 -> x13, Pallas kernels: 5.37 us -> 18.4 us  [the longest x2 9.25 us: load(): pl.pallas_call(load_kernel, in_specs=[pl.BlockSpec(memory_space=pltpu.HBM...]
    pallas_call x4 -> x2, Pallas kernels: 25.8 us -> 14.5 us  [expert_chunk(): pl.pallas_call(functools.partial(expert_kernel, experts, len(tokens)), in...]
    ppermute x27 -> x25, waiting for transfers between devices: 34.4 us -> 24.7 us  [swap(): return lax.ppermute(values, axis, pairs)]
    ppermute x27 -> x25, starting transfers between devices: 29.2 us -> 26.3 us  [swap(): return lax.ppermute(values, axis, pairs)]
  transfers between devices with their start and end apart: 27 -> 25, of which waited for: 6 -> 11; matrix products, arithmetic and copies ran while one was open for 1% -> 0% of each run, Pallas kernels for 22% -> 29%
where the time goes in v2:
time: 84.4 us; the launch traced here: 84.2 us
  Pallas kernels  32.9 us (39%)
  starting transfers between devices  26.3 us (31%)
  waiting for transfers between devices  24.7 us (29%)
    ppermute x25, starting transfers between devices, swap(): return lax.ppermute(values, axis, pairs)  26.3 us
    ppermute x25, waiting for transfers between devices, swap(): return lax.ppermute(values, axis, pairs)  24.7 us
    pallas_call x2, Pallas kernels, expert_chunk(): pl.pallas_call(functools.partial(expert_kernel, experts, len(tokens)), in...  14.5 us
    pallas_call x2, Pallas kernels, load(): pl.pallas_call(load_kernel, in_specs=[pl.BlockSpec(memory_space=pltpu.HBM...  9.25 us
    pallas_call x1, Pallas kernels, project(): pl.pallas_call(functools.partial(project_kernel, tile), in_specs=[pl.Bloc...  7.43 us
  transfers between devices with their start and end apart: 25, of which 11 were waited for; matrix products, arithmetic and copies ran while one was open for 0% of the time, Pallas kernels for 29%

profile of v2, /device:TPU:0, one launch (start us, length us, event | category | flops | bytes accessed | tf_op | source)
XLA Modules:
  0.0 84.2 jit_solution(6699868665806563085)
XLA Ops:
  0.0 7.4 %project.1 = (bf16[32,2880]{1,0:T(8,128)(2,1)S(1)}, bf16[32,2880]{1,0:T(8,128)(2,1)S(1)}) custom-call(s32[1]{0:T(128)} %bitcast.1.tensor_ref, bf16[64,2048]{1,0:T(8,128)(2,1)} %heads_hbm.1, bf16[2880,2048]{1,0:T(8,128)(2,1)} %bitcast.8), custom_call_target="tpu_custom_call" | custom-call | tf_op jit(solution)/shard_map/project/pallas_call | solution.py:51
  7.4 3.0 %collective-permute-start = (bf16[32,2880]{1,0:T(8,128)(2,1)S(1)}, bf16[32,2880]{1,0:T(8,128)(2,1)S(1)}, u32[]{:S(2)}, u32[]{:S(2)}) collective-permute-start(bf16[32,2880]{1,0:T(8,128)(2,1)S(1)} %get-tuple-element.26.refs_0_), channel_id=1, source_target_pairs={{0,1},{1,0},{2,3},{3,2},{4,5},{5,4},{6,7},{7,6},{8,9},{9,8},{10,11... | collective-permute-start | bytes 552968 | tf_op jit(solution)/shard_map/ppermute | solution.py:231
  10.5 0.1 copy.10.refs_2_.refs_3_
  10.6 0.1 copy.11.refs_3_.refs_4_
  10.7 5.8 %load.2 = (bf16[2,1440,2880]{2,1,0:T(8,128)(2,1)S(1)}, f32[8,128]{1,0:T(8,128)S(1)}) custom-call(bf16[2,1440,2880]{2,1,0:T(8,128)(2,1)} %bitcast.7, bf16[32,2880]{1,0:T(8,128)(2,1)S(1)} %get-tuple-element.26.refs_0_, f32[1,2880]{1,0:T(1,128)S(1)} %reshape.11.refs_1_.refs_2_, s32[32,4]{1,0:T(8,128)S(1)} %copy.10.refs_2_.refs_3_, ...), custom_call_target="tpu_custom_call" | custom-call | bytes 16588800 | tf_op jit(solution)/shard_map/load/pallas_call | solution.py:154
  16.5 0.3 norm.1.refs_0_
  16.8 1.6 %collective-permute-start.1 = (bf16[32,2944]{1,0:T(8,128)(2,1)S(1)}, bf16[32,2944]{1,0:T(8,128)(2,1)S(1)}, u32[]{:S(2)}, u32[]{:S(2)}) collective-permute-start(bf16[32,2944]{1,0:T(8,128)(2,1)S(1)} %norm.1.refs_0_), channel_id=1, source_target_pairs={{0,4},{2,6},{4,0},{6,2},{8,12},{10,14},{12,8},{14,10},{1,5},{3,7},... | collective-permute-start | bytes 565256 | tf_op jit(solution)/shard_map/ppermute | solution.py:231
  18.4 2.5 %collective-permute-start.8 = (bf16[32,2944]{1,0:T(8,128)(2,1)S(1)}, bf16[32,2944]{1,0:T(8,128)(2,1)S(1)}, u32[]{:S(2)}, u32[]{:S(2)}) collective-permute-start(bf16[32,2944]{1,0:T(8,128)(2,1)S(1)} %norm.1.refs_0_), channel_id=1, source_target_pairs={{0,12},{2,14},{4,8},{6,10},{8,4},{10,6},{12,0},{14,2},{1,13},{3,15... | collective-permute-start | bytes 565256 | tf_op jit(solution)/shard_map/ppermute | solution.py:231
  20.9 0.5 collective-permute-start.2
  21.4 2.2 %collective-permute-done.1.refs_1_ = bf16[32,2944]{1,0:T(8,128)(2,1)S(1)} collective-permute-done((bf16[32,2944]{1,0:T(8,128)(2,1)S(1)}, bf16[32,2944]{1,0:T(8,128)(2,1)S(1)}, u32[]{:S(2)}, u32[]{:S(2)}) %collective-permute-start.1) | collective-permute-done | bytes 188448 | tf_op jit(solution)/shard_map/ppermute | solution.py:231
  23.5 0.5 collective-permute-start.3
  24.1 3.4 %load.3 = (bf16[1440,2880]{1,0:T(8,128)(2,1)S(1)}, f32[8,128]{1,0:T(8,128)S(1)}) custom-call(bf16[1440,2880]{1,0:T(8,128)(2,1)} %bitcast.9, bf16[32,2944]{1,0:T(8,128)(2,1)S(1)} %norm.1.refs_0_), custom_call_target="tpu_custom_call" | custom-call | bytes 8294400 | tf_op jit(solution)/shard_map/load/pallas_call | solution.py:154
  27.5 1.7 %collective-permute-done.8.refs_0_ = bf16[32,2944]{1,0:T(8,128)(2,1)S(1)} collective-permute-done((bf16[32,2944]{1,0:T(8,128)(2,1)S(1)}, bf16[32,2944]{1,0:T(8,128)(2,1)S(1)}, u32[]{:S(2)}, u32[]{:S(2)}) %collective-permute-start.8) | collective-permute-done | bytes 188448 | tf_op jit(solution)/shard_map/ppermute | solution.py:231
  29.2 0.9 %collective-permute-start.9 = (bf16[32,2944]{1,0:T(8,128)(2,1)S(1)}, bf16[32,2944]{1,0:T(8,128)(2,1)S(1)}, u32[]{:S(2)}, u32[]{:S(2)}) collective-permute-start(bf16[32,2944]{1,0:T(8,128)(2,1)S(1)} %gate.3.refs_0_), channel_id=1, source_target_pairs={{0,4},{2,6},{4,0},{6,2},{8,12},{10,14},{12,8},{14,10},{1,5},{3,7},... | collective-permute-start | bytes 565256 | tf_op jit(solution)/shard_map/ppermute | solution.py:231
  30.1 1.5 %collective-permute-start.10 = (bf16[32,2944]{1,0:T(8,128)(2,1)S(1)}, bf16[32,2944]{1,0:T(8,128)(2,1)S(1)}, u32[]{:S(2)}, u32[]{:S(2)}) collective-permute-start(bf16[32,2944]{1,0:T(8,128)(2,1)S(1)} %gate.3.refs_0_), channel_id=1, source_target_pairs={{0,1},{1,0},{2,3},{3,2},{4,5},{5,4},{6,7},{7,6},{8,9},{9,8},{10,11... | collective-permute-start | bytes 565256 | tf_op jit(solution)/shard_map/ppermute | solution.py:231
  31.6 0.5 collective-permute-start.6
  32.1 0.1 collective-permute-start.7
  32.2 2.6 %collective-permute-done.9.refs_10_.refs_1_ = bf16[32,2944]{1,0:T(8,128)(2,1)S(1)} collective-permute-done((bf16[32,2944]{1,0:T(8,128)(2,1)S(1)}, bf16[32,2944]{1,0:T(8,128)(2,1)S(1)}, u32[]{:S(2)}, u32[]{:S(2)}) %collective-permute-start.9) | collective-permute-done | bytes 188448 | tf_op jit(solution)/shard_map/ppermute | solution.py:231
  34.8 0.5 collective-permute-start.11
  35.3 0.9 %collective-permute-done.10.refs_11_.refs_2_ = bf16[32,2944]{1,0:T(8,128)(2,1)S(1)} collective-permute-done((bf16[32,2944]{1,0:T(8,128)(2,1)S(1)}, bf16[32,2944]{1,0:T(8,128)(2,1)S(1)}, u32[]{:S(2)}, u32[]{:S(2)}) %collective-permute-start.10) | collective-permute-done | bytes 188448 | tf_op jit(solution)/shard_map/ppermute | solution.py:231
  36.2 7.2 %expert.2 = (bf16[4,32,2880]{2,1,0:T(8,128)(2,1)S(1)}, bf16[4,32,2880]{2,1,0:T(8,128)(2,1)S(1)}) custom-call(s32[1]{0:T(128)} %bitcast.refs_4_.expert_ref, bf16[32,2944]{1,0:T(8,128)(2,1)S(1)} %norm.1.refs_0_, bf16[32,2944]{1,0:T(8,128)(2,1)S(1)} %collective-permute-done.1.refs_1_, bf16[32,2944]{1,0:T(8,128)(2,1)S(1)} %collective-permute-done.2.refs_2_, ...), custom_call_target="tpu_custom_call" | custom-call | flops 6370099200 | bytes 737280 | tf_op jit(solution)/shard_map/expert/pallas_call | solution.py:123
  43.5 0.1 gate.4
  43.5 0.1 collective-permute-start.12
  43.6 0.5 collective-permute-start.16
  44.1 0.1 collective-permute-start.17
  44.2 0.4 collective-permute-start.18
  44.6 0.1 collective-permute-start.19
  44.7 1.1 %collective-permute-done.12.far_ref = bf16[4,32,2880]{2,1,0:T(8,128)(2,1)S(1)} collective-permute-done((bf16[4,32,2880]{2,1,0:T(8,128)(2,1)S(1)}, bf16[4,32,2880]{2,1,0:T(8,128)(2,1)S(1)}, u32[]{:S(2)}, u32[]{:S(2)}) %collective-permute-start.12) | collective-permute-done | bytes 737312 | tf_op jit(solution)/shard_map/ppermute | solution.py:231
  45.8 0.2 add_split.2
  46.0 2.6 %collective-permute-start.14 = (bf16[32,2880]{1,0:T(8,128)(2,1)S(1)}, bf16[32,2880]{1,0:T(8,128)(2,1)S(1)}, u32[]{:S(2)}, u32[]{:S(2)}) collective-permute-start(bf16[32,2880]{1,0:T(8,128)(2,1)S(1)} %get-tuple-element.37), channel_id=1, source_target_pairs={{0,1},{1,0},{2,3},{3,2},{4,5},{5,4},{6,7},{7,6},{8,9},{9,8},{10,11... | collective-permute-start | bytes 552968 | tf_op jit(solution)/shard_map/ppermute | solution.py:231
  48.6 7.3 %expert.3 = (bf16[4,32,2880]{2,1,0:T(8,128)(2,1)S(1)}, bf16[4,32,2880]{2,1,0:T(8,128)(2,1)S(1)}) custom-call(s32[1]{0:T(128)} %bitcast.refs_4_.expert_ref, bf16[32,2944]{1,0:T(8,128)(2,1)S(1)} %gate.3.refs_0_, bf16[32,2944]{1,0:T(8,128)(2,1)S(1)} %collective-permute-done.9.refs_10_.refs_1_, bf16[32,2944]{1,0:T(8,128)(2,1)S(1)} %collective-permute-done.10.refs_11_.refs_2_, ...), custom_call_target="tpu_custom_call" | custom-call | flops 6370099200 | bytes 737280 | tf_op jit(solution)/shard_map/expert/pallas_call | solution.py:123
  55.9 0.1 gate.5
  55.9 0.1 collective-permute-start.20
  56.1 0.7 collective-permute-start.15
  56.7 1.5 %collective-permute-done.20.far_ref = bf16[4,32,2880]{2,1,0:T(8,128)(2,1)S(1)} collective-permute-done((bf16[4,32,2880]{2,1,0:T(8,128)(2,1)S(1)}, bf16[4,32,2880]{2,1,0:T(8,128)(2,1)S(1)}, u32[]{:S(2)}, u32[]{:S(2)}) %collective-permute-start.20) | collective-permute-done | bytes 737312 | tf_op jit(solution)/shard_map/ppermute | solution.py:231
  58.2 0.2 add_split.3
  58.4 0.8 %collective-permute-start.22 = (bf16[32,2880]{1,0:T(8,128)(2,1)S(1)}, bf16[32,2880]{1,0:T(8,128)(2,1)S(1)}, u32[]{:S(2)}, u32[]{:S(2)}) collective-permute-start(bf16[32,2880]{1,0:T(8,128)(2,1)S(1)} %get-tuple-element.44), channel_id=1, source_target_pairs={{0,1},{1,0},{2,3},{3,2},{4,5},{5,4},{6,7},{7,6},{8,9},{9,8},{10,11... | collective-permute-start | bytes 552968 | tf_op jit(solution)/shard_map/ppermute | solution.py:231
  59.3 1.2 %collective-permute-start.21 = (bf16[32,2880]{1,0:T(8,128)(2,1)S(1)}, bf16[32,2880]{1,0:T(8,128)(2,1)S(1)}, u32[]{:S(2)}, u32[]{:S(2)}) collective-permute-start(bf16[32,2880]{1,0:T(8,128)(2,1)S(1)} %get-tuple-element.42), channel_id=1, source_target_pairs={{0,1},{1,0},{2,3},{3,2},{4,5},{5,4},{6,7},{7,6},{8,9},{9,8},{10,11... | collective-permute-start | bytes 552968 | tf_op jit(solution)/shard_map/ppermute | solution.py:231
  60.5 2.7 %collective-permute-done.15.refs_2_ = bf16[32,2880]{1,0:T(8,128)(2,1)S(1)} collective-permute-done((bf16[32,2880]{1,0:T(8,128)(2,1)S(1)}, bf16[32,2880]{1,0:T(8,128)(2,1)S(1)}, u32[]{:S(2)}, u32[]{:S(2)}) %collective-permute-start.15) | collective-permute-done | bytes 184352 | tf_op jit(solution)/shard_map/ppermute | solution.py:231
  63.3 2.8 %collective-permute-done.22.refs_1_ = bf16[32,2880]{1,0:T(8,128)(2,1)S(1)} collective-permute-done((bf16[32,2880]{1,0:T(8,128)(2,1)S(1)}, bf16[32,2880]{1,0:T(8,128)(2,1)S(1)}, u32[]{:S(2)}, u32[]{:S(2)}) %collective-permute-start.22) | collective-permute-done | bytes 184352 | tf_op jit(solution)/shard_map/ppermute | solution.py:231
  66.1 0.5 collective-permute-start.23
  66.7 1.2 %collective-permute-start.13 = (bf16[32,2880]{1,0:T(8,128)(2,1)S(1)}, bf16[32,2880]{1,0:T(8,128)(2,1)S(1)}, u32[]{:S(2)}, u32[]{:S(2)}) collective-permute-start(bf16[32,2880]{1,0:T(8,128)(2,1)S(1)} %get-tuple-element.35), channel_id=1, source_target_pairs={{0,1},{1,0},{2,3},{3,2},{4,5},{5,4},{6,7},{7,6},{8,9},{9,8},{10,11... | collective-permute-start | bytes 552968 | tf_op jit(solution)/shard_map/ppermute | solution.py:231
  67.9 2.2 %collective-permute-done.21.refs_1_ = bf16[32,2880]{1,0:T(8,128)(2,1)S(1)} collective-permute-done((bf16[32,2880]{1,0:T(8,128)(2,1)S(1)}, bf16[32,2880]{1,0:T(8,128)(2,1)S(1)}, u32[]{:S(2)}, u32[]{:S(2)}) %collective-permute-start.21) | collective-permute-done | bytes 184352 | tf_op jit(solution)/shard_map/ppermute | solution.py:231
  70.1 1.7 %collective-permute-done.23.refs_2_ = bf16[32,2880]{1,0:T(8,128)(2,1)S(1)} collective-permute-done((bf16[32,2880]{1,0:T(8,128)(2,1)S(1)}, bf16[32,2880]{1,0:T(8,128)(2,1)S(1)}, u32[]{:S(2)}, u32[]{:S(2)}) %collective-permute-start.23) | collective-permute-done | bytes 184352 | tf_op jit(solution)/shard_map/ppermute | solution.py:231
  71.8 0.1 add_up.6
  71.8 6.4 %collective-permute-start.24 = (bf16[32,2880]{1,0:T(8,128)(2,1)S(1)}, bf16[32,2880]{1,0:T(8,128)(2,1)S(1)}, u32[]{:S(2)}, u32[]{:S(2)}) collective-permute-start(bf16[32,2880]{1,0:T(8,128)(2,1)S(1)} %add_up.6), channel_id=1, source_target_pairs={{0,8},{2,10},{4,12},{6,14},{8,0},{10,2},{12,4},{14,6},{1,9},{3,11}... | collective-permute-start | bytes 552968 | tf_op jit(solution)/shard_map/ppermute | solution.py:231
  78.3 5.2 %collective-permute-done.24.refs_3_ = bf16[32,2880]{1,0:T(8,128)(2,1)S(1)} collective-permute-done((bf16[32,2880]{1,0:T(8,128)(2,1)S(1)}, bf16[32,2880]{1,0:T(8,128)(2,1)S(1)}, u32[]{:S(2)}, u32[]{:S(2)}) %collective-permute-start.24) | collective-permute-done | bytes 184352 | tf_op jit(solution)/shard_map/ppermute | solution.py:231
  83.5 0.8 add_up.7
  (26 shorter events, 0.2 us)
Async XLA Ops:
  0.0 10.5 %copy-start = (f32[2880]{0:T(1024)S(1)}, f32[2880]{0:T(1024)}, u32[]{:S(2)}) copy-start(f32[2880]{0:T(1024)} %param.9) | copy-start | bytes 34564
  0.0 10.5 %copy-start.1 = (s32[32,4]{0,1:T(4,128)S(1)}, s32[32,4]{0,1:T(4,128)}, u32[]{:S(2)}) copy-start(s32[32,4]{0,1:T(4,128)} %param.12) | copy-start | bytes 1540
  0.0 10.6 %copy-start.2 = (f32[32,4]{0,1:T(4,128)S(1)}, f32[32,4]{0,1:T(4,128)}, u32[]{:S(2)}) copy-start(f32[32,4]{0,1:T(4,128)} %param.13) | copy-start | bytes 1540
  7.4 9.1 %collective-permute-start = (bf16[32,2880]{1,0:T(8,128)(2,1)S(1)}, bf16[32,2880]{1,0:T(8,128)(2,1)S(1)}, u32[]{:S(2)}, u32[]{:S(2)}) collective-permute-start(bf16[32,2880]{1,0:T(8,128)(2,1)S(1)} %get-tuple-element.26.refs_0_), channel_id=1, source_target_pairs={{0,1},{1,0},{2,3},{3,2},{4,5},{5,4},{6,7},{7,6},{8,9},{9,8},{10,11... | collective-permute-start | bytes 552968 | tf_op jit(solution)/shard_map/ppermute | solution.py:231
  16.8 6.8 %collective-permute-start.1 = (bf16[32,2944]{1,0:T(8,128)(2,1)S(1)}, bf16[32,2944]{1,0:T(8,128)(2,1)S(1)}, u32[]{:S(2)}, u32[]{:S(2)}) collective-permute-start(bf16[32,2944]{1,0:T(8,128)(2,1)S(1)} %norm.1.refs_0_), channel_id=1, source_target_pairs={{0,4},{2,6},{4,0},{6,2},{8,12},{10,14},{12,8},{14,10},{1,5},{3,7},... | collective-permute-start | bytes 565256 | tf_op jit(solution)/shard_map/ppermute | solution.py:231
  18.4 10.8 %collective-permute-start.8 = (bf16[32,2944]{1,0:T(8,128)(2,1)S(1)}, bf16[32,2944]{1,0:T(8,128)(2,1)S(1)}, u32[]{:S(2)}, u32[]{:S(2)}) collective-permute-start(bf16[32,2944]{1,0:T(8,128)(2,1)S(1)} %norm.1.refs_0_), channel_id=1, source_target_pairs={{0,12},{2,14},{4,8},{6,10},{8,4},{10,6},{12,0},{14,2},{1,13},{3,15... | collective-permute-start | bytes 565256 | tf_op jit(solution)/shard_map/ppermute | solution.py:231
  20.9 10.7 %collective-permute-start.2 = (bf16[32,2944]{1,0:T(8,128)(2,1)S(1)}, bf16[32,2944]{1,0:T(8,128)(2,1)S(1)}, u32[]{:S(2)}, u32[]{:S(2)}) collective-permute-start(bf16[32,2944]{1,0:T(8,128)(2,1)S(1)} %norm.1.refs_0_), channel_id=1, source_target_pairs={{0,1},{1,0},{2,3},{3,2},{4,5},{5,4},{6,7},{7,6},{8,9},{9,8},{10,11... | collective-permute-start | bytes 565256 | tf_op jit(solution)/shard_map/ppermute | solution.py:231
  21.4 10.2 %collective-permute-start.4 = (bf16[32,2944]{1,0:T(8,128)(2,1)S(1)}, bf16[32,2944]{1,0:T(8,128)(2,1)S(1)}, u32[]{:S(2)}, u32[]{:S(2)}) collective-permute-start(bf16[32,2944]{1,0:T(8,128)(2,1)S(1)} %norm.1.refs_0_), channel_id=1, source_target_pairs={{0,2},{2,0},{4,6},{6,4},{8,10},{10,8},{12,14},{14,12},{1,3},{3,1},... | collective-permute-start | bytes 565256 | tf_op jit(solution)/shard_map/ppermute | solution.py:231
  23.5 8.6 %collective-permute-start.3 = (bf16[32,2944]{1,0:T(8,128)(2,1)S(1)}, bf16[32,2944]{1,0:T(8,128)(2,1)S(1)}, u32[]{:S(2)}, u32[]{:S(2)}) collective-permute-start(bf16[32,2944]{1,0:T(8,128)(2,1)S(1)} %collective-permute-done.1.refs_1_), channel_id=1, source_target_pairs={{0,1},{1,0},{2,3},{3,2},{4,5},{5,4},{6,7},{7,6},{8,9},{9,8},{10,11... | collective-permute-start | bytes 565256 | tf_op jit(solution)/shard_map/ppermute | solution.py:231
  29.2 5.6 %collective-permute-start.9 = (bf16[32,2944]{1,0:T(8,128)(2,1)S(1)}, bf16[32,2944]{1,0:T(8,128)(2,1)S(1)}, u32[]{:S(2)}, u32[]{:S(2)}) collective-permute-start(bf16[32,2944]{1,0:T(8,128)(2,1)S(1)} %gate.3.refs_0_), channel_id=1, source_target_pairs={{0,4},{2,6},{4,0},{6,2},{8,12},{10,14},{12,8},{14,10},{1,5},{3,7},... | collective-permute-start | bytes 565256 | tf_op jit(solution)/shard_map/ppermute | solution.py:231
  30.1 6.1 %collective-permute-start.10 = (bf16[32,2944]{1,0:T(8,128)(2,1)S(1)}, bf16[32,2944]{1,0:T(8,128)(2,1)S(1)}, u32[]{:S(2)}, u32[]{:S(2)}) collective-permute-start(bf16[32,2944]{1,0:T(8,128)(2,1)S(1)} %gate.3.refs_0_), channel_id=1, source_target_pairs={{0,1},{1,0},{2,3},{3,2},{4,5},{5,4},{6,7},{7,6},{8,9},{9,8},{10,11... | collective-permute-start | bytes 565256 | tf_op jit(solution)/shard_map/ppermute | solution.py:231
  31.6 3.7 %collective-permute-start.5 = (bf16[32,2944]{1,0:T(8,128)(2,1)S(1)}, bf16[32,2944]{1,0:T(8,128)(2,1)S(1)}, u32[]{:S(2)}, u32[]{:S(2)}) collective-permute-start(bf16[32,2944]{1,0:T(8,128)(2,1)S(1)} %collective-permute-done.1.refs_1_), channel_id=1, source_target_pairs={{0,2},{2,0},{4,6},{6,4},{8,10},{10,8},{12,14},{14,12},{1,3},{3,1},... | collective-permute-start | bytes 565256 | tf_op jit(solution)/shard_map/ppermute | solution.py:231
  31.6 3.7 %collective-permute-start.6 = (bf16[32,2944]{1,0:T(8,128)(2,1)S(1)}, bf16[32,2944]{1,0:T(8,128)(2,1)S(1)}, u32[]{:S(2)}, u32[]{:S(2)}) collective-permute-start(bf16[32,2944]{1,0:T(8,128)(2,1)S(1)} %collective-permute-done.2.refs_2_), channel_id=1, source_target_pairs={{0,2},{2,0},{4,6},{6,4},{8,10},{10,8},{12,14},{14,12},{1,3},{3,1},... | collective-permute-start | bytes 565256 | tf_op jit(solution)/shard_map/ppermute | solution.py:231
  32.1 4.1 %collective-permute-start.7 = (bf16[32,2944]{1,0:T(8,128)(2,1)S(1)}, bf16[32,2944]{1,0:T(8,128)(2,1)S(1)}, u32[]{:S(2)}, u32[]{:S(2)}) collective-permute-start(bf16[32,2944]{1,0:T(8,128)(2,1)S(1)} %collective-permute-done.3.refs_3_), channel_id=1, source_target_pairs={{0,2},{2,0},{4,6},{6,4},{8,10},{10,8},{12,14},{14,12},{1,3},{3,1},... | collective-permute-start | bytes 565256 | tf_op jit(solution)/shard_map/ppermute | solution.py:231
  34.8 8.6 %collective-permute-start.11 = (bf16[32,2944]{1,0:T(8,128)(2,1)S(1)}, bf16[32,2944]{1,0:T(8,128)(2,1)S(1)}, u32[]{:S(2)}, u32[]{:S(2)}) collective-permute-start(bf16[32,2944]{1,0:T(8,128)(2,1)S(1)} %collective-permute-done.9.refs_10_.refs_1_), channel_id=1, source_target_pairs={{0,1},{1,0},{2,3},{3,2},{4,5},{5,4},{6,7},{7,6},{8,9},{9,8},{10,11... | collective-permute-start | bytes 565256 | tf_op jit(solution)/shard_map/ppermute | solution.py:231
  43.5 2.3 %collective-permute-start.12 = (bf16[4,32,2880]{2,1,0:T(8,128)(2,1)S(1)}, bf16[4,32,2880]{2,1,0:T(8,128)(2,1)S(1)}, u32[]{:S(2)}, u32[]{:S(2)}) collective-permute-start(bf16[4,32,2880]{2,1,0:T(8,128)(2,1)S(1)} %get-tuple-element.33), channel_id=1, source_target_pairs={{0,2},{2,0},{4,6},{6,4},{8,10},{10,8},{12,14},{14,12},{1,3},{3,1},... | collective-permute-start | bytes 2211848 | tf_op jit(solution)/shard_map/ppermute | solution.py:231
  43.6 5.0 %collective-permute-start.16 = (bf16[32,2944]{1,0:T(8,128)(2,1)S(1)}, bf16[32,2944]{1,0:T(8,128)(2,1)S(1)}, u32[]{:S(2)}, u32[]{:S(2)}) collective-permute-start(bf16[32,2944]{1,0:T(8,128)(2,1)S(1)} %gate.3.refs_0_), channel_id=1, source_target_pairs={{0,2},{2,0},{4,6},{6,4},{8,10},{10,8},{12,14},{14,12},{1,3},{3,1},... | collective-permute-start | bytes 565256 | tf_op jit(solution)/shard_map/ppermute | solution.py:231
  44.1 4.5 %collective-permute-start.17 = (bf16[32,2944]{1,0:T(8,128)(2,1)S(1)}, bf16[32,2944]{1,0:T(8,128)(2,1)S(1)}, u32[]{:S(2)}, u32[]{:S(2)}) collective-permute-start(bf16[32,2944]{1,0:T(8,128)(2,1)S(1)} %collective-permute-done.9.refs_10_.refs_1_), channel_id=1, source_target_pairs={{0,2},{2,0},{4,6},{6,4},{8,10},{10,8},{12,14},{14,12},{1,3},{3,1},... | collective-permute-start | bytes 565256 | tf_op jit(solution)/shard_map/ppermute | solution.py:231
  44.2 4.4 %collective-permute-start.18 = (bf16[32,2944]{1,0:T(8,128)(2,1)S(1)}, bf16[32,2944]{1,0:T(8,128)(2,1)S(1)}, u32[]{:S(2)}, u32[]{:S(2)}) collective-permute-start(bf16[32,2944]{1,0:T(8,128)(2,1)S(1)} %collective-permute-done.10.refs_11_.refs_2_), channel_id=1, source_target_pairs={{0,2},{2,0},{4,6},{6,4},{8,10},{10,8},{12,14},{14,12},{1,3},{3,1},... | collective-permute-start | bytes 565256 | tf_op jit(solution)/shard_map/ppermute | solution.py:231
  44.6 4.0 %collective-permute-start.19 = (bf16[32,2944]{1,0:T(8,128)(2,1)S(1)}, bf16[32,2944]{1,0:T(8,128)(2,1)S(1)}, u32[]{:S(2)}, u32[]{:S(2)}) collective-permute-start(bf16[32,2944]{1,0:T(8,128)(2,1)S(1)} %get-tuple-element.38.refs_3_), channel_id=1, source_target_pairs={{0,2},{2,0},{4,6},{6,4},{8,10},{10,8},{12,14},{14,12},{1,3},{3,1},... | collective-permute-start | bytes 565256 | tf_op jit(solution)/shard_map/ppermute | solution.py:231
  46.0 9.8 %collective-permute-start.14 = (bf16[32,2880]{1,0:T(8,128)(2,1)S(1)}, bf16[32,2880]{1,0:T(8,128)(2,1)S(1)}, u32[]{:S(2)}, u32[]{:S(2)}) collective-permute-start(bf16[32,2880]{1,0:T(8,128)(2,1)S(1)} %get-tuple-element.37), channel_id=1, source_target_pairs={{0,1},{1,0},{2,3},{3,2},{4,5},{5,4},{6,7},{7,6},{8,9},{9,8},{10,11... | collective-permute-start | bytes 552968 | tf_op jit(solution)/shard_map/ppermute | solution.py:231
  55.9 2.3 %collective-permute-start.20 = (bf16[4,32,2880]{2,1,0:T(8,128)(2,1)S(1)}, bf16[4,32,2880]{2,1,0:T(8,128)(2,1)S(1)}, u32[]{:S(2)}, u32[]{:S(2)}) collective-permute-start(bf16[4,32,2880]{2,1,0:T(8,128)(2,1)S(1)} %gate.5), channel_id=1, source_target_pairs={{0,2},{2,0},{4,6},{6,4},{8,10},{10,8},{12,14},{14,12},{1,3},{3,1},... | collective-permute-start | bytes 2211848 | tf_op jit(solution)/shard_map/ppermute | solution.py:231
  56.1 7.2 %collective-permute-start.15 = (bf16[32,2880]{1,0:T(8,128)(2,1)S(1)}, bf16[32,2880]{1,0:T(8,128)(2,1)S(1)}, u32[]{:S(2)}, u32[]{:S(2)}) collective-permute-start(bf16[32,2880]{1,0:T(8,128)(2,1)S(1)} %add_up.4), channel_id=1, source_target_pairs={{0,4},{2,6},{4,0},{6,2},{8,12},{10,14},{12,8},{14,10},{1,5},{3,7},... | collective-permute-start | bytes 552968 | tf_op jit(solution)/shard_map/ppermute | solution.py:231
  58.4 7.6 %collective-permute-start.22 = (bf16[32,2880]{1,0:T(8,128)(2,1)S(1)}, bf16[32,2880]{1,0:T(8,128)(2,1)S(1)}, u32[]{:S(2)}, u32[]{:S(2)}) collective-permute-start(bf16[32,2880]{1,0:T(8,128)(2,1)S(1)} %get-tuple-element.44), channel_id=1, source_target_pairs={{0,1},{1,0},{2,3},{3,2},{4,5},{5,4},{6,7},{7,6},{8,9},{9,8},{10,11... | collective-permute-start | bytes 552968 | tf_op jit(solution)/shard_map/ppermute | solution.py:231
  59.3 10.8 %collective-permute-start.21 = (bf16[32,2880]{1,0:T(8,128)(2,1)S(1)}, bf16[32,2880]{1,0:T(8,128)(2,1)S(1)}, u32[]{:S(2)}, u32[]{:S(2)}) collective-permute-start(bf16[32,2880]{1,0:T(8,128)(2,1)S(1)} %get-tuple-element.42), channel_id=1, source_target_pairs={{0,1},{1,0},{2,3},{3,2},{4,5},{5,4},{6,7},{7,6},{8,9},{9,8},{10,11... | collective-permute-start | bytes 552968 | tf_op jit(solution)/shard_map/ppermute | solution.py:231
  66.1 5.6 %collective-permute-start.23 = (bf16[32,2880]{1,0:T(8,128)(2,1)S(1)}, bf16[32,2880]{1,0:T(8,128)(2,1)S(1)}, u32[]{:S(2)}, u32[]{:S(2)}) collective-permute-start(bf16[32,2880]{1,0:T(8,128)(2,1)S(1)} %add_up.5), channel_id=1, source_target_pairs={{0,4},{2,6},{4,0},{6,2},{8,12},{10,14},{12,8},{14,10},{1,5},{3,7},... | collective-permute-start | bytes 552968 | tf_op jit(solution)/shard_map/ppermute | solution.py:231
  66.7 11.6 %collective-permute-start.13 = (bf16[32,2880]{1,0:T(8,128)(2,1)S(1)}, bf16[32,2880]{1,0:T(8,128)(2,1)S(1)}, u32[]{:S(2)}, u32[]{:S(2)}) collective-permute-start(bf16[32,2880]{1,0:T(8,128)(2,1)S(1)} %get-tuple-element.35), channel_id=1, source_target_pairs={{0,1},{1,0},{2,3},{3,2},{4,5},{5,4},{6,7},{7,6},{8,9},{9,8},{10,11... | collective-permute-start | bytes 552968 | tf_op jit(solution)/shard_map/ppermute | solution.py:231
  71.8 11.6 %collective-permute-start.24 = (bf16[32,2880]{1,0:T(8,128)(2,1)S(1)}, bf16[32,2880]{1,0:T(8,128)(2,1)S(1)}, u32[]{:S(2)}, u32[]{:S(2)}) collective-permute-start(bf16[32,2880]{1,0:T(8,128)(2,1)S(1)} %add_up.6), channel_id=1, source_target_pairs={{0,8},{2,10},{4,12},{6,14},{8,0},{10,2},{12,4},{14,6},{1,9},{3,11}... | collective-permute-start | bytes 552968 | tf_op jit(solution)/shard_map/ppermute | solution.py:231

commit v3 on v2

--- a/solution.py
+++ b/solution.py
@@ -45,7 +45,7 @@
 def project(tensor, heads_out, out_proj_t, tensors):
     rows, depth = heads_out.shape
     width = out_proj_t.shape[0]
-    tile = 384
+    tile = 512
     hbm = pl.BlockSpec(memory_space=pltpu.HBM)
     part = jax.ShapeDtypeStruct((rows // tensors, width), BF16)
     return pl.pallas_call(
@@ -92,10 +92,10 @@
     ).astype(BF16)
 
 
-def expert_kernel(experts, pieces, expert_ref, *refs):
+def expert_kernel(experts, pieces, outputs, expert_ref, *refs):
     tokens = refs[:pieces]
     w_in_ref, w_out_ref = refs[pieces : pieces + 2]
-    near_ref, far_ref, act_ref = refs[-3:]
+    near_ref, *far_refs, act_ref = refs[outputs:]
     hidden, width = w_out_ref.shape
     block = jnp.concatenate([piece[...] for piece in tokens], axis=0)
     x, extra = block[:, :width], block[:, width:].astype(F32)
@@ -111,22 +111,28 @@
     out = lax.dot_general(act_ref[...], w_out_ref[...], TN, preferred_element_type=F32) * weight
     half = out.shape[0] // 2
     near_ref[...] = out[:half].astype(BF16).reshape(near_ref.shape)
-    far_ref[...] = out[half:].astype(BF16).reshape(far_ref.shape)
-
-
-def expert_chunk(expert, tokens, w_in, w_out, experts, after):
+    far = out[half:].astype(BF16)
+    size = half // len(far_refs)
+    for i, far_ref in enumerate(far_refs):
+        far_ref[...] = far[i * size : (i + 1) * size].reshape(far_ref.shape)
+
+
+def expert_chunk(expert, tokens, w_in, w_out, experts, after, split):
     rows = sum(piece.shape[0] for piece in tokens)
     hidden, width = w_out.shape
     vmem = pl.BlockSpec(memory_space=pltpu.VMEM)
     unit = tokens[0].shape[0]
-    half = jax.ShapeDtypeStruct((rows // 2 // unit, unit, width), BF16)
-    return pl.pallas_call(
-        functools.partial(expert_kernel, experts, len(tokens)),
+    blocks = rows // 2 // unit
+    near = jax.ShapeDtypeStruct((blocks, unit, width), BF16)
+    far = [jax.ShapeDtypeStruct((unit, width), BF16)] * blocks if split else [near]
+    inputs = len(tokens) + 2 + len(after)
+    return pl.pallas_call(
+        functools.partial(expert_kernel, experts, len(tokens), inputs),
         in_specs=[pl.BlockSpec(memory_space=pltpu.SMEM)]
         + [vmem] * (len(tokens) + 2)
         + [pl.BlockSpec(memory_space=pl.ANY)] * len(after),
-        out_specs=[vmem, vmem],
-        out_shape=[half, half],
+        out_specs=[vmem] * (1 + len(far)),
+        out_shape=[near, *far],
         scratch_shapes=[pltpu.VMEM((hidden, rows), BF16)],
         compiler_params=pltpu.CompilerParams(vmem_limit_bytes=24 * 2**20),
         cost_estimate=pl.CostEstimate(
@@ -163,21 +169,38 @@
     )(pltpu.with_memory_space_constraint(weights, pltpu.HBM), *after)
 
 
-def add_kernel(kept, near_ref, far_ref, *out_refs):
-    for i, out_ref in enumerate(out_refs):
-        total = near_ref[i].astype(F32) + far_ref[i].astype(F32)
-        out_ref[...] = total.astype(out_ref.dtype)
-
-
-def add_split(near, far, kept):
+def add_kernel(fars, outputs, near_ref, *refs):
+    far_refs = refs[:fars]
+
+    def block(i):
+        far = far_refs[0][i] if fars == 1 else far_refs[i][...]
+        return near_ref[i].astype(F32) + far.astype(F32)
+
+    done = 0
+    for out_ref in refs[-outputs:]:
+        if len(out_ref.shape) == 2:
+            out_ref[...] = block(done).astype(out_ref.dtype)
+            done += 1
+        else:
+            for i in range(out_ref.shape[0]):
+                out_ref[i] = block(done).astype(out_ref.dtype)
+                done += 1
+
+
+def add_split(near, fars, kept, after):
     blocks, *shape = near.shape
-    return pl.pallas_call(
-        functools.partial(add_kernel, kept),
-        out_shape=[jax.ShapeDtypeStruct(shape, F32 if i < kept else BF16) for i in range(blocks)],
+    vmem = pl.BlockSpec(memory_space=pltpu.VMEM)
+    sent = shape if kept == 1 else (kept, *shape)
+    shapes = [jax.ShapeDtypeStruct(shape, F32)] * kept + [jax.ShapeDtypeStruct(sent, BF16)] * (blocks // kept - 1)
+    return pl.pallas_call(
+        functools.partial(add_kernel, len(fars), len(shapes)),
+        in_specs=[vmem] * (1 + len(fars)) + [pl.BlockSpec(memory_space=pl.ANY)] * len(after),
+        out_specs=[vmem] * len(shapes),
+        out_shape=shapes,
         compiler_params=pltpu.CompilerParams(vmem_limit_bytes=16 * 2**20),
         cost_estimate=CHEAP,
         name="add_split",
-    )(near, far)
+    )(near, *fars, *after)
 
 
 def gate_kernel(count, *refs):
@@ -198,24 +221,27 @@
     )(*values, *after)
 
 
-def sum_kernel(count, *refs):
-    total = refs[0][...].astype(F32)
-    for term in refs[1:count]:
-        total = total + term[...].astype(F32)
+def sum_kernel(places, *refs):
+    total = None
+    for place, ref in zip(places, refs):
+        term = (ref[...] if place is None else ref[place]).astype(F32)
+        total = term if total is None else total + term
     refs[-1][...] = total.astype(refs[-1].dtype)
 
 
 def add_up(terms, dtype, after=()):
     vmem = pl.BlockSpec(memory_space=pltpu.VMEM)
-    return pl.pallas_call(
-        functools.partial(sum_kernel, len(terms)),
+    places = [term[1] if isinstance(term, tuple) else None for term in terms]
+    arrays = [term[0] if isinstance(term, tuple) else term for term in terms]
+    return pl.pallas_call(
+        functools.partial(sum_kernel, places),
         in_specs=[vmem] * len(terms) + [pl.BlockSpec(memory_space=pl.ANY)] * len(after),
         out_specs=vmem,
-        out_shape=jax.ShapeDtypeStruct(terms[0].shape, dtype),
+        out_shape=jax.ShapeDtypeStruct(arrays[0].shape, dtype),
         compiler_params=pltpu.CompilerParams(vmem_limit_bytes=16 * 2**20),
         cost_estimate=CHEAP,
         name="add_up",
-    )(*terms, *after)
+    )(*arrays, *after)
 
 
 def per_device(sizes, heads_out, out_proj, norm_gain, gate_up, down_proj, routes, gate_weights):
@@ -253,40 +279,58 @@
             arrived[k] = swap(arrived[3], "expert", 2)
         else:
             arrived[k] = swap(own, "expert", 2 * k)
-        if relayed and k == 3:
+        if k == 1:
             (arrived[k],) = gate([arrived[k]], [w_out_there])
-    chunks = [order[i : i + 2] for i in range(0, chips, 2)]
+    chunks = [[0], [1, 3], *([k] for k in order[3:])] if relayed else [[k] for k in order]
 
     def across(k):
         return [arrived[k]] + [swap(arrived[k], "tensor", j) for j in range(1, tensors)]
 
-    here = {k: across(k) for k in order}
-    sums, after = {}, ([arrived[2], *here[3][1:]] if relayed else [])
+    here = {k: across(k) for k in order if not relayed or k != 2}
+    sums, came, held = {}, {}, {}
     for number, chunk in enumerate(chunks):
         there = {k: [swap(piece, "expert", 1) for piece in here[k]] for k in chunk}
         ordered = [side[k][j] for side in (here, there) for j in range(tensors) for k in chunk]
-        near, far = expert_chunk(me, ordered, w_in, w_out, experts, after)
-        after = []
-        if number == 0 and len(chunks) > 1:
-            last = here[chunks[1][-1]]
-            far, *last[1:] = gate([far, *last[1:]], [])
-        elif number == 1:
-            (far,) = gate([far], sums[chunks[0][-1]][1:])
+        after = [arrived[3]] if relayed and number == 0 else []
+        near, *far = expert_chunk(me, ordered, w_in, w_out, experts, after, relayed and number == 2)
+        last = []
+        if relayed and number == 0:
+            arrived[2], *pieces = gate([arrived[2], *here[3][1:], *here[1][1:]], [near])
+            here[3][1:], here[1][1:] = pieces[: tensors - 1], pieces[tensors - 1 :]
+            here[2] = across(2)
+        elif relayed and number == 1:
+            both = gate([*far, *here[2][1:]], [])
+            far, here[2][1:] = both[: len(far)], both[len(far) :]
+        elif relayed and number == 2:
+            last = [pair for pair, _ in came[3]]
         count = len(chunk)
-        added = add_split(near, swap(far, "expert", 1), count)
+        added = add_split(near, [swap(block, "expert", 1) for block in far], count, last)
+        if len(chunk) > 1:
+            pairs = [swap(block, "tensor", j + 1) for j, block in enumerate(added[count:])]
+            for i, k in enumerate(chunk):
+                sums[k] = added[i]
+                came[k] = [(pair, i) for pair in pairs]
+            continue
         for i, k in enumerate(chunk):
-            sums[k] = [added[i], *(swap(added[j * count + i], "tensor", j) for j in range(1, tensors))]
-
-    def back(k, after=()):
+            sums[k] = added[i]
+            sent = [added[j * count + i] for j in range(1, tensors)]
+            if relayed and k == 0:
+                held[k] = sent
+            else:
+                came[k] = [swap(piece, "tensor", j + 1) for j, piece in enumerate(sent)]
+    if relayed:
+        held[0] = gate(held[0], came[2])
+        came[0] = [swap(piece, "tensor", j + 1) for j, piece in enumerate(held[0])]
+
+    def back(k, more=(), after=()):
         distance = 1 if relayed and k == 3 else k
-        return swap(add_up(sums[k], BF16, after), "expert", 2 * distance)
-
-    terms = list(sums[0])
+        return swap(add_up([sums[k], *came[k], *more], BF16, after), "expert", 2 * distance)
+
+    relay = [back(3)] if relayed else []
+    terms = [sums[0], *came[0]]
     for k in order[1:]:
-        if relayed and k == 3:
-            sums[2].append(back(k, terms[-1:]))
-        else:
-            terms.append(back(k))
+        if not relayed or k != 3:
+            terms.append(back(k, relay if k == 2 else (), relay if k == 1 else ()))
     return add_up(terms, BF16)
 
 

time: 84.4 us -> 77.2 us (0.915)
  waiting for transfers between devices: 24.7 us -> 18.5 us
  starting transfers between devices: 26.3 us -> 21.1 us
  Pallas kernels: 32.9 us -> 36.8 us
    ppermute x25 -> x26, waiting for transfers between devices: 24.7 us -> 18.5 us  [swap(): return lax.ppermute(values, axis, pairs)]
    ppermute x25 -> x26, starting transfers between devices: 26.3 us -> 21.1 us  [swap(): return lax.ppermute(values, axis, pairs)]
    pallas_call x8 -> x10, Pallas kernels: 15.8 us -> 20.5 us  [the longest x3 19.2 us: expert_chunk(): pl.pallas_call(functools.partial(expert_kernel, experts, len(tokens), inp...]
  transfers between devices with their start and end apart: 25 -> 26, of which waited for: 11 -> 13; matrix products, arithmetic and copies ran while one was open for 0% -> 0% of each run, Pallas kernels for 29% -> 38%
where the time goes in v3:
time: 77.2 us; the launch traced here: 76.7 us
  Pallas kernels  36.8 us (48%)
  starting transfers between devices  21.1 us (27%)
  waiting for transfers between devices  18.5 us (24%)
    ppermute x26, starting transfers between devices, swap(): return lax.ppermute(values, axis, pairs)  21.1 us
    pallas_call x3, Pallas kernels, expert_chunk(): pl.pallas_call(functools.partial(expert_kernel, experts, len(tokens), inp...  19.2 us
    ppermute x26, waiting for transfers between devices, swap(): return lax.ppermute(values, axis, pairs)  18.5 us
    pallas_call x2, Pallas kernels, load(): pl.pallas_call(load_kernel, in_specs=[pl.BlockSpec(memory_space=pltpu.HBM...  9.25 us
    pallas_call x1, Pallas kernels, project(): pl.pallas_call(functools.partial(project_kernel, tile), in_specs=[pl.Bloc...  6.66 us
  transfers between devices with their start and end apart: 26, of which 13 were waited for; matrix products, arithmetic and copies ran while one was open for 0% of the time, Pallas kernels for 38%

profile of v3, /device:TPU:0, one launch (start us, length us, event | category | flops | bytes accessed | tf_op | source)
XLA Modules:
  0.0 76.7 jit_solution(7237856407803205973)
XLA Ops:
  0.0 6.7 %project.1 = (bf16[32,2880]{1,0:T(8,128)(2,1)S(1)}, bf16[32,2880]{1,0:T(8,128)(2,1)S(1)}) custom-call(s32[1]{0:T(128)} %bitcast.1.tensor_ref, bf16[64,2048]{1,0:T(8,128)(2,1)} %heads_hbm.1, bf16[2880,2048]{1,0:T(8,128)(2,1)} %bitcast.8), custom_call_target="tpu_custom_call" | custom-call | tf_op jit(solution)/shard_map/project/pallas_call | solution.py:51
  6.7 3.0 %collective-permute-start = (bf16[32,2880]{1,0:T(8,128)(2,1)S(1)}, bf16[32,2880]{1,0:T(8,128)(2,1)S(1)}, u32[]{:S(2)}, u32[]{:S(2)}) collective-permute-start(bf16[32,2880]{1,0:T(8,128)(2,1)S(1)} %get-tuple-element.31.refs_0_), channel_id=1, source_target_pairs={{0,1},{1,0},{2,3},{3,2},{4,5},{5,4},{6,7},{7,6},{8,9},{9,8},{10,11... | collective-permute-start | bytes 552968 | tf_op jit(solution)/shard_map/ppermute | solution.py:257
  9.7 0.1 copy.10.refs_2_.refs_3_
  9.8 0.1 copy.11.refs_3_.refs_4_
  9.9 5.8 %load.2 = (bf16[2,1440,2880]{2,1,0:T(8,128)(2,1)S(1)}, f32[8,128]{1,0:T(8,128)S(1)}) custom-call(bf16[2,1440,2880]{2,1,0:T(8,128)(2,1)} %bitcast.7, bf16[32,2880]{1,0:T(8,128)(2,1)S(1)} %get-tuple-element.31.refs_0_, f32[1,2880]{1,0:T(1,128)S(1)} %reshape.11.refs_1_.refs_2_, s32[32,4]{1,0:T(8,128)S(1)} %copy.10.refs_2_.refs_3_, ...), custom_call_target="tpu_custom_call" | custom-call | bytes 16588800 | tf_op jit(solution)/shard_map/load/pallas_call | solution.py:160
  15.8 0.3 norm.1.refs_0_
  16.0 0.4 collective-permute-start.1
  16.4 1.7 %collective-permute-start.8 = (bf16[32,2944]{1,0:T(8,128)(2,1)S(1)}, bf16[32,2944]{1,0:T(8,128)(2,1)S(1)}, u32[]{:S(2)}, u32[]{:S(2)}) collective-permute-start(bf16[32,2944]{1,0:T(8,128)(2,1)S(1)} %norm.1.refs_0_), channel_id=1, source_target_pairs={{0,4},{2,6},{4,0},{6,2},{8,12},{10,14},{12,8},{14,10},{1,5},{3,7},... | collective-permute-start | bytes 565256 | tf_op jit(solution)/shard_map/ppermute | solution.py:257
  18.1 2.5 %collective-permute-start.4 = (bf16[32,2944]{1,0:T(8,128)(2,1)S(1)}, bf16[32,2944]{1,0:T(8,128)(2,1)S(1)}, u32[]{:S(2)}, u32[]{:S(2)}) collective-permute-start(bf16[32,2944]{1,0:T(8,128)(2,1)S(1)} %norm.1.refs_0_), channel_id=1, source_target_pairs={{0,12},{2,14},{4,8},{6,10},{8,4},{10,6},{12,0},{14,2},{1,13},{3,15... | collective-permute-start | bytes 565256 | tf_op jit(solution)/shard_map/ppermute | solution.py:257
  20.6 1.6 %collective-permute-done.1.refs_1_ = bf16[32,2944]{1,0:T(8,128)(2,1)S(1)} collective-permute-done((bf16[32,2944]{1,0:T(8,128)(2,1)S(1)}, bf16[32,2944]{1,0:T(8,128)(2,1)S(1)}, u32[]{:S(2)}, u32[]{:S(2)}) %collective-permute-start.1) | collective-permute-done | bytes 188448 | tf_op jit(solution)/shard_map/ppermute | solution.py:257
  22.2 3.4 %load.3 = (bf16[1440,2880]{1,0:T(8,128)(2,1)S(1)}, f32[8,128]{1,0:T(8,128)S(1)}) custom-call(bf16[1440,2880]{1,0:T(8,128)(2,1)} %bitcast.9, bf16[32,2944]{1,0:T(8,128)(2,1)S(1)} %norm.1.refs_0_), custom_call_target="tpu_custom_call" | custom-call | bytes 8294400 | tf_op jit(solution)/shard_map/load/pallas_call | solution.py:160
  25.7 0.5 collective-permute-start.9
  26.2 0.2 collective-permute-start.10
  26.3 2.3 %collective-permute-done.4.refs_6_.refs_1_ = bf16[32,2944]{1,0:T(8,128)(2,1)S(1)} collective-permute-done((bf16[32,2944]{1,0:T(8,128)(2,1)S(1)}, bf16[32,2944]{1,0:T(8,128)(2,1)S(1)}, u32[]{:S(2)}, u32[]{:S(2)}) %collective-permute-start.4) | collective-permute-done | bytes 188448 | tf_op jit(solution)/shard_map/ppermute | solution.py:257
  28.6 0.6 collective-permute-start.6
  29.2 1.5 %collective-permute-start.7 = (bf16[32,2944]{1,0:T(8,128)(2,1)S(1)}, bf16[32,2944]{1,0:T(8,128)(2,1)S(1)}, u32[]{:S(2)}, u32[]{:S(2)}) collective-permute-start(bf16[32,2944]{1,0:T(8,128)(2,1)S(1)} %collective-permute-done.4.refs_6_.refs_1_), channel_id=1, source_target_pairs={{0,1},{1,0},{2,3},{3,2},{4,5},{5,4},{6,7},{7,6},{8,9},{9,8},{10,11... | collective-permute-start | bytes 565256 | tf_op jit(solution)/shard_map/ppermute | solution.py:257
  30.7 5.9 %expert.3 = (bf16[2,32,2880]{2,1,0:T(8,128)(2,1)S(1)}, bf16[2,32,2880]{2,1,0:T(8,128)(2,1)S(1)}) custom-call(s32[1]{0:T(128)} %bitcast.refs_4_.expert_ref, bf16[32,2944]{1,0:T(8,128)(2,1)S(1)} %norm.1.refs_0_, bf16[32,2944]{1,0:T(8,128)(2,1)S(1)} %collective-permute-done.1.refs_1_, bf16[32,2944]{1,0:T(8,128)(2,1)S(1)} %collective-permute-done.2.refs_2_, ...), custom_call_target="tpu_custom_call" | custom-call | flops 3185049600 | bytes 368640 | tf_op jit(solution)/shard_map/expert/pallas_call | solution.py:129
  36.6 0.3 collective-permute-done.7.refs_1_
  37.0 0.3 collective-permute-start.12
  37.3 0.3 collective-permute-start.13
  37.5 0.3 collective-permute-start.14
  37.9 0.6 collective-permute-done.12.refs_6_
  38.5 0.3 collective-permute-done.13.refs_7_
  38.7 7.2 %expert.4 = (bf16[4,32,2880]{2,1,0:T(8,128)(2,1)S(1)}, bf16[4,32,2880]{2,1,0:T(8,128)(2,1)S(1)}) custom-call(s32[1]{0:T(128)} %bitcast.refs_4_.expert_ref, bf16[32,2944]{1,0:T(8,128)(2,1)S(1)} %gate.4.refs_0_, bf16[32,2944]{1,0:T(8,128)(2,1)S(1)} %collective-permute-done.4.refs_6_.refs_1_, bf16[32,2944]{1,0:T(8,128)(2,1)S(1)} %get-tuple-element.41.refs_2_, ...), custom_call_target="tpu_custom_call" | custom-call | flops 6370099200 | bytes 737280 | tf_op jit(solution)/shard_map/expert/pallas_call | solution.py:129
  46.1 0.3 collective-permute-start.19
  46.4 0.3 collective-permute-start.15
  46.7 0.2 collective-permute-start.16
  46.9 1.5 %collective-permute-done.19.refs_0_ = bf16[4,32,2880]{2,1,0:T(8,128)(2,1)S(1)} collective-permute-done((bf16[4,32,2880]{2,1,0:T(8,128)(2,1)S(1)}, bf16[4,32,2880]{2,1,0:T(8,128)(2,1)S(1)}, u32[]{:S(2)}, u32[]{:S(2)}) %collective-permute-start.19) | collective-permute-done | bytes 737312 | tf_op jit(solution)/shard_map/ppermute | solution.py:257
  48.4 0.2 add_split.4
  48.6 0.9 %collective-permute-start.20 = (bf16[2,32,2880]{2,1,0:T(8,128)(2,1)S(1)}, bf16[2,32,2880]{2,1,0:T(8,128)(2,1)S(1)}, u32[]{:S(2)}, u32[]{:S(2)}) collective-permute-start(bf16[2,32,2880]{2,1,0:T(8,128)(2,1)S(1)} %get-tuple-element.50), channel_id=1, source_target_pairs={{0,1},{1,0},{2,3},{3,2},{4,5},{5,4},{6,7},{7,6},{8,9},{9,8},{10,11... | collective-permute-start | bytes 1105928 | tf_op jit(solution)/shard_map/ppermute | solution.py:257
  49.5 6.1 %expert.5 = (bf16[2,32,2880]{2,1,0:T(8,128)(2,1)S(1)}, bf16[32,2880]{1,0:T(8,128)(2,1)S(1)}, bf16[32,2880]{1,0:T(8,128)(2,1)S(1)}) custom-call(s32[1]{0:T(128)} %bitcast.refs_4_.expert_ref, bf16[32,2944]{1,0:T(8,128)(2,1)S(1)} %get-tuple-element.40.refs_0_, bf16[32,2944]{1,0:T(8,128)(2,1)S(1)} %get-tuple-element.44.refs_1_, ...), custom_call_target="tpu_custom_call" | custom-call | flops 3185049600 | bytes 368640 | tf_op jit(solution)/shard_map/expert/pallas_call | solution.py:129
  55.7 0.5 collective-permute-start.18
  56.2 0.1 collective-permute-start.5
  56.2 0.8 %collective-permute-done.17.refs_0_ = bf16[32,2880]{1,0:T(8,128)(2,1)S(1)} collective-permute-done((bf16[32,2880]{1,0:T(8,128)(2,1)S(1)}, bf16[32,2880]{1,0:T(8,128)(2,1)S(1)}, u32[]{:S(2)}, u32[]{:S(2)}) %collective-permute-start.17) | collective-permute-done | bytes 184352 | tf_op jit(solution)/shard_map/ppermute | solution.py:257
  57.1 0.3 collective-permute-done.18.refs_1_
  57.4 2.2 %collective-permute-done.20.refs_2_.refs_1_ = bf16[2,32,2880]{2,1,0:T(8,128)(2,1)S(1)} collective-permute-done((bf16[2,32,2880]{2,1,0:T(8,128)(2,1)S(1)}, bf16[2,32,2880]{2,1,0:T(8,128)(2,1)S(1)}, u32[]{:S(2)}, u32[]{:S(2)}) %collective-permute-start.20) | collective-permute-done | bytes 368672 | tf_op jit(solution)/shard_map/ppermute | solution.py:257
  59.6 0.1 add_split.5
  59.6 0.8 %collective-permute-start.21 = (bf16[32,2880]{1,0:T(8,128)(2,1)S(1)}, bf16[32,2880]{1,0:T(8,128)(2,1)S(1)}, u32[]{:S(2)}, u32[]{:S(2)}) collective-permute-start(bf16[32,2880]{1,0:T(8,128)(2,1)S(1)} %get-tuple-element.51), channel_id=1, source_target_pairs={{0,1},{1,0},{2,3},{3,2},{4,5},{5,4},{6,7},{7,6},{8,9},{9,8},{10,11... | collective-permute-start | bytes 552968 | tf_op jit(solution)/shard_map/ppermute | solution.py:257
  60.5 1.6 %collective-permute-start.23 = (bf16[32,2880]{1,0:T(8,128)(2,1)S(1)}, bf16[32,2880]{1,0:T(8,128)(2,1)S(1)}, u32[]{:S(2)}, u32[]{:S(2)}) collective-permute-start(bf16[32,2880]{1,0:T(8,128)(2,1)S(1)} %add_up.4), channel_id=1, source_target_pairs={{0,4},{2,6},{4,0},{6,2},{8,12},{10,14},{12,8},{14,10},{1,5},{3,7},... | collective-permute-start | bytes 552968 | tf_op jit(solution)/shard_map/ppermute | solution.py:257
  62.2 0.1 add_split.3
  62.2 3.5 %collective-permute-done.21.refs_1_ = bf16[32,2880]{1,0:T(8,128)(2,1)S(1)} collective-permute-done((bf16[32,2880]{1,0:T(8,128)(2,1)S(1)}, bf16[32,2880]{1,0:T(8,128)(2,1)S(1)}, u32[]{:S(2)}, u32[]{:S(2)}) %collective-permute-start.21) | collective-permute-done | bytes 184352 | tf_op jit(solution)/shard_map/ppermute | solution.py:257
  65.8 0.7 collective-permute-start.22
  66.5 1.6 %collective-permute-start.24 = (bf16[32,2880]{1,0:T(8,128)(2,1)S(1)}, bf16[32,2880]{1,0:T(8,128)(2,1)S(1)}, u32[]{:S(2)}, u32[]{:S(2)}) collective-permute-start(bf16[32,2880]{1,0:T(8,128)(2,1)S(1)} %add_up.5), channel_id=1, source_target_pairs={{0,4},{2,6},{4,0},{6,2},{8,12},{10,14},{12,8},{14,10},{1,5},{3,7},... | collective-permute-start | bytes 552968 | tf_op jit(solution)/shard_map/ppermute | solution.py:257
  68.3 2.7 %collective-permute-start.25 = (bf16[32,2880]{1,0:T(8,128)(2,1)S(1)}, bf16[32,2880]{1,0:T(8,128)(2,1)S(1)}, u32[]{:S(2)}, u32[]{:S(2)}) collective-permute-start(bf16[32,2880]{1,0:T(8,128)(2,1)S(1)} %add_up.6), channel_id=1, source_target_pairs={{0,8},{2,10},{4,12},{6,14},{8,0},{10,2},{12,4},{14,6},{1,9},{3,11}... | collective-permute-start | bytes 552968 | tf_op jit(solution)/shard_map/ppermute | solution.py:257
  71.0 0.5 collective-permute-done.22.refs_1_
  71.4 3.2 %collective-permute-done.24.refs_2_ = bf16[32,2880]{1,0:T(8,128)(2,1)S(1)} collective-permute-done((bf16[32,2880]{1,0:T(8,128)(2,1)S(1)}, bf16[32,2880]{1,0:T(8,128)(2,1)S(1)}, u32[]{:S(2)}, u32[]{:S(2)}) %collective-permute-start.24) | collective-permute-done | bytes 184352 | tf_op jit(solution)/shard_map/ppermute | solution.py:257
  74.6 1.4 %collective-permute-done.25.refs_3_ = bf16[32,2880]{1,0:T(8,128)(2,1)S(1)} collective-permute-done((bf16[32,2880]{1,0:T(8,128)(2,1)S(1)}, bf16[32,2880]{1,0:T(8,128)(2,1)S(1)}, u32[]{:S(2)}, u32[]{:S(2)}) %collective-permute-start.25) | collective-permute-done | bytes 184352 | tf_op jit(solution)/shard_map/ppermute | solution.py:257
  76.0 0.8 %add_up.7 = bf16[32,2880]{1,0:T(8,128)(2,1)} custom-call(f32[32,2880]{1,0:T(8,128)S(1)} %get-tuple-element.37.refs_0_, bf16[32,2880]{1,0:T(8,128)(2,1)S(1)} %collective-permute-done.22.refs_1_, bf16[32,2880]{1,0:T(8,128)(2,1)S(1)} %collective-permute-done.24.refs_2_, bf16[32,2880]{1,0:T(8,128)(2,1)S(1)} %collective-permute-done.25.refs_3_), custom_call_target="tpu_custom_call" | custom-call | tf_op jit(solution)/shard_map/add_up/pallas_call | solution.py:236
  (31 shorter events, 0.4 us)
Async XLA Ops:
  0.0 9.7 %copy-start = (f32[2880]{0:T(1024)S(1)}, f32[2880]{0:T(1024)}, u32[]{:S(2)}) copy-start(f32[2880]{0:T(1024)} %param.9) | copy-start | bytes 34564
  0.0 9.7 %copy-start.1 = (s32[32,4]{0,1:T(4,128)S(1)}, s32[32,4]{0,1:T(4,128)}, u32[]{:S(2)}) copy-start(s32[32,4]{0,1:T(4,128)} %param.12) | copy-start | bytes 1540
  0.0 9.8 %copy-start.2 = (f32[32,4]{0,1:T(4,128)S(1)}, f32[32,4]{0,1:T(4,128)}, u32[]{:S(2)}) copy-start(f32[32,4]{0,1:T(4,128)} %param.13) | copy-start | bytes 1540
  6.7 9.1 %collective-permute-start = (bf16[32,2880]{1,0:T(8,128)(2,1)S(1)}, bf16[32,2880]{1,0:T(8,128)(2,1)S(1)}, u32[]{:S(2)}, u32[]{:S(2)}) collective-permute-start(bf16[32,2880]{1,0:T(8,128)(2,1)S(1)} %get-tuple-element.31.refs_0_), channel_id=1, source_target_pairs={{0,1},{1,0},{2,3},{3,2},{4,5},{5,4},{6,7},{7,6},{8,9},{9,8},{10,11... | collective-permute-start | bytes 552968 | tf_op jit(solution)/shard_map/ppermute | solution.py:257
  16.0 6.2 %collective-permute-start.1 = (bf16[32,2944]{1,0:T(8,128)(2,1)S(1)}, bf16[32,2944]{1,0:T(8,128)(2,1)S(1)}, u32[]{:S(2)}, u32[]{:S(2)}) collective-permute-start(bf16[32,2944]{1,0:T(8,128)(2,1)S(1)} %norm.1.refs_0_), channel_id=1, source_target_pairs={{0,1},{1,0},{2,3},{3,2},{4,5},{5,4},{6,7},{7,6},{8,9},{9,8},{10,11... | collective-permute-start | bytes 565256 | tf_op jit(solution)/shard_map/ppermute | solution.py:257
  16.4 9.2 %collective-permute-start.8 = (bf16[32,2944]{1,0:T(8,128)(2,1)S(1)}, bf16[32,2944]{1,0:T(8,128)(2,1)S(1)}, u32[]{:S(2)}, u32[]{:S(2)}) collective-permute-start(bf16[32,2944]{1,0:T(8,128)(2,1)S(1)} %norm.1.refs_0_), channel_id=1, source_target_pairs={{0,4},{2,6},{4,0},{6,2},{8,12},{10,14},{12,8},{14,10},{1,5},{3,7},... | collective-permute-start | bytes 565256 | tf_op jit(solution)/shard_map/ppermute | solution.py:257
  18.1 10.5 %collective-permute-start.4 = (bf16[32,2944]{1,0:T(8,128)(2,1)S(1)}, bf16[32,2944]{1,0:T(8,128)(2,1)S(1)}, u32[]{:S(2)}, u32[]{:S(2)}) collective-permute-start(bf16[32,2944]{1,0:T(8,128)(2,1)S(1)} %norm.1.refs_0_), channel_id=1, source_target_pairs={{0,12},{2,14},{4,8},{6,10},{8,4},{10,6},{12,0},{14,2},{1,13},{3,15... | collective-permute-start | bytes 565256 | tf_op jit(solution)/shard_map/ppermute | solution.py:257
  20.6 8.6 %collective-permute-start.2 = (bf16[32,2944]{1,0:T(8,128)(2,1)S(1)}, bf16[32,2944]{1,0:T(8,128)(2,1)S(1)}, u32[]{:S(2)}, u32[]{:S(2)}) collective-permute-start(bf16[32,2944]{1,0:T(8,128)(2,1)S(1)} %norm.1.refs_0_), channel_id=1, source_target_pairs={{0,2},{2,0},{4,6},{6,4},{8,10},{10,8},{12,14},{14,12},{1,3},{3,1},... | collective-permute-start | bytes 565256 | tf_op jit(solution)/shard_map/ppermute | solution.py:257
  22.2 8.5 %collective-permute-start.3 = (bf16[32,2944]{1,0:T(8,128)(2,1)S(1)}, bf16[32,2944]{1,0:T(8,128)(2,1)S(1)}, u32[]{:S(2)}, u32[]{:S(2)}) collective-permute-start(bf16[32,2944]{1,0:T(8,128)(2,1)S(1)} %collective-permute-done.1.refs_1_), channel_id=1, source_target_pairs={{0,2},{2,0},{4,6},{6,4},{8,10},{10,8},{12,14},{14,12},{1,3},{3,1},... | collective-permute-start | bytes 565256 | tf_op jit(solution)/shard_map/ppermute | solution.py:257
  25.7 11.2 %collective-permute-start.9 = (bf16[32,2944]{1,0:T(8,128)(2,1)S(1)}, bf16[32,2944]{1,0:T(8,128)(2,1)S(1)}, u32[]{:S(2)}, u32[]{:S(2)}) collective-permute-start(bf16[32,2944]{1,0:T(8,128)(2,1)S(1)} %gate.4.refs_0_), channel_id=1, source_target_pairs={{0,1},{1,0},{2,3},{3,2},{4,5},{5,4},{6,7},{7,6},{8,9},{9,8},{10,11... | collective-permute-start | bytes 565256 | tf_op jit(solution)/shard_map/ppermute | solution.py:257
  26.2 11.7 %collective-permute-start.10 = (bf16[32,2944]{1,0:T(8,128)(2,1)S(1)}, bf16[32,2944]{1,0:T(8,128)(2,1)S(1)}, u32[]{:S(2)}, u32[]{:S(2)}) collective-permute-start(bf16[32,2944]{1,0:T(8,128)(2,1)S(1)} %gate.4.refs_0_), channel_id=1, source_target_pairs={{0,2},{2,0},{4,6},{6,4},{8,10},{10,8},{12,14},{14,12},{1,3},{3,1},... | collective-permute-start | bytes 565256 | tf_op jit(solution)/shard_map/ppermute | solution.py:257
  28.6 8.0 %collective-permute-start.6 = (bf16[32,2944]{1,0:T(8,128)(2,1)S(1)}, bf16[32,2944]{1,0:T(8,128)(2,1)S(1)}, u32[]{:S(2)}, u32[]{:S(2)}) collective-permute-start(bf16[32,2944]{1,0:T(8,128)(2,1)S(1)} %collective-permute-done.4.refs_6_.refs_1_), channel_id=1, source_target_pairs={{0,4},{2,6},{4,0},{6,2},{8,12},{10,14},{12,8},{14,10},{1,5},{3,7},... | collective-permute-start | bytes 565256 | tf_op jit(solution)/shard_map/ppermute | solution.py:257
  29.2 7.7 %collective-permute-start.7 = (bf16[32,2944]{1,0:T(8,128)(2,1)S(1)}, bf16[32,2944]{1,0:T(8,128)(2,1)S(1)}, u32[]{:S(2)}, u32[]{:S(2)}) collective-permute-start(bf16[32,2944]{1,0:T(8,128)(2,1)S(1)} %collective-permute-done.4.refs_6_.refs_1_), channel_id=1, source_target_pairs={{0,1},{1,0},{2,3},{3,2},{4,5},{5,4},{6,7},{7,6},{8,9},{9,8},{10,11... | collective-permute-start | bytes 565256 | tf_op jit(solution)/shard_map/ppermute | solution.py:257
  30.7 7.2 %collective-permute-start.11 = (bf16[32,2944]{1,0:T(8,128)(2,1)S(1)}, bf16[32,2944]{1,0:T(8,128)(2,1)S(1)}, u32[]{:S(2)}, u32[]{:S(2)}) collective-permute-start(bf16[32,2944]{1,0:T(8,128)(2,1)S(1)} %collective-permute-done.4.refs_6_.refs_1_), channel_id=1, source_target_pairs={{0,2},{2,0},{4,6},{6,4},{8,10},{10,8},{12,14},{14,12},{1,3},{3,1},... | collective-permute-start | bytes 565256 | tf_op jit(solution)/shard_map/ppermute | solution.py:257
  37.0 1.5 %collective-permute-start.12 = (bf16[32,2944]{1,0:T(8,128)(2,1)S(1)}, bf16[32,2944]{1,0:T(8,128)(2,1)S(1)}, u32[]{:S(2)}, u32[]{:S(2)}) collective-permute-start(bf16[32,2944]{1,0:T(8,128)(2,1)S(1)} %get-tuple-element.41.refs_2_), channel_id=1, source_target_pairs={{0,2},{2,0},{4,6},{6,4},{8,10},{10,8},{12,14},{14,12},{1,3},{3,1},... | collective-permute-start | bytes 565256 | tf_op jit(solution)/shard_map/ppermute | solution.py:257
  37.3 1.5 %collective-permute-start.13 = (bf16[32,2944]{1,0:T(8,128)(2,1)S(1)}, bf16[32,2944]{1,0:T(8,128)(2,1)S(1)}, u32[]{:S(2)}, u32[]{:S(2)}) collective-permute-start(bf16[32,2944]{1,0:T(8,128)(2,1)S(1)} %get-tuple-element.42.refs_3_), channel_id=1, source_target_pairs={{0,2},{2,0},{4,6},{6,4},{8,10},{10,8},{12,14},{14,12},{1,3},{3,1},... | collective-permute-start | bytes 565256 | tf_op jit(solution)/shard_map/ppermute | solution.py:257
  37.5 8.4 %collective-permute-start.14 = (bf16[32,2944]{1,0:T(8,128)(2,1)S(1)}, bf16[32,2944]{1,0:T(8,128)(2,1)S(1)}, u32[]{:S(2)}, u32[]{:S(2)}) collective-permute-start(bf16[32,2944]{1,0:T(8,128)(2,1)S(1)} %get-tuple-element.40.refs_0_), channel_id=1, source_target_pairs={{0,1},{1,0},{2,3},{3,2},{4,5},{5,4},{6,7},{7,6},{8,9},{9,8},{10,11... | collective-permute-start | bytes 565256 | tf_op jit(solution)/shard_map/ppermute | solution.py:257
  46.1 2.3 %collective-permute-start.19 = (bf16[4,32,2880]{2,1,0:T(8,128)(2,1)S(1)}, bf16[4,32,2880]{2,1,0:T(8,128)(2,1)S(1)}, u32[]{:S(2)}, u32[]{:S(2)}) collective-permute-start(bf16[4,32,2880]{2,1,0:T(8,128)(2,1)S(1)} %get-tuple-element.49), channel_id=1, source_target_pairs={{0,2},{2,0},{4,6},{6,4},{8,10},{10,8},{12,14},{14,12},{1,3},{3,1},... | collective-permute-start | bytes 2211848 | tf_op jit(solution)/shard_map/ppermute | solution.py:257
  46.4 3.1 %collective-permute-start.15 = (bf16[32,2944]{1,0:T(8,128)(2,1)S(1)}, bf16[32,2944]{1,0:T(8,128)(2,1)S(1)}, u32[]{:S(2)}, u32[]{:S(2)}) collective-permute-start(bf16[32,2944]{1,0:T(8,128)(2,1)S(1)} %get-tuple-element.40.refs_0_), channel_id=1, source_target_pairs={{0,2},{2,0},{4,6},{6,4},{8,10},{10,8},{12,14},{14,12},{1,3},{3,1},... | collective-permute-start | bytes 565256 | tf_op jit(solution)/shard_map/ppermute | solution.py:257
  46.7 2.9 %collective-permute-start.16 = (bf16[32,2944]{1,0:T(8,128)(2,1)S(1)}, bf16[32,2944]{1,0:T(8,128)(2,1)S(1)}, u32[]{:S(2)}, u32[]{:S(2)}) collective-permute-start(bf16[32,2944]{1,0:T(8,128)(2,1)S(1)} %get-tuple-element.44.refs_1_), channel_id=1, source_target_pairs={{0,2},{2,0},{4,6},{6,4},{8,10},{10,8},{12,14},{14,12},{1,3},{3,1},... | collective-permute-start | bytes 565256 | tf_op jit(solution)/shard_map/ppermute | solution.py:257
  48.6 11.0 %collective-permute-start.20 = (bf16[2,32,2880]{2,1,0:T(8,128)(2,1)S(1)}, bf16[2,32,2880]{2,1,0:T(8,128)(2,1)S(1)}, u32[]{:S(2)}, u32[]{:S(2)}) collective-permute-start(bf16[2,32,2880]{2,1,0:T(8,128)(2,1)S(1)} %get-tuple-element.50), channel_id=1, source_target_pairs={{0,1},{1,0},{2,3},{3,2},{4,5},{5,4},{6,7},{7,6},{8,9},{9,8},{10,11... | collective-permute-start | bytes 1105928 | tf_op jit(solution)/shard_map/ppermute | solution.py:257
  55.6 1.5 %collective-permute-start.17 = (bf16[32,2880]{1,0:T(8,128)(2,1)S(1)}, bf16[32,2880]{1,0:T(8,128)(2,1)S(1)}, u32[]{:S(2)}, u32[]{:S(2)}) collective-permute-start(bf16[32,2880]{1,0:T(8,128)(2,1)S(1)} %get-tuple-element.46), channel_id=1, source_target_pairs={{0,2},{2,0},{4,6},{6,4},{8,10},{10,8},{12,14},{14,12},{1,3},{3,1},... | collective-permute-start | bytes 552968 | tf_op jit(solution)/shard_map/ppermute | solution.py:257
  55.7 1.7 %collective-permute-start.18 = (bf16[32,2880]{1,0:T(8,128)(2,1)S(1)}, bf16[32,2880]{1,0:T(8,128)(2,1)S(1)}, u32[]{:S(2)}, u32[]{:S(2)}) collective-permute-start(bf16[32,2880]{1,0:T(8,128)(2,1)S(1)} %get-tuple-element.47), channel_id=1, source_target_pairs={{0,2},{2,0},{4,6},{6,4},{8,10},{10,8},{12,14},{14,12},{1,3},{3,1},... | collective-permute-start | bytes 552968 | tf_op jit(solution)/shard_map/ppermute | solution.py:257
  56.2 6.0 %collective-permute-start.5 = (bf16[2,32,2880]{2,1,0:T(8,128)(2,1)S(1)}, bf16[2,32,2880]{2,1,0:T(8,128)(2,1)S(1)}, u32[]{:S(2)}, u32[]{:S(2)}) collective-permute-start(bf16[2,32,2880]{2,1,0:T(8,128)(2,1)S(1)} %get-tuple-element.36), channel_id=1, source_target_pairs={{0,2},{2,0},{4,6},{6,4},{8,10},{10,8},{12,14},{14,12},{1,3},{3,1},... | collective-permute-start | bytes 1105928 | tf_op jit(solution)/shard_map/ppermute | solution.py:257
  59.6 6.1 %collective-permute-start.21 = (bf16[32,2880]{1,0:T(8,128)(2,1)S(1)}, bf16[32,2880]{1,0:T(8,128)(2,1)S(1)}, u32[]{:S(2)}, u32[]{:S(2)}) collective-permute-start(bf16[32,2880]{1,0:T(8,128)(2,1)S(1)} %get-tuple-element.51), channel_id=1, source_target_pairs={{0,1},{1,0},{2,3},{3,2},{4,5},{5,4},{6,7},{7,6},{8,9},{9,8},{10,11... | collective-permute-start | bytes 552968 | tf_op jit(solution)/shard_map/ppermute | solution.py:257
  60.5 6.0 %collective-permute-start.23 = (bf16[32,2880]{1,0:T(8,128)(2,1)S(1)}, bf16[32,2880]{1,0:T(8,128)(2,1)S(1)}, u32[]{:S(2)}, u32[]{:S(2)}) collective-permute-start(bf16[32,2880]{1,0:T(8,128)(2,1)S(1)} %add_up.4), channel_id=1, source_target_pairs={{0,4},{2,6},{4,0},{6,2},{8,12},{10,14},{12,8},{14,10},{1,5},{3,7},... | collective-permute-start | bytes 552968 | tf_op jit(solution)/shard_map/ppermute | solution.py:257
  65.8 5.6 %collective-permute-start.22 = (bf16[32,2880]{1,0:T(8,128)(2,1)S(1)}, bf16[32,2880]{1,0:T(8,128)(2,1)S(1)}, u32[]{:S(2)}, u32[]{:S(2)}) collective-permute-start(bf16[32,2880]{1,0:T(8,128)(2,1)S(1)} %gate.7), channel_id=1, source_target_pairs={{0,1},{1,0},{2,3},{3,2},{4,5},{5,4},{6,7},{7,6},{8,9},{9,8},{10,11... | collective-permute-start | bytes 552968 | tf_op jit(solution)/shard_map/ppermute | solution.py:257
  66.5 8.1 %collective-permute-start.24 = (bf16[32,2880]{1,0:T(8,128)(2,1)S(1)}, bf16[32,2880]{1,0:T(8,128)(2,1)S(1)}, u32[]{:S(2)}, u32[]{:S(2)}) collective-permute-start(bf16[32,2880]{1,0:T(8,128)(2,1)S(1)} %add_up.5), channel_id=1, source_target_pairs={{0,4},{2,6},{4,0},{6,2},{8,12},{10,14},{12,8},{14,10},{1,5},{3,7},... | collective-permute-start | bytes 552968 | tf_op jit(solution)/shard_map/ppermute | solution.py:257
  68.3 7.7 %collective-permute-start.25 = (bf16[32,2880]{1,0:T(8,128)(2,1)S(1)}, bf16[32,2880]{1,0:T(8,128)(2,1)S(1)}, u32[]{:S(2)}, u32[]{:S(2)}) collective-permute-start(bf16[32,2880]{1,0:T(8,128)(2,1)S(1)} %add_up.6), channel_id=1, source_target_pairs={{0,8},{2,10},{4,12},{6,14},{8,0},{10,2},{12,4},{14,6},{1,9},{3,11}... | collective-permute-start | bytes 552968 | tf_op jit(solution)/shard_map/ppermute | solution.py:257

commit v4 on v3

--- a/solution.py
+++ b/solution.py
@@ -97,7 +97,7 @@
     w_in_ref, w_out_ref = refs[pieces : pieces + 2]
     near_ref, *far_refs, act_ref = refs[outputs:]
     hidden, width = w_out_ref.shape
-    block = jnp.concatenate([piece[...] for piece in tokens], axis=0)
+    block = jnp.concatenate([piece[...].reshape(-1, piece.shape[-1]) for piece in tokens], axis=0)
     x, extra = block[:, :width], block[:, width:].astype(F32)
     column = lax.broadcasted_iota(jnp.int32, extra.shape, 1)
     mine = (lax.rem(column, experts) == expert_ref[0]) & (column < 3 * experts)
@@ -118,7 +118,7 @@
 
 
 def expert_chunk(expert, tokens, w_in, w_out, experts, after, split):
-    rows = sum(piece.shape[0] for piece in tokens)
+    rows = sum(piece.size // piece.shape[-1] for piece in tokens)
     hidden, width = w_out.shape
     vmem = pl.BlockSpec(memory_space=pltpu.VMEM)
     unit = tokens[0].shape[0]
@@ -221,6 +221,28 @@
     )(*values, *after)
 
 
+def stack_kernel(first_ref, second_ref, other_ref, *refs):
+    pair_ref, copy_ref = refs[-2:]
+    pair_ref[0], pair_ref[1] = first_ref[...], second_ref[...]
+    copy_ref[...] = other_ref[...]
+
+
+def stack(first, second, other, after):
+    vmem = pl.BlockSpec(memory_space=pltpu.VMEM)
+    return pl.pallas_call(
+        stack_kernel,
+        in_specs=[vmem] * 3 + [pl.BlockSpec(memory_space=pl.ANY)] * len(after),
+        out_specs=[vmem] * 2,
+        out_shape=[
+            jax.ShapeDtypeStruct((2, *first.shape), first.dtype),
+            jax.ShapeDtypeStruct(other.shape, other.dtype),
+        ],
+        compiler_params=pltpu.CompilerParams(vmem_limit_bytes=4 * 2**20),
+        cost_estimate=CHEAP,
+        name="stack",
+    )(first, second, other, *after)
+
+
 def sum_kernel(places, *refs):
     total = None
     for place, ref in zip(places, refs):
@@ -289,14 +311,20 @@
     here = {k: across(k) for k in order if not relayed or k != 2}
     sums, came, held = {}, {}, {}
     for number, chunk in enumerate(chunks):
-        there = {k: [swap(piece, "expert", 1) for piece in here[k]] for k in chunk}
-        ordered = [side[k][j] for side in (here, there) for j in range(tensors) for k in chunk]
+        ordered = [here[k][j] for j in range(tensors) for k in chunk]
+        ordered += [swap(here[k][0], "expert", 1) for k in chunk]
+        if len(chunk) > 1:
+            ordered += [swap(pair, "expert", 1) for pair in stacked]
+        else:
+            ordered += [swap(piece, "expert", 1) for piece in here[chunk[0]][1:]]
         after = [arrived[3]] if relayed and number == 0 else []
         near, *far = expert_chunk(me, ordered, w_in, w_out, experts, after, relayed and number == 2)
         last = []
         if relayed and number == 0:
-            arrived[2], *pieces = gate([arrived[2], *here[3][1:], *here[1][1:]], [near])
-            here[3][1:], here[1][1:] = pieces[: tensors - 1], pieces[tensors - 1 :]
+            stacked = []
+            for j in range(1, tensors):
+                pair, arrived[2] = stack(here[1][j], here[3][j], arrived[2], [near])
+                stacked.append(pair)
             here[2] = across(2)
         elif relayed and number == 1:
             both = gate([*far, *here[2][1:]], [])

time: 77.2 us -> 78.9 us (1.022)
  waiting for transfers between devices: 18.5 us -> 21.6 us
  starting transfers between devices: 21.1 us -> 20 us
    ppermute x26 -> x25, waiting for transfers between devices: 18.5 us -> 21.6 us  [swap(): return lax.ppermute(values, axis, pairs)]
    ppermute x26 -> x25, starting transfers between devices: 21.1 us -> 20 us  [swap(): return lax.ppermute(values, axis, pairs)]
  transfers between devices with their start and end apart: 26 -> 25, of which waited for: 13 -> 13; matrix products, arithmetic and copies ran while one was open for 0% -> 0% of each run, Pallas kernels for 38% -> 37%
where the time goes in v4:
time: 78.9 us; the launch traced here: 78.7 us
  Pallas kernels  36.7 us (47%)
  waiting for transfers between devices  21.6 us (27%)
  starting transfers between devices  20 us (25%)
    ppermute x25, waiting for transfers between devices, swap(): return lax.ppermute(values, axis, pairs)  21.6 us
    ppermute x25, starting transfers between devices, swap(): return lax.ppermute(values, axis, pairs)  20 us
    pallas_call x3, Pallas kernels, expert_chunk(): pl.pallas_call(functools.partial(expert_kernel, experts, len(tokens), inp...  19.2 us
    pallas_call x2, Pallas kernels, load(): pl.pallas_call(load_kernel, in_specs=[pl.BlockSpec(memory_space=pltpu.HBM...  9.25 us
    pallas_call x1, Pallas kernels, project(): pl.pallas_call(functools.partial(project_kernel, tile), in_specs=[pl.Bloc...  6.66 us
  transfers between devices with their start and end apart: 25, of which 13 were waited for; matrix products, arithmetic and copies ran while one was open for 0% of the time, Pallas kernels for 37%

profile of v4, /device:TPU:0, one launch (start us, length us, event | category | flops | bytes accessed | tf_op | source)
XLA Modules:
  0.0 78.7 jit_solution(17771576230308562191)
XLA Ops:
  0.0 6.7 %project.1 = (bf16[32,2880]{1,0:T(8,128)(2,1)S(1)}, bf16[32,2880]{1,0:T(8,128)(2,1)S(1)}) custom-call(s32[1]{0:T(128)} %bitcast.1.tensor_ref, bf16[64,2048]{1,0:T(8,128)(2,1)} %heads_hbm.1, bf16[2880,2048]{1,0:T(8,128)(2,1)} %bitcast.8), custom_call_target="tpu_custom_call" | custom-call | tf_op jit(solution)/shard_map/project/pallas_call | solution.py:51
  6.7 3.0 %collective-permute-start = (bf16[32,2880]{1,0:T(8,128)(2,1)S(1)}, bf16[32,2880]{1,0:T(8,128)(2,1)S(1)}, u32[]{:S(2)}, u32[]{:S(2)}) collective-permute-start(bf16[32,2880]{1,0:T(8,128)(2,1)S(1)} %get-tuple-element.30.refs_0_), channel_id=1, source_target_pairs={{0,1},{1,0},{2,3},{3,2},{4,5},{5,4},{6,7},{7,6},{8,9},{9,8},{10,11... | collective-permute-start | bytes 552968 | tf_op jit(solution)/shard_map/ppermute | solution.py:279
  9.7 0.1 copy.10.refs_2_.refs_3_
  9.8 0.1 copy.11.refs_3_.refs_4_
  9.9 5.8 %load.2 = (bf16[2,1440,2880]{2,1,0:T(8,128)(2,1)S(1)}, f32[8,128]{1,0:T(8,128)S(1)}) custom-call(bf16[2,1440,2880]{2,1,0:T(8,128)(2,1)} %bitcast.7, bf16[32,2880]{1,0:T(8,128)(2,1)S(1)} %get-tuple-element.30.refs_0_, f32[1,2880]{1,0:T(1,128)S(1)} %reshape.11.refs_1_.refs_2_, s32[32,4]{1,0:T(8,128)S(1)} %copy.10.refs_2_.refs_3_, ...), custom_call_target="tpu_custom_call" | custom-call | bytes 16588800 | tf_op jit(solution)/shard_map/load/pallas_call | solution.py:160
  15.8 0.3 norm.1.refs_0_
  16.0 0.4 collective-permute-start.1
  16.4 1.7 %collective-permute-start.6 = (bf16[32,2944]{1,0:T(8,128)(2,1)S(1)}, bf16[32,2944]{1,0:T(8,128)(2,1)S(1)}, u32[]{:S(2)}, u32[]{:S(2)}) collective-permute-start(bf16[32,2944]{1,0:T(8,128)(2,1)S(1)} %norm.1.refs_0_), channel_id=1, source_target_pairs={{0,4},{2,6},{4,0},{6,2},{8,12},{10,14},{12,8},{14,10},{1,5},{3,7},... | collective-permute-start | bytes 565256 | tf_op jit(solution)/shard_map/ppermute | solution.py:279
  18.1 2.5 %collective-permute-start.4 = (bf16[32,2944]{1,0:T(8,128)(2,1)S(1)}, bf16[32,2944]{1,0:T(8,128)(2,1)S(1)}, u32[]{:S(2)}, u32[]{:S(2)}) collective-permute-start(bf16[32,2944]{1,0:T(8,128)(2,1)S(1)} %norm.1.refs_0_), channel_id=1, source_target_pairs={{0,12},{2,14},{4,8},{6,10},{8,4},{10,6},{12,0},{14,2},{1,13},{3,15... | collective-permute-start | bytes 565256 | tf_op jit(solution)/shard_map/ppermute | solution.py:279
  20.6 1.6 %collective-permute-done.1.refs_1_ = bf16[32,2944]{1,0:T(8,128)(2,1)S(1)} collective-permute-done((bf16[32,2944]{1,0:T(8,128)(2,1)S(1)}, bf16[32,2944]{1,0:T(8,128)(2,1)S(1)}, u32[]{:S(2)}, u32[]{:S(2)}) %collective-permute-start.1) | collective-permute-done | bytes 188448 | tf_op jit(solution)/shard_map/ppermute | solution.py:279
  22.2 3.4 %load.3 = (bf16[1440,2880]{1,0:T(8,128)(2,1)S(1)}, f32[8,128]{1,0:T(8,128)S(1)}) custom-call(bf16[1440,2880]{1,0:T(8,128)(2,1)} %bitcast.9, bf16[32,2944]{1,0:T(8,128)(2,1)S(1)} %norm.1.refs_0_), custom_call_target="tpu_custom_call" | custom-call | bytes 8294400 | tf_op jit(solution)/shard_map/load/pallas_call | solution.py:160
  25.7 0.5 collective-permute-start.7
  26.2 2.5 %collective-permute-done.4.refs_6_.refs_1_ = bf16[32,2944]{1,0:T(8,128)(2,1)S(1)} collective-permute-done((bf16[32,2944]{1,0:T(8,128)(2,1)S(1)}, bf16[32,2944]{1,0:T(8,128)(2,1)S(1)}, u32[]{:S(2)}, u32[]{:S(2)}) %collective-permute-start.4) | collective-permute-done | bytes 188448 | tf_op jit(solution)/shard_map/ppermute | solution.py:279
  28.6 1.5 %collective-permute-start.8 = (bf16[32,2944]{1,0:T(8,128)(2,1)S(1)}, bf16[32,2944]{1,0:T(8,128)(2,1)S(1)}, u32[]{:S(2)}, u32[]{:S(2)}) collective-permute-start(bf16[32,2944]{1,0:T(8,128)(2,1)S(1)} %collective-permute-done.4.refs_6_.refs_1_), channel_id=1, source_target_pairs={{0,1},{1,0},{2,3},{3,2},{4,5},{5,4},{6,7},{7,6},{8,9},{9,8},{10,11... | collective-permute-start | bytes 565256 | tf_op jit(solution)/shard_map/ppermute | solution.py:279
  30.1 0.6 collective-permute-start.9
  30.7 5.9 %expert.3 = (bf16[2,32,2880]{2,1,0:T(8,128)(2,1)S(1)}, bf16[2,32,2880]{2,1,0:T(8,128)(2,1)S(1)}) custom-call(s32[1]{0:T(128)} %bitcast.refs_4_.expert_ref, bf16[32,2944]{1,0:T(8,128)(2,1)S(1)} %norm.1.refs_0_, bf16[32,2944]{1,0:T(8,128)(2,1)S(1)} %collective-permute-done.1.refs_1_, bf16[32,2944]{1,0:T(8,128)(2,1)S(1)} %collective-permute-done.2.refs_2_, ...), custom_call_target="tpu_custom_call" | custom-call | flops 3185049600 | bytes 368640 | tf_op jit(solution)/shard_map/expert/pallas_call | solution.py:129
  36.6 0.3 collective-permute-done.8.second_ref.refs_3_
  37.1 0.5 collective-permute-start.10
  37.5 0.1 collective-permute-start.11
  37.6 0.3 collective-permute-start.13
  38.0 1.1 %collective-permute-done.10.refs_4_ = bf16[32,2944]{1,0:T(8,128)(2,1)S(1)} collective-permute-done((bf16[32,2944]{1,0:T(8,128)(2,1)S(1)}, bf16[32,2944]{1,0:T(8,128)(2,1)S(1)}, u32[]{:S(2)}, u32[]{:S(2)}) %collective-permute-start.10) | collective-permute-done | bytes 188448 | tf_op jit(solution)/shard_map/ppermute | solution.py:279
  39.0 0.3 collective-permute-done.11.refs_5_
  39.3 7.2 %expert.4 = (bf16[4,32,2880]{2,1,0:T(8,128)(2,1)S(1)}, bf16[4,32,2880]{2,1,0:T(8,128)(2,1)S(1)}) custom-call(s32[1]{0:T(128)} %bitcast.refs_4_.expert_ref, bf16[32,2944]{1,0:T(8,128)(2,1)S(1)} %gate.3.refs_0_, bf16[32,2944]{1,0:T(8,128)(2,1)S(1)} %collective-permute-done.4.refs_6_.refs_1_, bf16[32,2944]{1,0:T(8,128)(2,1)S(1)} %collective-permute-done.7.first_ref.refs_2_, ...), custom_call_target="tpu_custom_call" | custom-call | flops 6370099200 | bytes 737280 | tf_op jit(solution)/shard_map/expert/pallas_call | solution.py:129
  46.6 0.2 collective-permute-start.18
  46.8 0.4 collective-permute-start.14
  47.2 0.2 collective-permute-start.15
  47.3 1.6 %collective-permute-done.18.refs_0_ = bf16[4,32,2880]{2,1,0:T(8,128)(2,1)S(1)} collective-permute-done((bf16[4,32,2880]{2,1,0:T(8,128)(2,1)S(1)}, bf16[4,32,2880]{2,1,0:T(8,128)(2,1)S(1)}, u32[]{:S(2)}, u32[]{:S(2)}) %collective-permute-start.18) | collective-permute-done | bytes 737312 | tf_op jit(solution)/shard_map/ppermute | solution.py:279
  48.9 0.2 add_split.4
  49.1 0.5 collective-permute-start.19
  49.6 6.0 %expert.5 = (bf16[2,32,2880]{2,1,0:T(8,128)(2,1)S(1)}, bf16[32,2880]{1,0:T(8,128)(2,1)S(1)}, bf16[32,2880]{1,0:T(8,128)(2,1)S(1)}) custom-call(s32[1]{0:T(128)} %bitcast.refs_4_.expert_ref, bf16[32,2944]{1,0:T(8,128)(2,1)S(1)} %get-tuple-element.39.refs_0_, bf16[32,2944]{1,0:T(8,128)(2,1)S(1)} %get-tuple-element.42.refs_1_, ...), custom_call_target="tpu_custom_call" | custom-call | flops 3185049600 | bytes 368640 | tf_op jit(solution)/shard_map/expert/pallas_call | solution.py:129
  55.6 0.1 collective-permute-start.16
  55.7 0.5 collective-permute-start.17
  56.2 0.1 collective-permute-start.5
  56.3 0.8 %collective-permute-done.16.refs_0_ = bf16[32,2880]{1,0:T(8,128)(2,1)S(1)} collective-permute-done((bf16[32,2880]{1,0:T(8,128)(2,1)S(1)}, bf16[32,2880]{1,0:T(8,128)(2,1)S(1)}, u32[]{:S(2)}, u32[]{:S(2)}) %collective-permute-start.16) | collective-permute-done | bytes 184352 | tf_op jit(solution)/shard_map/ppermute | solution.py:279
  57.1 0.3 collective-permute-done.17.refs_1_
  57.4 2.6 %collective-permute-done.19.refs_2_.refs_1_ = bf16[2,32,2880]{2,1,0:T(8,128)(2,1)S(1)} collective-permute-done((bf16[2,32,2880]{2,1,0:T(8,128)(2,1)S(1)}, bf16[2,32,2880]{2,1,0:T(8,128)(2,1)S(1)}, u32[]{:S(2)}, u32[]{:S(2)}) %collective-permute-start.19) | collective-permute-done | bytes 368672 | tf_op jit(solution)/shard_map/ppermute | solution.py:279
  60.0 0.1 add_split.5
  60.1 0.5 collective-permute-start.20
  60.6 1.7 %collective-permute-start.22 = (bf16[32,2880]{1,0:T(8,128)(2,1)S(1)}, bf16[32,2880]{1,0:T(8,128)(2,1)S(1)}, u32[]{:S(2)}, u32[]{:S(2)}) collective-permute-start(bf16[32,2880]{1,0:T(8,128)(2,1)S(1)} %add_up.4), channel_id=1, source_target_pairs={{0,4},{2,6},{4,0},{6,2},{8,12},{10,14},{12,8},{14,10},{1,5},{3,7},... | collective-permute-start | bytes 552968 | tf_op jit(solution)/shard_map/ppermute | solution.py:279
  62.3 0.1 add_split.3
  62.4 3.7 %collective-permute-done.20.refs_1_ = bf16[32,2880]{1,0:T(8,128)(2,1)S(1)} collective-permute-done((bf16[32,2880]{1,0:T(8,128)(2,1)S(1)}, bf16[32,2880]{1,0:T(8,128)(2,1)S(1)}, u32[]{:S(2)}, u32[]{:S(2)}) %collective-permute-start.20) | collective-permute-done | bytes 184352 | tf_op jit(solution)/shard_map/ppermute | solution.py:279
  66.1 0.5 collective-permute-start.21
  66.7 1.7 %collective-permute-start.23 = (bf16[32,2880]{1,0:T(8,128)(2,1)S(1)}, bf16[32,2880]{1,0:T(8,128)(2,1)S(1)}, u32[]{:S(2)}, u32[]{:S(2)}) collective-permute-start(bf16[32,2880]{1,0:T(8,128)(2,1)S(1)} %add_up.5), channel_id=1, source_target_pairs={{0,4},{2,6},{4,0},{6,2},{8,12},{10,14},{12,8},{14,10},{1,5},{3,7},... | collective-permute-start | bytes 552968 | tf_op jit(solution)/shard_map/ppermute | solution.py:279
  68.4 2.7 %collective-permute-start.24 = (bf16[32,2880]{1,0:T(8,128)(2,1)S(1)}, bf16[32,2880]{1,0:T(8,128)(2,1)S(1)}, u32[]{:S(2)}, u32[]{:S(2)}) collective-permute-start(bf16[32,2880]{1,0:T(8,128)(2,1)S(1)} %add_up.6), channel_id=1, source_target_pairs={{0,8},{2,10},{4,12},{6,14},{8,0},{10,2},{12,4},{14,6},{1,9},{3,11}... | collective-permute-start | bytes 552968 | tf_op jit(solution)/shard_map/ppermute | solution.py:279
  71.1 0.7 collective-permute-done.21.refs_1_
  71.8 3.0 %collective-permute-done.23.refs_2_ = bf16[32,2880]{1,0:T(8,128)(2,1)S(1)} collective-permute-done((bf16[32,2880]{1,0:T(8,128)(2,1)S(1)}, bf16[32,2880]{1,0:T(8,128)(2,1)S(1)}, u32[]{:S(2)}, u32[]{:S(2)}) %collective-permute-start.23) | collective-permute-done | bytes 184352 | tf_op jit(solution)/shard_map/ppermute | solution.py:279
  74.8 3.2 %collective-permute-done.24.refs_3_ = bf16[32,2880]{1,0:T(8,128)(2,1)S(1)} collective-permute-done((bf16[32,2880]{1,0:T(8,128)(2,1)S(1)}, bf16[32,2880]{1,0:T(8,128)(2,1)S(1)}, u32[]{:S(2)}, u32[]{:S(2)}) %collective-permute-start.24) | collective-permute-done | bytes 184352 | tf_op jit(solution)/shard_map/ppermute | solution.py:279
  77.9 0.8 add_up.7
  (29 shorter events, 0.4 us)
Async XLA Ops:
  0.0 9.7 %copy-start = (f32[2880]{0:T(1024)S(1)}, f32[2880]{0:T(1024)}, u32[]{:S(2)}) copy-start(f32[2880]{0:T(1024)} %param.9) | copy-start | bytes 34564
  0.0 9.7 %copy-start.1 = (s32[32,4]{0,1:T(4,128)S(1)}, s32[32,4]{0,1:T(4,128)}, u32[]{:S(2)}) copy-start(s32[32,4]{0,1:T(4,128)} %param.12) | copy-start | bytes 1540
  0.0 9.8 %copy-start.2 = (f32[32,4]{0,1:T(4,128)S(1)}, f32[32,4]{0,1:T(4,128)}, u32[]{:S(2)}) copy-start(f32[32,4]{0,1:T(4,128)} %param.13) | copy-start | bytes 1540
  6.7 9.1 %collective-permute-start = (bf16[32,2880]{1,0:T(8,128)(2,1)S(1)}, bf16[32,2880]{1,0:T(8,128)(2,1)S(1)}, u32[]{:S(2)}, u32[]{:S(2)}) collective-permute-start(bf16[32,2880]{1,0:T(8,128)(2,1)S(1)} %get-tuple-element.30.refs_0_), channel_id=1, source_target_pairs={{0,1},{1,0},{2,3},{3,2},{4,5},{5,4},{6,7},{7,6},{8,9},{9,8},{10,11... | collective-permute-start | bytes 552968 | tf_op jit(solution)/shard_map/ppermute | solution.py:279
  16.0 6.2 %collective-permute-start.1 = (bf16[32,2944]{1,0:T(8,128)(2,1)S(1)}, bf16[32,2944]{1,0:T(8,128)(2,1)S(1)}, u32[]{:S(2)}, u32[]{:S(2)}) collective-permute-start(bf16[32,2944]{1,0:T(8,128)(2,1)S(1)} %norm.1.refs_0_), channel_id=1, source_target_pairs={{0,1},{1,0},{2,3},{3,2},{4,5},{5,4},{6,7},{7,6},{8,9},{9,8},{10,11... | collective-permute-start | bytes 565256 | tf_op jit(solution)/shard_map/ppermute | solution.py:279
  16.4 9.2 %collective-permute-start.6 = (bf16[32,2944]{1,0:T(8,128)(2,1)S(1)}, bf16[32,2944]{1,0:T(8,128)(2,1)S(1)}, u32[]{:S(2)}, u32[]{:S(2)}) collective-permute-start(bf16[32,2944]{1,0:T(8,128)(2,1)S(1)} %norm.1.refs_0_), channel_id=1, source_target_pairs={{0,4},{2,6},{4,0},{6,2},{8,12},{10,14},{12,8},{14,10},{1,5},{3,7},... | collective-permute-start | bytes 565256 | tf_op jit(solution)/shard_map/ppermute | solution.py:279
  18.1 10.5 %collective-permute-start.4 = (bf16[32,2944]{1,0:T(8,128)(2,1)S(1)}, bf16[32,2944]{1,0:T(8,128)(2,1)S(1)}, u32[]{:S(2)}, u32[]{:S(2)}) collective-permute-start(bf16[32,2944]{1,0:T(8,128)(2,1)S(1)} %norm.1.refs_0_), channel_id=1, source_target_pairs={{0,12},{2,14},{4,8},{6,10},{8,4},{10,6},{12,0},{14,2},{1,13},{3,15... | collective-permute-start | bytes 565256 | tf_op jit(solution)/shard_map/ppermute | solution.py:279
  20.6 10.1 %collective-permute-start.2 = (bf16[32,2944]{1,0:T(8,128)(2,1)S(1)}, bf16[32,2944]{1,0:T(8,128)(2,1)S(1)}, u32[]{:S(2)}, u32[]{:S(2)}) collective-permute-start(bf16[32,2944]{1,0:T(8,128)(2,1)S(1)} %norm.1.refs_0_), channel_id=1, source_target_pairs={{0,2},{2,0},{4,6},{6,4},{8,10},{10,8},{12,14},{14,12},{1,3},{3,1},... | collective-permute-start | bytes 565256 | tf_op jit(solution)/shard_map/ppermute | solution.py:279
  22.2 8.5 %collective-permute-start.3 = (bf16[32,2944]{1,0:T(8,128)(2,1)S(1)}, bf16[32,2944]{1,0:T(8,128)(2,1)S(1)}, u32[]{:S(2)}, u32[]{:S(2)}) collective-permute-start(bf16[32,2944]{1,0:T(8,128)(2,1)S(1)} %collective-permute-done.1.refs_1_), channel_id=1, source_target_pairs={{0,2},{2,0},{4,6},{6,4},{8,10},{10,8},{12,14},{14,12},{1,3},{3,1},... | collective-permute-start | bytes 565256 | tf_op jit(solution)/shard_map/ppermute | solution.py:279
  25.7 10.9 %collective-permute-start.7 = (bf16[32,2944]{1,0:T(8,128)(2,1)S(1)}, bf16[32,2944]{1,0:T(8,128)(2,1)S(1)}, u32[]{:S(2)}, u32[]{:S(2)}) collective-permute-start(bf16[32,2944]{1,0:T(8,128)(2,1)S(1)} %gate.3.refs_0_), channel_id=1, source_target_pairs={{0,1},{1,0},{2,3},{3,2},{4,5},{5,4},{6,7},{7,6},{8,9},{9,8},{10,11... | collective-permute-start | bytes 565256 | tf_op jit(solution)/shard_map/ppermute | solution.py:279
  28.6 8.3 %collective-permute-start.8 = (bf16[32,2944]{1,0:T(8,128)(2,1)S(1)}, bf16[32,2944]{1,0:T(8,128)(2,1)S(1)}, u32[]{:S(2)}, u32[]{:S(2)}) collective-permute-start(bf16[32,2944]{1,0:T(8,128)(2,1)S(1)} %collective-permute-done.4.refs_6_.refs_1_), channel_id=1, source_target_pairs={{0,1},{1,0},{2,3},{3,2},{4,5},{5,4},{6,7},{7,6},{8,9},{9,8},{10,11... | collective-permute-start | bytes 565256 | tf_op jit(solution)/shard_map/ppermute | solution.py:279
  30.1 6.8 %collective-permute-start.9 = (bf16[32,2944]{1,0:T(8,128)(2,1)S(1)}, bf16[32,2944]{1,0:T(8,128)(2,1)S(1)}, u32[]{:S(2)}, u32[]{:S(2)}) collective-permute-start(bf16[32,2944]{1,0:T(8,128)(2,1)S(1)} %collective-permute-done.4.refs_6_.refs_1_), channel_id=1, source_target_pairs={{0,4},{2,6},{4,0},{6,2},{8,12},{10,14},{12,8},{14,10},{1,5},{3,7},... | collective-permute-start | bytes 565256 | tf_op jit(solution)/shard_map/ppermute | solution.py:279
  37.0 2.3 %collective-permute-start.12 = (bf16[2,32,2944]{2,1,0:T(8,128)(2,1)S(1)}, bf16[2,32,2944]{2,1,0:T(8,128)(2,1)S(1)}, u32[]{:S(2)}, u32[]{:S(2)}) collective-permute-start(bf16[2,32,2944]{2,1,0:T(8,128)(2,1)S(1)} %get-tuple-element.40), channel_id=1, source_target_pairs={{0,2},{2,0},{4,6},{6,4},{8,10},{10,8},{12,14},{14,12},{1,3},{3,1},... | collective-permute-start | bytes 1130504 | tf_op jit(solution)/shard_map/ppermute | solution.py:279
  37.1 2.0 %collective-permute-start.10 = (bf16[32,2944]{1,0:T(8,128)(2,1)S(1)}, bf16[32,2944]{1,0:T(8,128)(2,1)S(1)}, u32[]{:S(2)}, u32[]{:S(2)}) collective-permute-start(bf16[32,2944]{1,0:T(8,128)(2,1)S(1)} %gate.3.refs_0_), channel_id=1, source_target_pairs={{0,2},{2,0},{4,6},{6,4},{8,10},{10,8},{12,14},{14,12},{1,3},{3,1},... | collective-permute-start | bytes 565256 | tf_op jit(solution)/shard_map/ppermute | solution.py:279
  37.5 1.7 %collective-permute-start.11 = (bf16[32,2944]{1,0:T(8,128)(2,1)S(1)}, bf16[32,2944]{1,0:T(8,128)(2,1)S(1)}, u32[]{:S(2)}, u32[]{:S(2)}) collective-permute-start(bf16[32,2944]{1,0:T(8,128)(2,1)S(1)} %collective-permute-done.4.refs_6_.refs_1_), channel_id=1, source_target_pairs={{0,2},{2,0},{4,6},{6,4},{8,10},{10,8},{12,14},{14,12},{1,3},{3,1},... | collective-permute-start | bytes 565256 | tf_op jit(solution)/shard_map/ppermute | solution.py:279
  37.6 8.9 %collective-permute-start.13 = (bf16[32,2944]{1,0:T(8,128)(2,1)S(1)}, bf16[32,2944]{1,0:T(8,128)(2,1)S(1)}, u32[]{:S(2)}, u32[]{:S(2)}) collective-permute-start(bf16[32,2944]{1,0:T(8,128)(2,1)S(1)} %get-tuple-element.39.refs_0_), channel_id=1, source_target_pairs={{0,1},{1,0},{2,3},{3,2},{4,5},{5,4},{6,7},{7,6},{8,9},{9,8},{10,11... | collective-permute-start | bytes 565256 | tf_op jit(solution)/shard_map/ppermute | solution.py:279
  46.6 2.3 %collective-permute-start.18 = (bf16[4,32,2880]{2,1,0:T(8,128)(2,1)S(1)}, bf16[4,32,2880]{2,1,0:T(8,128)(2,1)S(1)}, u32[]{:S(2)}, u32[]{:S(2)}) collective-permute-start(bf16[4,32,2880]{2,1,0:T(8,128)(2,1)S(1)} %get-tuple-element.47), channel_id=1, source_target_pairs={{0,2},{2,0},{4,6},{6,4},{8,10},{10,8},{12,14},{14,12},{1,3},{3,1},... | collective-permute-start | bytes 2211848 | tf_op jit(solution)/shard_map/ppermute | solution.py:279
  46.8 2.7 %collective-permute-start.14 = (bf16[32,2944]{1,0:T(8,128)(2,1)S(1)}, bf16[32,2944]{1,0:T(8,128)(2,1)S(1)}, u32[]{:S(2)}, u32[]{:S(2)}) collective-permute-start(bf16[32,2944]{1,0:T(8,128)(2,1)S(1)} %get-tuple-element.39.refs_0_), channel_id=1, source_target_pairs={{0,2},{2,0},{4,6},{6,4},{8,10},{10,8},{12,14},{14,12},{1,3},{3,1},... | collective-permute-start | bytes 565256 | tf_op jit(solution)/shard_map/ppermute | solution.py:279
  47.2 2.4 %collective-permute-start.15 = (bf16[32,2944]{1,0:T(8,128)(2,1)S(1)}, bf16[32,2944]{1,0:T(8,128)(2,1)S(1)}, u32[]{:S(2)}, u32[]{:S(2)}) collective-permute-start(bf16[32,2944]{1,0:T(8,128)(2,1)S(1)} %get-tuple-element.42.refs_1_), channel_id=1, source_target_pairs={{0,2},{2,0},{4,6},{6,4},{8,10},{10,8},{12,14},{14,12},{1,3},{3,1},... | collective-permute-start | bytes 565256 | tf_op jit(solution)/shard_map/ppermute | solution.py:279
  49.1 10.9 %collective-permute-start.19 = (bf16[2,32,2880]{2,1,0:T(8,128)(2,1)S(1)}, bf16[2,32,2880]{2,1,0:T(8,128)(2,1)S(1)}, u32[]{:S(2)}, u32[]{:S(2)}) collective-permute-start(bf16[2,32,2880]{2,1,0:T(8,128)(2,1)S(1)} %get-tuple-element.48), channel_id=1, source_target_pairs={{0,1},{1,0},{2,3},{3,2},{4,5},{5,4},{6,7},{7,6},{8,9},{9,8},{10,11... | collective-permute-start | bytes 1105928 | tf_op jit(solution)/shard_map/ppermute | solution.py:279
  55.6 1.5 %collective-permute-start.16 = (bf16[32,2880]{1,0:T(8,128)(2,1)S(1)}, bf16[32,2880]{1,0:T(8,128)(2,1)S(1)}, u32[]{:S(2)}, u32[]{:S(2)}) collective-permute-start(bf16[32,2880]{1,0:T(8,128)(2,1)S(1)} %get-tuple-element.44), channel_id=1, source_target_pairs={{0,2},{2,0},{4,6},{6,4},{8,10},{10,8},{12,14},{14,12},{1,3},{3,1},... | collective-permute-start | bytes 552968 | tf_op jit(solution)/shard_map/ppermute | solution.py:279
  55.7 1.7 %collective-permute-start.17 = (bf16[32,2880]{1,0:T(8,128)(2,1)S(1)}, bf16[32,2880]{1,0:T(8,128)(2,1)S(1)}, u32[]{:S(2)}, u32[]{:S(2)}) collective-permute-start(bf16[32,2880]{1,0:T(8,128)(2,1)S(1)} %get-tuple-element.45), channel_id=1, source_target_pairs={{0,2},{2,0},{4,6},{6,4},{8,10},{10,8},{12,14},{14,12},{1,3},{3,1},... | collective-permute-start | bytes 552968 | tf_op jit(solution)/shard_map/ppermute | solution.py:279
  56.2 6.1 %collective-permute-start.5 = (bf16[2,32,2880]{2,1,0:T(8,128)(2,1)S(1)}, bf16[2,32,2880]{2,1,0:T(8,128)(2,1)S(1)}, u32[]{:S(2)}, u32[]{:S(2)}) collective-permute-start(bf16[2,32,2880]{2,1,0:T(8,128)(2,1)S(1)} %get-tuple-element.35), channel_id=1, source_target_pairs={{0,2},{2,0},{4,6},{6,4},{8,10},{10,8},{12,14},{14,12},{1,3},{3,1},... | collective-permute-start | bytes 1105928 | tf_op jit(solution)/shard_map/ppermute | solution.py:279
  60.1 6.0 %collective-permute-start.20 = (bf16[32,2880]{1,0:T(8,128)(2,1)S(1)}, bf16[32,2880]{1,0:T(8,128)(2,1)S(1)}, u32[]{:S(2)}, u32[]{:S(2)}) collective-permute-start(bf16[32,2880]{1,0:T(8,128)(2,1)S(1)} %get-tuple-element.49), channel_id=1, source_target_pairs={{0,1},{1,0},{2,3},{3,2},{4,5},{5,4},{6,7},{7,6},{8,9},{9,8},{10,11... | collective-permute-start | bytes 552968 | tf_op jit(solution)/shard_map/ppermute | solution.py:279
  60.6 6.0 %collective-permute-start.22 = (bf16[32,2880]{1,0:T(8,128)(2,1)S(1)}, bf16[32,2880]{1,0:T(8,128)(2,1)S(1)}, u32[]{:S(2)}, u32[]{:S(2)}) collective-permute-start(bf16[32,2880]{1,0:T(8,128)(2,1)S(1)} %add_up.4), channel_id=1, source_target_pairs={{0,4},{2,6},{4,0},{6,2},{8,12},{10,14},{12,8},{14,10},{1,5},{3,7},... | collective-permute-start | bytes 552968 | tf_op jit(solution)/shard_map/ppermute | solution.py:279
  66.1 5.6 %collective-permute-start.21 = (bf16[32,2880]{1,0:T(8,128)(2,1)S(1)}, bf16[32,2880]{1,0:T(8,128)(2,1)S(1)}, u32[]{:S(2)}, u32[]{:S(2)}) collective-permute-start(bf16[32,2880]{1,0:T(8,128)(2,1)S(1)} %gate.5), channel_id=1, source_target_pairs={{0,1},{1,0},{2,3},{3,2},{4,5},{5,4},{6,7},{7,6},{8,9},{9,8},{10,11... | collective-permute-start | bytes 552968 | tf_op jit(solution)/shard_map/ppermute | solution.py:279
  66.7 8.1 %collective-permute-start.23 = (bf16[32,2880]{1,0:T(8,128)(2,1)S(1)}, bf16[32,2880]{1,0:T(8,128)(2,1)S(1)}, u32[]{:S(2)}, u32[]{:S(2)}) collective-permute-start(bf16[32,2880]{1,0:T(8,128)(2,1)S(1)} %add_up.5), channel_id=1, source_target_pairs={{0,4},{2,6},{4,0},{6,2},{8,12},{10,14},{12,8},{14,10},{1,5},{3,7},... | collective-permute-start | bytes 552968 | tf_op jit(solution)/shard_map/ppermute | solution.py:279
  68.4 9.5 %collective-permute-start.24 = (bf16[32,2880]{1,0:T(8,128)(2,1)S(1)}, bf16[32,2880]{1,0:T(8,128)(2,1)S(1)}, u32[]{:S(2)}, u32[]{:S(2)}) collective-permute-start(bf16[32,2880]{1,0:T(8,128)(2,1)S(1)} %add_up.6), channel_id=1, source_target_pairs={{0,8},{2,10},{4,12},{6,14},{8,0},{10,2},{12,4},{14,6},{1,9},{3,11}... | collective-permute-start | bytes 552968 | tf_op jit(solution)/shard_map/ppermute | solution.py:279

commit v5 on v3

--- a/solution.py
+++ b/solution.py
@@ -34,7 +34,9 @@
         copies[i].wait()
         if i + AHEAD < len(tiles):
             copies[i + AHEAD].start()
-        out = lax.dot_general(heads, w_ref[start : start + size], NT, preferred_element_type=F32)
+        half = depth // 2
+        out = lax.dot_general(heads[:, :half], w_ref[start : start + size, :half], NT, preferred_element_type=F32)
+        out = out + lax.dot_general(heads[:, half:], w_ref[start : start + size, half:], NT, preferred_element_type=F32)
         out_ref[:, start : start + size] = out.astype(BF16)
     tokens = part_refs[0].shape[0]
     for j, part_ref in enumerate(part_refs):

time: 77.2 us -> 77.2 us (level)
  no operation moved by 1% of the time
where the time goes in v5:
time: 77.2 us; the launch traced here: 76.7 us
  Pallas kernels  36.8 us (48%)
  starting transfers between devices  21.1 us (27%)
  waiting for transfers between devices  18.5 us (24%)
    ppermute x26, starting transfers between devices, swap(): return lax.ppermute(values, axis, pairs)  21.1 us
    pallas_call x3, Pallas kernels, expert_chunk(): pl.pallas_call(functools.partial(expert_kernel, experts, len(tokens), inp...  19.2 us
    ppermute x26, waiting for transfers between devices, swap(): return lax.ppermute(values, axis, pairs)  18.5 us
    pallas_call x2, Pallas kernels, load(): pl.pallas_call(load_kernel, in_specs=[pl.BlockSpec(memory_space=pltpu.HBM...  9.25 us
    pallas_call x1, Pallas kernels, project(): pl.pallas_call(functools.partial(project_kernel, tile), in_specs=[pl.Bloc...  6.66 us
  transfers between devices with their start and end apart: 26, of which 13 were waited for; matrix products, arithmetic and copies ran while one was open for 0% of the time, Pallas kernels for 38%

profile of v5, /device:TPU:0, one launch (start us, length us, event | category | flops | bytes accessed | tf_op | source)
XLA Modules:
  0.0 76.7 jit_solution(12211904472677689799)
XLA Ops:
  0.0 6.7 %project.1 = (bf16[32,2880]{1,0:T(8,128)(2,1)S(1)}, bf16[32,2880]{1,0:T(8,128)(2,1)S(1)}) custom-call(s32[1]{0:T(128)} %bitcast.1.tensor_ref, bf16[64,2048]{1,0:T(8,128)(2,1)} %heads_hbm.1, bf16[2880,2048]{1,0:T(8,128)(2,1)} %bitcast.8), custom_call_target="tpu_custom_call" | custom-call | tf_op jit(solution)/shard_map/project/pallas_call | solution.py:53
  6.7 3.0 %collective-permute-start = (bf16[32,2880]{1,0:T(8,128)(2,1)S(1)}, bf16[32,2880]{1,0:T(8,128)(2,1)S(1)}, u32[]{:S(2)}, u32[]{:S(2)}) collective-permute-start(bf16[32,2880]{1,0:T(8,128)(2,1)S(1)} %get-tuple-element.31.refs_0_), channel_id=1, source_target_pairs={{0,1},{1,0},{2,3},{3,2},{4,5},{5,4},{6,7},{7,6},{8,9},{9,8},{10,11... | collective-permute-start | bytes 552968 | tf_op jit(solution)/shard_map/ppermute | solution.py:259
  9.7 0.1 copy.10.refs_2_.refs_3_
  9.8 0.1 copy.11.refs_3_.refs_4_
  9.9 5.8 %load.2 = (bf16[2,1440,2880]{2,1,0:T(8,128)(2,1)S(1)}, f32[8,128]{1,0:T(8,128)S(1)}) custom-call(bf16[2,1440,2880]{2,1,0:T(8,128)(2,1)} %bitcast.7, bf16[32,2880]{1,0:T(8,128)(2,1)S(1)} %get-tuple-element.31.refs_0_, f32[1,2880]{1,0:T(1,128)S(1)} %reshape.11.refs_1_.refs_2_, s32[32,4]{1,0:T(8,128)S(1)} %copy.10.refs_2_.refs_3_, ...), custom_call_target="tpu_custom_call" | custom-call | bytes 16588800 | tf_op jit(solution)/shard_map/load/pallas_call | solution.py:162
  15.8 0.3 norm.1.refs_0_
  16.0 0.4 collective-permute-start.1
  16.4 1.7 %collective-permute-start.8 = (bf16[32,2944]{1,0:T(8,128)(2,1)S(1)}, bf16[32,2944]{1,0:T(8,128)(2,1)S(1)}, u32[]{:S(2)}, u32[]{:S(2)}) collective-permute-start(bf16[32,2944]{1,0:T(8,128)(2,1)S(1)} %norm.1.refs_0_), channel_id=1, source_target_pairs={{0,4},{2,6},{4,0},{6,2},{8,12},{10,14},{12,8},{14,10},{1,5},{3,7},... | collective-permute-start | bytes 565256 | tf_op jit(solution)/shard_map/ppermute | solution.py:259
  18.1 2.5 %collective-permute-start.4 = (bf16[32,2944]{1,0:T(8,128)(2,1)S(1)}, bf16[32,2944]{1,0:T(8,128)(2,1)S(1)}, u32[]{:S(2)}, u32[]{:S(2)}) collective-permute-start(bf16[32,2944]{1,0:T(8,128)(2,1)S(1)} %norm.1.refs_0_), channel_id=1, source_target_pairs={{0,12},{2,14},{4,8},{6,10},{8,4},{10,6},{12,0},{14,2},{1,13},{3,15... | collective-permute-start | bytes 565256 | tf_op jit(solution)/shard_map/ppermute | solution.py:259
  20.6 1.6 %collective-permute-done.1.refs_1_ = bf16[32,2944]{1,0:T(8,128)(2,1)S(1)} collective-permute-done((bf16[32,2944]{1,0:T(8,128)(2,1)S(1)}, bf16[32,2944]{1,0:T(8,128)(2,1)S(1)}, u32[]{:S(2)}, u32[]{:S(2)}) %collective-permute-start.1) | collective-permute-done | bytes 188448 | tf_op jit(solution)/shard_map/ppermute | solution.py:259
  22.2 3.4 %load.3 = (bf16[1440,2880]{1,0:T(8,128)(2,1)S(1)}, f32[8,128]{1,0:T(8,128)S(1)}) custom-call(bf16[1440,2880]{1,0:T(8,128)(2,1)} %bitcast.9, bf16[32,2944]{1,0:T(8,128)(2,1)S(1)} %norm.1.refs_0_), custom_call_target="tpu_custom_call" | custom-call | bytes 8294400 | tf_op jit(solution)/shard_map/load/pallas_call | solution.py:162
  25.7 0.5 collective-permute-start.9
  26.2 0.2 collective-permute-start.10
  26.3 2.3 %collective-permute-done.4.refs_6_.refs_1_ = bf16[32,2944]{1,0:T(8,128)(2,1)S(1)} collective-permute-done((bf16[32,2944]{1,0:T(8,128)(2,1)S(1)}, bf16[32,2944]{1,0:T(8,128)(2,1)S(1)}, u32[]{:S(2)}, u32[]{:S(2)}) %collective-permute-start.4) | collective-permute-done | bytes 188448 | tf_op jit(solution)/shard_map/ppermute | solution.py:259
  28.6 0.6 collective-permute-start.6
  29.2 1.5 %collective-permute-start.7 = (bf16[32,2944]{1,0:T(8,128)(2,1)S(1)}, bf16[32,2944]{1,0:T(8,128)(2,1)S(1)}, u32[]{:S(2)}, u32[]{:S(2)}) collective-permute-start(bf16[32,2944]{1,0:T(8,128)(2,1)S(1)} %collective-permute-done.4.refs_6_.refs_1_), channel_id=1, source_target_pairs={{0,1},{1,0},{2,3},{3,2},{4,5},{5,4},{6,7},{7,6},{8,9},{9,8},{10,11... | collective-permute-start | bytes 565256 | tf_op jit(solution)/shard_map/ppermute | solution.py:259
  30.7 5.9 %expert.3 = (bf16[2,32,2880]{2,1,0:T(8,128)(2,1)S(1)}, bf16[2,32,2880]{2,1,0:T(8,128)(2,1)S(1)}) custom-call(s32[1]{0:T(128)} %bitcast.refs_4_.expert_ref, bf16[32,2944]{1,0:T(8,128)(2,1)S(1)} %norm.1.refs_0_, bf16[32,2944]{1,0:T(8,128)(2,1)S(1)} %collective-permute-done.1.refs_1_, bf16[32,2944]{1,0:T(8,128)(2,1)S(1)} %collective-permute-done.2.refs_2_, ...), custom_call_target="tpu_custom_call" | custom-call | flops 3185049600 | bytes 368640 | tf_op jit(solution)/shard_map/expert/pallas_call | solution.py:131
  36.6 0.3 collective-permute-done.7.refs_1_
  37.0 0.3 collective-permute-start.12
  37.3 0.3 collective-permute-start.13
  37.5 0.3 collective-permute-start.14
  37.9 0.6 collective-permute-done.12.refs_6_
  38.5 0.3 collective-permute-done.13.refs_7_
  38.7 7.2 %expert.4 = (bf16[4,32,2880]{2,1,0:T(8,128)(2,1)S(1)}, bf16[4,32,2880]{2,1,0:T(8,128)(2,1)S(1)}) custom-call(s32[1]{0:T(128)} %bitcast.refs_4_.expert_ref, bf16[32,2944]{1,0:T(8,128)(2,1)S(1)} %gate.4.refs_0_, bf16[32,2944]{1,0:T(8,128)(2,1)S(1)} %collective-permute-done.4.refs_6_.refs_1_, bf16[32,2944]{1,0:T(8,128)(2,1)S(1)} %get-tuple-element.41.refs_2_, ...), custom_call_target="tpu_custom_call" | custom-call | flops 6370099200 | bytes 737280 | tf_op jit(solution)/shard_map/expert/pallas_call | solution.py:131
  46.1 0.3 collective-permute-start.19
  46.4 0.3 collective-permute-start.15
  46.7 0.2 collective-permute-start.16
  46.9 1.5 %collective-permute-done.19.refs_0_ = bf16[4,32,2880]{2,1,0:T(8,128)(2,1)S(1)} collective-permute-done((bf16[4,32,2880]{2,1,0:T(8,128)(2,1)S(1)}, bf16[4,32,2880]{2,1,0:T(8,128)(2,1)S(1)}, u32[]{:S(2)}, u32[]{:S(2)}) %collective-permute-start.19) | collective-permute-done | bytes 737312 | tf_op jit(solution)/shard_map/ppermute | solution.py:259
  48.4 0.2 add_split.4
  48.6 0.9 %collective-permute-start.20 = (bf16[2,32,2880]{2,1,0:T(8,128)(2,1)S(1)}, bf16[2,32,2880]{2,1,0:T(8,128)(2,1)S(1)}, u32[]{:S(2)}, u32[]{:S(2)}) collective-permute-start(bf16[2,32,2880]{2,1,0:T(8,128)(2,1)S(1)} %get-tuple-element.50), channel_id=1, source_target_pairs={{0,1},{1,0},{2,3},{3,2},{4,5},{5,4},{6,7},{7,6},{8,9},{9,8},{10,11... | collective-permute-start | bytes 1105928 | tf_op jit(solution)/shard_map/ppermute | solution.py:259
  49.5 6.1 %expert.5 = (bf16[2,32,2880]{2,1,0:T(8,128)(2,1)S(1)}, bf16[32,2880]{1,0:T(8,128)(2,1)S(1)}, bf16[32,2880]{1,0:T(8,128)(2,1)S(1)}) custom-call(s32[1]{0:T(128)} %bitcast.refs_4_.expert_ref, bf16[32,2944]{1,0:T(8,128)(2,1)S(1)} %get-tuple-element.40.refs_0_, bf16[32,2944]{1,0:T(8,128)(2,1)S(1)} %get-tuple-element.44.refs_1_, ...), custom_call_target="tpu_custom_call" | custom-call | flops 3185049600 | bytes 368640 | tf_op jit(solution)/shard_map/expert/pallas_call | solution.py:131
  55.7 0.5 collective-permute-start.18
  56.2 0.1 collective-permute-start.5
  56.2 0.8 %collective-permute-done.17.refs_0_ = bf16[32,2880]{1,0:T(8,128)(2,1)S(1)} collective-permute-done((bf16[32,2880]{1,0:T(8,128)(2,1)S(1)}, bf16[32,2880]{1,0:T(8,128)(2,1)S(1)}, u32[]{:S(2)}, u32[]{:S(2)}) %collective-permute-start.17) | collective-permute-done | bytes 184352 | tf_op jit(solution)/shard_map/ppermute | solution.py:259
  57.1 0.3 collective-permute-done.18.refs_1_
  57.4 2.2 %collective-permute-done.20.refs_2_.refs_1_ = bf16[2,32,2880]{2,1,0:T(8,128)(2,1)S(1)} collective-permute-done((bf16[2,32,2880]{2,1,0:T(8,128)(2,1)S(1)}, bf16[2,32,2880]{2,1,0:T(8,128)(2,1)S(1)}, u32[]{:S(2)}, u32[]{:S(2)}) %collective-permute-start.20) | collective-permute-done | bytes 368672 | tf_op jit(solution)/shard_map/ppermute | solution.py:259
  59.6 0.1 add_split.5
  59.6 0.8 %collective-permute-start.21 = (bf16[32,2880]{1,0:T(8,128)(2,1)S(1)}, bf16[32,2880]{1,0:T(8,128)(2,1)S(1)}, u32[]{:S(2)}, u32[]{:S(2)}) collective-permute-start(bf16[32,2880]{1,0:T(8,128)(2,1)S(1)} %get-tuple-element.51), channel_id=1, source_target_pairs={{0,1},{1,0},{2,3},{3,2},{4,5},{5,4},{6,7},{7,6},{8,9},{9,8},{10,11... | collective-permute-start | bytes 552968 | tf_op jit(solution)/shard_map/ppermute | solution.py:259
  60.5 1.6 %collective-permute-start.23 = (bf16[32,2880]{1,0:T(8,128)(2,1)S(1)}, bf16[32,2880]{1,0:T(8,128)(2,1)S(1)}, u32[]{:S(2)}, u32[]{:S(2)}) collective-permute-start(bf16[32,2880]{1,0:T(8,128)(2,1)S(1)} %add_up.4), channel_id=1, source_target_pairs={{0,4},{2,6},{4,0},{6,2},{8,12},{10,14},{12,8},{14,10},{1,5},{3,7},... | collective-permute-start | bytes 552968 | tf_op jit(solution)/shard_map/ppermute | solution.py:259
  62.2 0.1 add_split.3
  62.2 3.5 %collective-permute-done.21.refs_1_ = bf16[32,2880]{1,0:T(8,128)(2,1)S(1)} collective-permute-done((bf16[32,2880]{1,0:T(8,128)(2,1)S(1)}, bf16[32,2880]{1,0:T(8,128)(2,1)S(1)}, u32[]{:S(2)}, u32[]{:S(2)}) %collective-permute-start.21) | collective-permute-done | bytes 184352 | tf_op jit(solution)/shard_map/ppermute | solution.py:259
  65.8 0.7 collective-permute-start.22
  66.5 1.6 %collective-permute-start.24 = (bf16[32,2880]{1,0:T(8,128)(2,1)S(1)}, bf16[32,2880]{1,0:T(8,128)(2,1)S(1)}, u32[]{:S(2)}, u32[]{:S(2)}) collective-permute-start(bf16[32,2880]{1,0:T(8,128)(2,1)S(1)} %add_up.5), channel_id=1, source_target_pairs={{0,4},{2,6},{4,0},{6,2},{8,12},{10,14},{12,8},{14,10},{1,5},{3,7},... | collective-permute-start | bytes 552968 | tf_op jit(solution)/shard_map/ppermute | solution.py:259
  68.3 2.7 %collective-permute-start.25 = (bf16[32,2880]{1,0:T(8,128)(2,1)S(1)}, bf16[32,2880]{1,0:T(8,128)(2,1)S(1)}, u32[]{:S(2)}, u32[]{:S(2)}) collective-permute-start(bf16[32,2880]{1,0:T(8,128)(2,1)S(1)} %add_up.6), channel_id=1, source_target_pairs={{0,8},{2,10},{4,12},{6,14},{8,0},{10,2},{12,4},{14,6},{1,9},{3,11}... | collective-permute-start | bytes 552968 | tf_op jit(solution)/shard_map/ppermute | solution.py:259
  71.0 0.5 collective-permute-done.22.refs_1_
  71.4 3.2 %collective-permute-done.24.refs_2_ = bf16[32,2880]{1,0:T(8,128)(2,1)S(1)} collective-permute-done((bf16[32,2880]{1,0:T(8,128)(2,1)S(1)}, bf16[32,2880]{1,0:T(8,128)(2,1)S(1)}, u32[]{:S(2)}, u32[]{:S(2)}) %collective-permute-start.24) | collective-permute-done | bytes 184352 | tf_op jit(solution)/shard_map/ppermute | solution.py:259
  74.6 1.4 %collective-permute-done.25.refs_3_ = bf16[32,2880]{1,0:T(8,128)(2,1)S(1)} collective-permute-done((bf16[32,2880]{1,0:T(8,128)(2,1)S(1)}, bf16[32,2880]{1,0:T(8,128)(2,1)S(1)}, u32[]{:S(2)}, u32[]{:S(2)}) %collective-permute-start.25) | collective-permute-done | bytes 184352 | tf_op jit(solution)/shard_map/ppermute | solution.py:259
  76.0 0.8 %add_up.7 = bf16[32,2880]{1,0:T(8,128)(2,1)} custom-call(f32[32,2880]{1,0:T(8,128)S(1)} %get-tuple-element.37.refs_0_, bf16[32,2880]{1,0:T(8,128)(2,1)S(1)} %collective-permute-done.22.refs_1_, bf16[32,2880]{1,0:T(8,128)(2,1)S(1)} %collective-permute-done.24.refs_2_, bf16[32,2880]{1,0:T(8,128)(2,1)S(1)} %collective-permute-done.25.refs_3_), custom_call_target="tpu_custom_call" | custom-call | tf_op jit(solution)/shard_map/add_up/pallas_call | solution.py:238
  (31 shorter events, 0.4 us)
Async XLA Ops:
  0.0 9.7 %copy-start = (f32[2880]{0:T(1024)S(1)}, f32[2880]{0:T(1024)}, u32[]{:S(2)}) copy-start(f32[2880]{0:T(1024)} %param.9) | copy-start | bytes 34564
  0.0 9.7 %copy-start.1 = (s32[32,4]{0,1:T(4,128)S(1)}, s32[32,4]{0,1:T(4,128)}, u32[]{:S(2)}) copy-start(s32[32,4]{0,1:T(4,128)} %param.12) | copy-start | bytes 1540
  0.0 9.8 %copy-start.2 = (f32[32,4]{0,1:T(4,128)S(1)}, f32[32,4]{0,1:T(4,128)}, u32[]{:S(2)}) copy-start(f32[32,4]{0,1:T(4,128)} %param.13) | copy-start | bytes 1540
  6.7 9.1 %collective-permute-start = (bf16[32,2880]{1,0:T(8,128)(2,1)S(1)}, bf16[32,2880]{1,0:T(8,128)(2,1)S(1)}, u32[]{:S(2)}, u32[]{:S(2)}) collective-permute-start(bf16[32,2880]{1,0:T(8,128)(2,1)S(1)} %get-tuple-element.31.refs_0_), channel_id=1, source_target_pairs={{0,1},{1,0},{2,3},{3,2},{4,5},{5,4},{6,7},{7,6},{8,9},{9,8},{10,11... | collective-permute-start | bytes 552968 | tf_op jit(solution)/shard_map/ppermute | solution.py:259
  16.0 6.2 %collective-permute-start.1 = (bf16[32,2944]{1,0:T(8,128)(2,1)S(1)}, bf16[32,2944]{1,0:T(8,128)(2,1)S(1)}, u32[]{:S(2)}, u32[]{:S(2)}) collective-permute-start(bf16[32,2944]{1,0:T(8,128)(2,1)S(1)} %norm.1.refs_0_), channel_id=1, source_target_pairs={{0,1},{1,0},{2,3},{3,2},{4,5},{5,4},{6,7},{7,6},{8,9},{9,8},{10,11... | collective-permute-start | bytes 565256 | tf_op jit(solution)/shard_map/ppermute | solution.py:259
  16.4 9.2 %collective-permute-start.8 = (bf16[32,2944]{1,0:T(8,128)(2,1)S(1)}, bf16[32,2944]{1,0:T(8,128)(2,1)S(1)}, u32[]{:S(2)}, u32[]{:S(2)}) collective-permute-start(bf16[32,2944]{1,0:T(8,128)(2,1)S(1)} %norm.1.refs_0_), channel_id=1, source_target_pairs={{0,4},{2,6},{4,0},{6,2},{8,12},{10,14},{12,8},{14,10},{1,5},{3,7},... | collective-permute-start | bytes 565256 | tf_op jit(solution)/shard_map/ppermute | solution.py:259
  18.1 10.5 %collective-permute-start.4 = (bf16[32,2944]{1,0:T(8,128)(2,1)S(1)}, bf16[32,2944]{1,0:T(8,128)(2,1)S(1)}, u32[]{:S(2)}, u32[]{:S(2)}) collective-permute-start(bf16[32,2944]{1,0:T(8,128)(2,1)S(1)} %norm.1.refs_0_), channel_id=1, source_target_pairs={{0,12},{2,14},{4,8},{6,10},{8,4},{10,6},{12,0},{14,2},{1,13},{3,15... | collective-permute-start | bytes 565256 | tf_op jit(solution)/shard_map/ppermute | solution.py:259
  20.6 8.6 %collective-permute-start.2 = (bf16[32,2944]{1,0:T(8,128)(2,1)S(1)}, bf16[32,2944]{1,0:T(8,128)(2,1)S(1)}, u32[]{:S(2)}, u32[]{:S(2)}) collective-permute-start(bf16[32,2944]{1,0:T(8,128)(2,1)S(1)} %norm.1.refs_0_), channel_id=1, source_target_pairs={{0,2},{2,0},{4,6},{6,4},{8,10},{10,8},{12,14},{14,12},{1,3},{3,1},... | collective-permute-start | bytes 565256 | tf_op jit(solution)/shard_map/ppermute | solution.py:259
  22.2 8.5 %collective-permute-start.3 = (bf16[32,2944]{1,0:T(8,128)(2,1)S(1)}, bf16[32,2944]{1,0:T(8,128)(2,1)S(1)}, u32[]{:S(2)}, u32[]{:S(2)}) collective-permute-start(bf16[32,2944]{1,0:T(8,128)(2,1)S(1)} %collective-permute-done.1.refs_1_), channel_id=1, source_target_pairs={{0,2},{2,0},{4,6},{6,4},{8,10},{10,8},{12,14},{14,12},{1,3},{3,1},... | collective-permute-start | bytes 565256 | tf_op jit(solution)/shard_map/ppermute | solution.py:259
  25.7 11.2 %collective-permute-start.9 = (bf16[32,2944]{1,0:T(8,128)(2,1)S(1)}, bf16[32,2944]{1,0:T(8,128)(2,1)S(1)}, u32[]{:S(2)}, u32[]{:S(2)}) collective-permute-start(bf16[32,2944]{1,0:T(8,128)(2,1)S(1)} %gate.4.refs_0_), channel_id=1, source_target_pairs={{0,1},{1,0},{2,3},{3,2},{4,5},{5,4},{6,7},{7,6},{8,9},{9,8},{10,11... | collective-permute-start | bytes 565256 | tf_op jit(solution)/shard_map/ppermute | solution.py:259
  26.2 11.7 %collective-permute-start.10 = (bf16[32,2944]{1,0:T(8,128)(2,1)S(1)}, bf16[32,2944]{1,0:T(8,128)(2,1)S(1)}, u32[]{:S(2)}, u32[]{:S(2)}) collective-permute-start(bf16[32,2944]{1,0:T(8,128)(2,1)S(1)} %gate.4.refs_0_), channel_id=1, source_target_pairs={{0,2},{2,0},{4,6},{6,4},{8,10},{10,8},{12,14},{14,12},{1,3},{3,1},... | collective-permute-start | bytes 565256 | tf_op jit(solution)/shard_map/ppermute | solution.py:259
  28.6 8.0 %collective-permute-start.6 = (bf16[32,2944]{1,0:T(8,128)(2,1)S(1)}, bf16[32,2944]{1,0:T(8,128)(2,1)S(1)}, u32[]{:S(2)}, u32[]{:S(2)}) collective-permute-start(bf16[32,2944]{1,0:T(8,128)(2,1)S(1)} %collective-permute-done.4.refs_6_.refs_1_), channel_id=1, source_target_pairs={{0,4},{2,6},{4,0},{6,2},{8,12},{10,14},{12,8},{14,10},{1,5},{3,7},... | collective-permute-start | bytes 565256 | tf_op jit(solution)/shard_map/ppermute | solution.py:259
  29.2 7.7 %collective-permute-start.7 = (bf16[32,2944]{1,0:T(8,128)(2,1)S(1)}, bf16[32,2944]{1,0:T(8,128)(2,1)S(1)}, u32[]{:S(2)}, u32[]{:S(2)}) collective-permute-start(bf16[32,2944]{1,0:T(8,128)(2,1)S(1)} %collective-permute-done.4.refs_6_.refs_1_), channel_id=1, source_target_pairs={{0,1},{1,0},{2,3},{3,2},{4,5},{5,4},{6,7},{7,6},{8,9},{9,8},{10,11... | collective-permute-start | bytes 565256 | tf_op jit(solution)/shard_map/ppermute | solution.py:259
  30.7 7.2 %collective-permute-start.11 = (bf16[32,2944]{1,0:T(8,128)(2,1)S(1)}, bf16[32,2944]{1,0:T(8,128)(2,1)S(1)}, u32[]{:S(2)}, u32[]{:S(2)}) collective-permute-start(bf16[32,2944]{1,0:T(8,128)(2,1)S(1)} %collective-permute-done.4.refs_6_.refs_1_), channel_id=1, source_target_pairs={{0,2},{2,0},{4,6},{6,4},{8,10},{10,8},{12,14},{14,12},{1,3},{3,1},... | collective-permute-start | bytes 565256 | tf_op jit(solution)/shard_map/ppermute | solution.py:259
  37.0 1.5 %collective-permute-start.12 = (bf16[32,2944]{1,0:T(8,128)(2,1)S(1)}, bf16[32,2944]{1,0:T(8,128)(2,1)S(1)}, u32[]{:S(2)}, u32[]{:S(2)}) collective-permute-start(bf16[32,2944]{1,0:T(8,128)(2,1)S(1)} %get-tuple-element.41.refs_2_), channel_id=1, source_target_pairs={{0,2},{2,0},{4,6},{6,4},{8,10},{10,8},{12,14},{14,12},{1,3},{3,1},... | collective-permute-start | bytes 565256 | tf_op jit(solution)/shard_map/ppermute | solution.py:259
  37.3 1.5 %collective-permute-start.13 = (bf16[32,2944]{1,0:T(8,128)(2,1)S(1)}, bf16[32,2944]{1,0:T(8,128)(2,1)S(1)}, u32[]{:S(2)}, u32[]{:S(2)}) collective-permute-start(bf16[32,2944]{1,0:T(8,128)(2,1)S(1)} %get-tuple-element.42.refs_3_), channel_id=1, source_target_pairs={{0,2},{2,0},{4,6},{6,4},{8,10},{10,8},{12,14},{14,12},{1,3},{3,1},... | collective-permute-start | bytes 565256 | tf_op jit(solution)/shard_map/ppermute | solution.py:259
  37.5 8.4 %collective-permute-start.14 = (bf16[32,2944]{1,0:T(8,128)(2,1)S(1)}, bf16[32,2944]{1,0:T(8,128)(2,1)S(1)}, u32[]{:S(2)}, u32[]{:S(2)}) collective-permute-start(bf16[32,2944]{1,0:T(8,128)(2,1)S(1)} %get-tuple-element.40.refs_0_), channel_id=1, source_target_pairs={{0,1},{1,0},{2,3},{3,2},{4,5},{5,4},{6,7},{7,6},{8,9},{9,8},{10,11... | collective-permute-start | bytes 565256 | tf_op jit(solution)/shard_map/ppermute | solution.py:259
  46.1 2.3 %collective-permute-start.19 = (bf16[4,32,2880]{2,1,0:T(8,128)(2,1)S(1)}, bf16[4,32,2880]{2,1,0:T(8,128)(2,1)S(1)}, u32[]{:S(2)}, u32[]{:S(2)}) collective-permute-start(bf16[4,32,2880]{2,1,0:T(8,128)(2,1)S(1)} %get-tuple-element.49), channel_id=1, source_target_pairs={{0,2},{2,0},{4,6},{6,4},{8,10},{10,8},{12,14},{14,12},{1,3},{3,1},... | collective-permute-start | bytes 2211848 | tf_op jit(solution)/shard_map/ppermute | solution.py:259
  46.4 3.1 %collective-permute-start.15 = (bf16[32,2944]{1,0:T(8,128)(2,1)S(1)}, bf16[32,2944]{1,0:T(8,128)(2,1)S(1)}, u32[]{:S(2)}, u32[]{:S(2)}) collective-permute-start(bf16[32,2944]{1,0:T(8,128)(2,1)S(1)} %get-tuple-element.40.refs_0_), channel_id=1, source_target_pairs={{0,2},{2,0},{4,6},{6,4},{8,10},{10,8},{12,14},{14,12},{1,3},{3,1},... | collective-permute-start | bytes 565256 | tf_op jit(solution)/shard_map/ppermute | solution.py:259
  46.7 2.9 %collective-permute-start.16 = (bf16[32,2944]{1,0:T(8,128)(2,1)S(1)}, bf16[32,2944]{1,0:T(8,128)(2,1)S(1)}, u32[]{:S(2)}, u32[]{:S(2)}) collective-permute-start(bf16[32,2944]{1,0:T(8,128)(2,1)S(1)} %get-tuple-element.44.refs_1_), channel_id=1, source_target_pairs={{0,2},{2,0},{4,6},{6,4},{8,10},{10,8},{12,14},{14,12},{1,3},{3,1},... | collective-permute-start | bytes 565256 | tf_op jit(solution)/shard_map/ppermute | solution.py:259
  48.6 11.0 %collective-permute-start.20 = (bf16[2,32,2880]{2,1,0:T(8,128)(2,1)S(1)}, bf16[2,32,2880]{2,1,0:T(8,128)(2,1)S(1)}, u32[]{:S(2)}, u32[]{:S(2)}) collective-permute-start(bf16[2,32,2880]{2,1,0:T(8,128)(2,1)S(1)} %get-tuple-element.50), channel_id=1, source_target_pairs={{0,1},{1,0},{2,3},{3,2},{4,5},{5,4},{6,7},{7,6},{8,9},{9,8},{10,11... | collective-permute-start | bytes 1105928 | tf_op jit(solution)/shard_map/ppermute | solution.py:259
  55.6 1.5 %collective-permute-start.17 = (bf16[32,2880]{1,0:T(8,128)(2,1)S(1)}, bf16[32,2880]{1,0:T(8,128)(2,1)S(1)}, u32[]{:S(2)}, u32[]{:S(2)}) collective-permute-start(bf16[32,2880]{1,0:T(8,128)(2,1)S(1)} %get-tuple-element.46), channel_id=1, source_target_pairs={{0,2},{2,0},{4,6},{6,4},{8,10},{10,8},{12,14},{14,12},{1,3},{3,1},... | collective-permute-start | bytes 552968 | tf_op jit(solution)/shard_map/ppermute | solution.py:259
  55.7 1.7 %collective-permute-start.18 = (bf16[32,2880]{1,0:T(8,128)(2,1)S(1)}, bf16[32,2880]{1,0:T(8,128)(2,1)S(1)}, u32[]{:S(2)}, u32[]{:S(2)}) collective-permute-start(bf16[32,2880]{1,0:T(8,128)(2,1)S(1)} %get-tuple-element.47), channel_id=1, source_target_pairs={{0,2},{2,0},{4,6},{6,4},{8,10},{10,8},{12,14},{14,12},{1,3},{3,1},... | collective-permute-start | bytes 552968 | tf_op jit(solution)/shard_map/ppermute | solution.py:259
  56.2 6.0 %collective-permute-start.5 = (bf16[2,32,2880]{2,1,0:T(8,128)(2,1)S(1)}, bf16[2,32,2880]{2,1,0:T(8,128)(2,1)S(1)}, u32[]{:S(2)}, u32[]{:S(2)}) collective-permute-start(bf16[2,32,2880]{2,1,0:T(8,128)(2,1)S(1)} %get-tuple-element.36), channel_id=1, source_target_pairs={{0,2},{2,0},{4,6},{6,4},{8,10},{10,8},{12,14},{14,12},{1,3},{3,1},... | collective-permute-start | bytes 1105928 | tf_op jit(solution)/shard_map/ppermute | solution.py:259
  59.6 6.1 %collective-permute-start.21 = (bf16[32,2880]{1,0:T(8,128)(2,1)S(1)}, bf16[32,2880]{1,0:T(8,128)(2,1)S(1)}, u32[]{:S(2)}, u32[]{:S(2)}) collective-permute-start(bf16[32,2880]{1,0:T(8,128)(2,1)S(1)} %get-tuple-element.51), channel_id=1, source_target_pairs={{0,1},{1,0},{2,3},{3,2},{4,5},{5,4},{6,7},{7,6},{8,9},{9,8},{10,11... | collective-permute-start | bytes 552968 | tf_op jit(solution)/shard_map/ppermute | solution.py:259
  60.5 6.0 %collective-permute-start.23 = (bf16[32,2880]{1,0:T(8,128)(2,1)S(1)}, bf16[32,2880]{1,0:T(8,128)(2,1)S(1)}, u32[]{:S(2)}, u32[]{:S(2)}) collective-permute-start(bf16[32,2880]{1,0:T(8,128)(2,1)S(1)} %add_up.4), channel_id=1, source_target_pairs={{0,4},{2,6},{4,0},{6,2},{8,12},{10,14},{12,8},{14,10},{1,5},{3,7},... | collective-permute-start | bytes 552968 | tf_op jit(solution)/shard_map/ppermute | solution.py:259
  65.8 5.6 %collective-permute-start.22 = (bf16[32,2880]{1,0:T(8,128)(2,1)S(1)}, bf16[32,2880]{1,0:T(8,128)(2,1)S(1)}, u32[]{:S(2)}, u32[]{:S(2)}) collective-permute-start(bf16[32,2880]{1,0:T(8,128)(2,1)S(1)} %gate.7), channel_id=1, source_target_pairs={{0,1},{1,0},{2,3},{3,2},{4,5},{5,4},{6,7},{7,6},{8,9},{9,8},{10,11... | collective-permute-start | bytes 552968 | tf_op jit(solution)/shard_map/ppermute | solution.py:259
  66.5 8.1 %collective-permute-start.24 = (bf16[32,2880]{1,0:T(8,128)(2,1)S(1)}, bf16[32,2880]{1,0:T(8,128)(2,1)S(1)}, u32[]{:S(2)}, u32[]{:S(2)}) collective-permute-start(bf16[32,2880]{1,0:T(8,128)(2,1)S(1)} %add_up.5), channel_id=1, source_target_pairs={{0,4},{2,6},{4,0},{6,2},{8,12},{10,14},{12,8},{14,10},{1,5},{3,7},... | collective-permute-start | bytes 552968 | tf_op jit(solution)/shard_map/ppermute | solution.py:259
  68.3 7.7 %collective-permute-start.25 = (bf16[32,2880]{1,0:T(8,128)(2,1)S(1)}, bf16[32,2880]{1,0:T(8,128)(2,1)S(1)}, u32[]{:S(2)}, u32[]{:S(2)}) collective-permute-start(bf16[32,2880]{1,0:T(8,128)(2,1)S(1)} %add_up.6), channel_id=1, source_target_pairs={{0,8},{2,10},{4,12},{6,14},{8,0},{10,2},{12,4},{14,6},{1,9},{3,11}... | collective-permute-start | bytes 552968 | tf_op jit(solution)/shard_map/ppermute | solution.py:259
